TPU v7x, 32 devices: a whole 2x2x4 slice. The times are simulated.
32 devices in a mesh: blk: 8 (over y, x, core), rows: 4 (over z).
Axes of the slice: x: 2, y: 2, z: 4, core: 2. Of those that a mesh axis runs over, the one named last changes fastest.
Arguments:
- embeddings: bfloat16 [16384, 384], P(('blk', 'rows')), may hold values from -40 to 40
- factors: bfloat16 [8, 384, 384], P('blk'), may hold values from -4 to 4
- centres: bfloat16 [8, 384], P('blk'), may hold values from -3 to 3
- log_prior: bfloat16 [8], P('blk'), may hold values from -1 to 201
Outputs:
- responsibility: float32 [8, 16384], P(None, ('blk', 'rows'))
- counts: float32 [8], replicated
- first_moment: float32 [8, 384], replicated
- second_moment: float32 [8, 384, 384], P('blk')
All inputs are finite; a program needn't handle non-finite values.
Results may differ from a plain program's by a relative error of at most 0.0011.
Values may be sent and summed in bfloat16 or wider, within the bound.
No kernel may reach another device: no remote copies, remote signals or barrier semaphores. Data moves between devices by JAX's collectives and lax.ppermute only.
A program may use at most 128 MiB of HBM per device.

v0:
```python
import jax
import jax.numpy as jnp
from jax import lax
from jax.sharding import PartitionSpec as P

half_temper = 0.05


def shards(embeddings, factors, centres, log_prior):
    rows_here = embeddings.shape[0]
    width = factors.shape[1]
    owned = factors.shape[0]
    n_comp = owned * lax.axis_size("blk")
    normalizer = n_comp / (rows_here * lax.axis_size("blk") * lax.axis_size("rows"))

    def score_one(packed):
        factor_mat, centre_row, prior_val = packed
        whitened = jnp.dot(
            embeddings, factor_mat, preferred_element_type=jnp.float32
        ) - centre_row.astype(jnp.float32)
        return prior_val.astype(jnp.float32) - half_temper * jnp.sum(whitened * whitened, axis=1)

    block_scores = lax.map(
        score_one,
        (
            lax.all_gather(factors, "blk", axis=0, tiled=True),
            lax.all_gather(centres, "blk", axis=0, tiled=True),
            lax.all_gather(log_prior, "blk", axis=0, tiled=True),
        ),
    )
    peak = jnp.max(block_scores, axis=0, keepdims=True)
    unnorm = jnp.exp(block_scores - peak)
    responsibility = unnorm / jnp.sum(unnorm, axis=0, keepdims=True)
    as_float = embeddings.astype(jnp.float32)
    local_counts = jnp.sum(responsibility, axis=1) * normalizer
    local_first = (
        jnp.dot(
            responsibility,
            as_float,
            precision=lax.Precision.HIGHEST,
            preferred_element_type=jnp.float32,
        )
        * normalizer
    )
    counts, first_moment = lax.psum((local_counts, local_first), ("blk", "rows"))
    columns = as_float.T
    positions = lax.iota(jnp.int32, owned * width * lax.axis_size("blk"))
    component = positions // width
    feature = positions % width
    picked_resp = jnp.take(responsibility, component, axis=0)
    picked_cols = jnp.take(columns, feature, axis=0)
    weighted = picked_resp * picked_cols
    owned_rows = lax.psum_scatter(
        jnp.dot(
            weighted, as_float, precision=lax.Precision.HIGHEST, preferred_element_type=jnp.float32
        )
        * normalizer,
        "blk",
        scatter_dimension=0,
        tiled=True,
    )
    summed = lax.psum(owned_rows, "rows")
    second_moment = summed.reshape(owned, width, width)
    return (responsibility, counts, first_moment, second_moment)


def solution(mesh):
    in_specs = (P(("blk", "rows"), None), P("blk", None, None), P("blk", None), P("blk"))
    out_specs = (P(None, ("blk", "rows")), P(), P(), P("blk", None, None))
    return jax.shard_map(shards, mesh=mesh, in_specs=in_specs, out_specs=out_specs, check_vma=False)
```

profile of v0, /device:TPU:0, one launch (start us, length us, event | category | flops | bytes accessed | tf_op | source)
XLA Modules:
  0.0 198.6 jit_solution(9516805809923923314)
XLA Ops:
  7.2 0.0 all-gather.3.cloned.1.call-start
  7.2 0.7 all-gather.3.cloned.1.call-update
  7.9 0.0 reduce-scatter.2.cloned.1.call-start
  8.6 1.2 dynamic-slice
  9.8 0.8 dynamic-update-slice
  10.6 15.3 %all-reduce = bf16[8]{0:T(256)(128)(2,1)S(1)} all-reduce(bf16[8]{0:T(256)(128)(2,1)S(1)} %dynamic-update-slice), channel_id=1, replica_groups=mesh['blk'=8,'rows'=4] {'blk'}, use_global_device_ids=true, to_apply=%add | all-reduce | flops 8 | bytes 32
  25.9 8.0 %all-gather = bf16[8,1,384]{2,1,0:T(2,128)(2,1)S(1)} all-gather(bf16[1,1,384]{2,1,0:T(2,128)(2,1)} %bitcast.33), channel_id=1, replica_groups=mesh['blk'=8,'rows'=4] {'blk'}, dimensions={0}, use_global_device_ids=true | all-gather | bytes 6912 | tf_op jit(solution)/shard_map/all_gather | solution.py:27
  33.9 1.2 copy.11
  35.1 0.1 compare_select_fusion
  35.2 0.1 convert_bitcast_fusion
  35.3 12.9 %gather_fusion.1 = f32[3072,512]{1,0:T(8,128)} fusion(f32[384,512]{1,0:T(8,128)S(1)} %convert_bitcast_fusion, s32[3072]{0:T(1024)S(1)} %broadcast_clamp_fusion), kind=kCustom, calls=%fused_computation.1 | custom fusion | bytes 12595200 | tf_op jit(solution)/shard_map/jit(_take)/gather | solution.py:51
  48.2 0.0 all-gather.3.cloned.1.call-done
  48.2 22.1 %while.10 = (s32[]{:T(128)}, f32[8,512]{1,0:T(8,128)S(1)}, bf16[8]{0:T(256)(128)(2,1)S(1)}, bf16[8,384,384]{2,1,0:T(8,128)(2,1)}, bf16[512,384]{1,0:T(8,128)(2,1...) while((s32[]{:T(128)}, f32[8,512]{1,0:T(8,128)S(1)}, bf16[8]{0:T(256)(128)(2,1)S(1)}, ...), condition=%wide.region_2.3_spmd, body=%wide.region_0.2_spmd.sunk | while | flops 151585664 | bytes 702331 | solution.py:23
  48.3 0.6 dynamic_slice.22
  49.5 1.4 fusion.36
  50.9 0.1 dynamic_update_slice.5
  51.0 0.6 dynamic_slice.22
  52.3 1.4 fusion.36
  53.7 0.1 dynamic_update_slice.5
  53.8 0.6 dynamic_slice.22
  55.1 1.4 fusion.36
  56.5 0.1 dynamic_update_slice.5
  56.6 0.6 dynamic_slice.22
  57.8 1.4 fusion.36
  59.2 0.1 dynamic_update_slice.5
  59.3 0.6 dynamic_slice.22
  60.6 1.4 fusion.36
  62.0 0.1 dynamic_update_slice.5
  62.1 0.6 dynamic_slice.22
  63.4 1.4 fusion.36
  64.8 0.1 dynamic_update_slice.5
  64.9 0.6 dynamic_slice.22
  66.1 1.4 fusion.36
  67.5 0.1 dynamic_update_slice.5
  67.6 0.6 dynamic_slice.22
  68.9 1.4 fusion.36
  70.3 0.1 dynamic_update_slice.5
  70.4 0.1 fusion.25
  70.6 12.9 %gather_fusion = f32[3072,512]{1,0:T(8,128)} fusion(f32[8,512]{1,0:T(8,128)S(1)} %get-tuple-element.116, s32[3072]{0:T(1024)S(1)} %broadcast_clamp_fusion.1), kind=kCustom, calls=%fused_computation | custom fusion | bytes 12595200 | tf_op jit(solution)/shard_map/jit(_take)/gather | solution.py:50
  83.4 10.5 %fusion.9 = f32[3072,384]{1,0:T(8,128)} fusion(bf16[512,384]{1,0:T(8,128)(2,1)S(1)} %get-tuple-element.125, f32[3072,512]{1,0:T(8,128)} %gather_fusion.1, f32[3072,512]{1,0:T(8,128)} %gather_fusion, pred[3072]{0:T(1024)(128)(4,1)S(1)} %get-tuple-element.53, pred[3072]{0:T(1024)(128)(4,1)S(1)} %get-tuple-element.54), kind=kOutput, calls=%fused_computation.14 | convolution fusion | flops 7253655552 | bytes 17700864 | tf_op jit(solution)/shard_map/dot_general | solution.py:54
  93.9 0.0 reduce-scatter.2.cloned.1.call-update
  93.9 0.0 all-reduce.4.cloned.1.call-start
  94.0 54.3 %reduce-scatter.2.cloned.1.call-done = f32[384,384]{1,0:T(8,128)} async-done(((f32[3072,384]{1,0:T(8,128)}), f32[384,384]{1,0:T(8,128)}) %reduce-scatter.2.cloned.1.call-update) | async-done | bytes 589840 | tf_op jit(solution)/shard_map/reduce_scatter | solution.py:53
  148.3 0.0 all-reduce.4.cloned.1.call-update
  148.3 0.3 convolution_multiply_fusion
  148.6 40.2 %all-reduce.1 = (f32[8]{0:T(128)}, f32[8,384]{1,0:T(8,128)}) all-reduce(f32[8]{0:T(128)S(1)} %broadcast_multiply_fusion, f32[8,384]{1,0:T(8,128)S(1)} %convolution_multiply_fusion), channel_id=1, replica_groups=mesh['blk'=8,'rows'=4] {'blk','rows'}, use_global_device_ids=true, to_apply=%region_6.7 | all-reduce | flops 3080 | bytes 24640 | tf_op jit(solution)/shard_map/psum | solution.py:45
  188.8 1.3 all-reduce.4.cloned.1.call-done
  190.1 1.9 copy.25
  (30 shorter events, 0.4 us)
Async XLA Ops:
  7.2 41.1 %all-gather.3.cloned.1.call-start = ((), (), s32[]{:S(2)}) async-start(), calls=%async_computation.1 | async-start | bytes 2654208 | tf_op jit(solution)/shard_map/all_gather | solution.py:26
  7.9 140.4 %reduce-scatter.2.cloned.1.call-start = ((), (), s32[]{:S(2)}) async-start(), calls=%async_computation.2 | async-start | bytes 5308416 | tf_op jit(solution)/shard_map/reduce_scatter | solution.py:53
  35.3 13.0 %copy-start.1 = (bf16[512,384]{1,0:T(8,128)(2,1)S(1)}, bf16[512,384]{1,0:T(8,128)(2,1)}, u32[]{:S(2)}) copy-start(bf16[512,384]{1,0:T(8,128)(2,1)} %param.6) | copy-start | bytes 1179652
  70.6 77.8 %copy-start = (f32[8,512]{1,0:T(8,128)}, f32[8,512]{1,0:T(8,128)S(1)}, u32[]{:S(2)}) copy-start(f32[8,512]{1,0:T(8,128)S(1)} %get-tuple-element.116) | copy-start | bytes 49156
  93.9 96.2 %all-reduce.4.cloned.1.call-start = ((), (), s32[]{:S(2)}) async-start(), calls=%async_computation.3 | async-start | bytes 1179648 | tf_op jit(solution)/shard_map/psum | solution.py:62
Sparse Core Ops, SparseCore 0:
  9.9 31.7 all-gather.2
  94.1 54.1 reduce-scatter.1
  150.8 39.3 all-reduce.3
where the time goes:
time: 199 us
  blocking collectives  63.6 us (32%)
  waiting for transfers between devices  56.3 us (28%)
  local copies, waits for them, and re-layouts  36 us (18%)
  matrix products  21.9 us (11%)
  between operations  14.5 us (7%)
  loops' own time  5.51 us (3%)
    reduce_scatter x1, waiting for transfers between devices, shards(): lax.psum_scatter(jnp.dot(weighted, as_float, precision=lax.Precision.HIGH...  54.3 us
    psum x1, blocking collectives, shards(): lax.psum((local_counts, local_first), ('blk', 'rows'))  40.2 us
    unnamed x1, blocking collectives  15.3 us
    gather x1, local copies, waits for them, and re-layouts, shards(): picked_resp = jnp.take(responsibility, component, axis=0)  12.9 us
    gather x1, local copies, waits for them, and re-layouts, shards(): picked_cols = jnp.take(columns, feature, axis=0)  12.9 us
    dot_general x8, matrix products, score_one(): jnp.dot(embeddings, factor_mat, preferred_element_type=jnp.float32)  11.2 us
    dot_general x1, matrix products, shards(): jnp.dot(weighted, as_float, precision=lax.Precision.HIGHEST, preferred_el...  10.5 us
    all_gather x1, blocking collectives, shards(): lax.all_gather(centres, 'blk', axis=0, tiled=True)  7.99 us
  transfers between devices with their start and end apart: 3, of which 2 were waited for; matrix products, arithmetic and copies ran while one was open for 8% of the time, Pallas kernels for 0%

commit v1 on v0

v1 whole, which is shorter than its diff:
```python
import jax
import jax.numpy as jnp
from jax import lax
from jax.experimental import pallas as pl
from jax.experimental.pallas import tpu as pltpu
from jax.sharding import PartitionSpec as P

half_temper = 0.05
LANES = 128
TAIL = 16
HEAD = 16
VMEM_LIMIT = 40 * 1024 * 1024
NT = (((1,), (1,)), ((), ()))


def split_two(value):
    high = value.astype(jnp.bfloat16)
    low = (value - high.astype(jnp.float32)).astype(jnp.bfloat16)
    return high, low


def exponent_of(largest):
    bits = jnp.ceil(jnp.log(jnp.maximum(largest, 1e-35)) * 1.4426950408889634) - 12.0
    return jnp.clip(bits, -110.0, 110.0)


def score_kernel(offsets, me_ref, own_ref, near_ref, *refs):
    packs, out_ref = refs[:-1], refs[-1]
    rows, width = own_ref.shape
    me = me_ref[0]
    for offset, pack_ref in zip(offsets, packs, strict=True):
        turned = pack_ref[:width, :].T
        tail = pack_ref[width:, :].astype(jnp.float32)
        centre = tail.T[:, 0:1]
        prior = tail[1:2, 0:1]
        for part, rows_ref in enumerate((own_ref, near_ref)):
            whitened = (
                lax.dot_general(turned, rows_ref[...], NT, preferred_element_type=jnp.float32) - centre
            )
            score = prior - half_temper * jnp.sum(whitened * whitened, axis=0, keepdims=True)
            out_ref[pl.ds(me ^ offset, 1), part * rows : (part + 1) * rows] = score


def softmax(scores):
    peak = jnp.max(scores, axis=0, keepdims=True)
    unnorm = jnp.exp(scores - peak)
    return unnorm / jnp.sum(unnorm, axis=0, keepdims=True)


def moment(resp, component, blocks):
    width = blocks[0].shape[1]
    parts = width // LANES
    total = [0.0] * parts
    for weights, block_ref in zip(resp, blocks, strict=True):
        picked = lax.broadcasted_iota(jnp.int32, weights.shape, 0) == component
        row = jnp.sum(jnp.where(picked, weights, 0.0), axis=0, keepdims=True)
        block = block_ref[...]
        high, low = split_two(block.T.astype(jnp.float32) * row)
        for a in range(parts):
            left = jnp.concatenate(
                [high[a * LANES : (a + 1) * LANES], low[a * LANES : (a + 1) * LANES]], axis=0
            )
            both = jnp.dot(left, block[:, a * LANES :], preferred_element_type=jnp.float32)
            total[a] = total[a] + (both[:LANES] + both[LANES:])
    return total


def store_moment(total, normalizer, out_ref, head):
    largest = jnp.zeros((1, 1), jnp.float32)
    for band in total:
        largest = jnp.maximum(largest, jnp.max(jnp.abs(band[:, :LANES]), keepdims=True))
    exponent = exponent_of(largest * normalizer)
    factor = normalizer * jnp.exp2(-exponent)
    at = 0
    for band in total:
        for b in range(band.shape[1] // LANES):
            out_ref[at : at + LANES, :] = band[:, b * LANES : (b + 1) * LANES] * factor
            at += LANES
    out_ref[head : head + 1, :] = jnp.broadcast_to(exponent, (1, LANES))


def give_kernel(offsets, normalizer, me_ref, own_s, near_s, core_s, far_s, *refs):
    blocks, (resp_ref, low_ref), outs = refs[:4], refs[4:6], refs[6:]
    comps, rows = resp_ref.shape[0], blocks[0].shape[0]
    width = blocks[0].shape[1]
    me = me_ref[0]
    index = lax.broadcasted_iota(jnp.int32, (comps, rows), 0)
    mine = ((index ^ me) & 2) == 0
    resp = []
    for here, there in ((own_s, near_s), (core_s, far_s)):
        resp.append(softmax(jnp.where(mine, here[:, :rows], there[:, rows:])))
        resp.append(softmax(jnp.where(mine, here[:, rows:], there[:, :rows])))
    for part, weights in enumerate(resp):
        resp_ref[:, part * rows : (part + 1) * rows] = weights
    for offset, out_ref in zip(offsets, outs, strict=True):
        store_moment(moment(resp, me ^ offset, blocks), normalizer, out_ref, out_ref.shape[0] - HEAD)
    firsts, counts = [], []
    for weights, block_ref in zip(resp, blocks, strict=True):
        high = weights.astype(jnp.bfloat16).astype(jnp.float32)
        rest = weights - high
        middle = rest.astype(jnp.bfloat16).astype(jnp.float32)
        stacked = jnp.concatenate([high, middle, rest - middle], axis=0).astype(jnp.bfloat16)
        product = jnp.dot(stacked, block_ref[...], preferred_element_type=jnp.float32)
        firsts.append(product[:comps] + (product[comps : 2 * comps] + product[2 * comps :]))
        counts.append(jnp.sum(weights, axis=1, keepdims=True))
    first = ((firsts[0] + firsts[2]) + (firsts[1] + firsts[3])) * normalizer
    count = ((counts[0] + counts[2]) + (counts[1] + counts[3])) * normalizer
    exponent = exponent_of(jnp.max(jnp.abs(first), keepdims=True))
    first = first * jnp.exp2(-exponent)
    parts = width // LANES
    for a in range(parts):
        low_ref[a * comps : (a + 1) * comps, :] = first[:, a * LANES : (a + 1) * LANES]
    low_ref[parts * comps : (parts + 1) * comps, :] = jnp.broadcast_to(count, (comps, LANES))
    low_ref[(parts + 1) * comps :, :] = jnp.broadcast_to(exponent, (HEAD, LANES))
    for out_ref in outs:
        end = out_ref.shape[0]
        start = end - low_ref.shape[0]
        out_ref[start : end - HEAD, :] = low_ref[: (parts + 1) * comps, :]
        out_ref[end - HEAD + 1 :, :] = low_ref[(parts + 1) * comps + 1 :, :]


def keep_kernel(normalizer, me_ref, resp_ref, low_ref, *refs):
    blocks, (out_ref, here_ref) = refs[:4], refs[4:]
    rows = blocks[0].shape[0]
    resp = [resp_ref[:, part * rows : (part + 1) * rows] for part in range(4)]
    end = out_ref.shape[0]
    start = end - low_ref.shape[0]
    out_ref[start:, :] = low_ref[...]
    store_moment(moment(resp, me_ref[0], blocks), normalizer, out_ref, end - HEAD)
    here_ref[...] = resp_ref[:, :rows]


def unpack_kernel(packed_ref, second_ref, first_ref, count_ref):
    width = second_ref.shape[1]
    comps = first_ref.shape[0]
    parts = width // LANES
    at = 0
    for a in range(parts):
        for b in range(a, parts):
            block = packed_ref[at : at + LANES, :]
            second_ref[a * LANES : (a + 1) * LANES, b * LANES : (b + 1) * LANES] = block
            if b > a:
                second_ref[b * LANES : (b + 1) * LANES, a * LANES : (a + 1) * LANES] = block.T
            at += LANES
    for a in range(parts):
        first_ref[:, a * LANES : (a + 1) * LANES] = packed_ref[at : at + comps, :]
        at += comps
    count_ref[...] = packed_ref[at : at + comps, :].T[0:1, :]


def tree(values):
    while len(values) > 1:
        values = [values[i] + values[i + 1] for i in range(0, len(values), 2)]
    return values[0]


def combine(messages, second_rows, first_rows, encode):
    height = messages[0].shape[0]
    head = height - HEAD
    row = lax.broadcasted_iota(jnp.int32, messages[0].shape, 0)
    wide = [m.astype(jnp.float32) for m in messages]

    def at_rows(second, first, other):
        return jnp.where(row < second_rows, second, jnp.where(row < second_rows + first_rows, first, other))

    seconds = [w[head : head + 1] for w in wide]
    firsts = [w[head + 1 : head + 2] for w in wide]
    total = tree([w * at_rows(jnp.exp2(s), jnp.exp2(f), 1.0) for w, s, f in zip(wide, seconds, firsts, strict=True)])
    if not encode:
        return total
    grow = float((len(messages) - 1).bit_length())
    second, first = seconds[0], firsts[0]
    for s, f in zip(seconds[1:], firsts[1:], strict=True):
        second, first = jnp.maximum(second, s), jnp.maximum(first, f)
    second, first = second + grow, first + grow
    scaled = total * at_rows(jnp.exp2(-second), jnp.exp2(-first), 1.0)
    scaled = jnp.where(row < head, scaled, jnp.where(row == head, second, first))
    return scaled.astype(jnp.float16)


def call(kernel, out_shape, args, flops, smem_first=True):
    specs = [pl.BlockSpec(memory_space=pltpu.VMEM)] * len(args)
    if smem_first:
        specs[0] = pl.BlockSpec(memory_space=pltpu.SMEM)
    moved = sum(a.size * a.dtype.itemsize for a in args) + sum(
        o.size * o.dtype.itemsize for o in jax.tree.leaves(out_shape)
    )
    return pl.pallas_call(
        kernel,
        out_shape=out_shape,
        in_specs=specs,
        out_specs=jax.tree.map(lambda _: pl.BlockSpec(memory_space=pltpu.VMEM), out_shape),
        compiler_params=pltpu.CompilerParams(vmem_limit_bytes=VMEM_LIMIT),
        cost_estimate=pl.CostEstimate(flops=flops, bytes_accessed=moved, transcendentals=0),
    )(*args)


def solution(mesh):
    n_blk, n_rows = mesh.shape["blk"], mesh.shape["rows"]
    groups = n_blk // 4

    def hop(value, blk, rows):
        if rows == 0:
            return lax.ppermute(value, "blk", [(i, i ^ blk) for i in range(n_blk)])
        if blk == 0:
            return lax.ppermute(value, "rows", [(i, i ^ rows) for i in range(n_rows)])
        pairs = [
            (i * n_rows + j, (i ^ blk) * n_rows + (j ^ rows)) for i in range(n_blk) for j in range(n_rows)
        ]
        return lax.ppermute(value, ("blk", "rows"), pairs)

    def shards(embeddings, factors, centres, log_prior):
        rows, width = embeddings.shape
        comps = factors.shape[0] * n_blk
        normalizer = comps / (rows * n_blk * n_rows)
        parts = width // LANES
        second_rows = parts * (parts + 1) // 2 * LANES
        first_rows = parts * comps
        low_rows = first_rows + comps + HEAD
        height = second_rows + low_rows
        me = lax.axis_index("blk").astype(jnp.int32).reshape(1)

        near = hop(embeddings, 2, 0)
        pack = jnp.concatenate(
            [
                factors.reshape(width, width),
                centres,
                jnp.broadcast_to(log_prior[:, None], (1, width)),
                jnp.zeros((TAIL - 2, width), jnp.bfloat16),
            ],
            axis=0,
        )
        packs = [pack] + [hop(pack, 4 * b, 0) for b in range(1, groups)]
        core = hop(embeddings, 1, 0)
        packs = [p for q in packs for p in (q, hop(q, 1, 0))]
        offsets = [4 * b + c for b in range(groups) for c in range(2)]

        scores = call(
            lambda *refs: score_kernel(offsets, *refs),
            jax.ShapeDtypeStruct((comps, 2 * rows), jnp.float32),
            (me, embeddings, near, *packs),
            2 * len(offsets) * 2 * rows * width * width,
        )
        near_scores = hop(scores, 2, 0)
        core_scores = hop(scores, 1, 0)
        far = hop(near, 1, 0)
        far_scores = hop(near_scores, 1, 0)

        blocks = (embeddings, near, core, far)
        message = jax.ShapeDtypeStruct((height, LANES), jnp.float32)
        flops = 4 * 4 * rows * width * width
        resp, low, *given = call(
            lambda *refs: give_kernel([4 * b for b in range(1, groups)], normalizer, *refs),
            (
                jax.ShapeDtypeStruct((comps, 4 * rows), jnp.float32),
                jax.ShapeDtypeStruct((low_rows, LANES), jnp.float32),
                *[message] * (groups - 1),
            ),
            (me, scores, near_scores, core_scores, far_scores, *blocks),
            flops * (groups - 1),
        )
        given = [g.astype(jnp.float16) for g in given]
        received = {}
        for b in range(1, groups):
            received[b, 1] = hop(given[b - 1], 4 * b, 1)
            received[b, 0] = hop(given[b - 1], 4 * b, 0)
        kept, here = call(
            lambda *refs: keep_kernel(normalizer, *refs),
            (message, jax.ShapeDtypeStruct((comps, rows), jnp.float32)),
            (me, resp, low, *blocks),
            flops,
        )
        received[0, 0] = kept.astype(jnp.float16)
        received[0, 1] = hop(received[0, 0], 0, 1)
        messages = [received[b, z] for b in range(groups) for z in range(2)]
        bit = 2
        while bit < n_rows:
            summed = combine(messages, second_rows, first_rows, True)
            messages = [summed, hop(summed, 0, bit)]
            bit *= 2
        packed = combine(messages, second_rows, first_rows, False)
        second, first, count = call(
            unpack_kernel,
            (
                jax.ShapeDtypeStruct((width, width), jnp.float32),
                jax.ShapeDtypeStruct((comps, width), jnp.float32),
                jax.ShapeDtypeStruct((1, comps), jnp.float32),
            ),
            (packed,),
            0,
            smem_first=False,
        )
        return here, count.reshape(comps), first, second.reshape(1, width, width)

    in_specs = (P(("blk", "rows"), None), P("blk", None, None), P("blk", None), P("blk"))
    out_specs = (P(None, ("blk", "rows")), P(), P(), P("blk", None, None))
    return jax.shard_map(shards, mesh=mesh, in_specs=in_specs, out_specs=out_specs, check_vma=False)
```

time: 199 us -> 52.3 us (0.26)
  blocking collectives: 63.6 us -> 0 us
  local copies, waits for them, and re-layouts: 36 us -> 0.16 us
  waiting for transfers between devices: 56.3 us -> 28.2 us
  matrix products: 21.9 us -> 0 us
  between operations: 14.5 us -> 1.46 us
  starting transfers between devices: 0.12 us -> 13.1 us
  Pallas kernels: 0 us -> 6.66 us
  loops' own time: 5.51 us -> 0 us
    reduce_scatter x1 -> x0, waiting for transfers between devices: 54.3 us -> none  [shards(): lax.psum_scatter(jnp.dot(weighted, as_float, precision=lax.Precision.HIGH...]
    psum x1 -> x0, blocking collectives: 40.2 us -> none  [shards(): lax.psum((local_counts, local_first), ('blk', 'rows'))]
    ppermute x0 -> x13, waiting for transfers between devices: none -> 28.2 us  [the longest x10 15.6 us: hop(): return lax.ppermute(value, 'blk', [(i, i ^ blk) for i in range(n_blk)])]
    gather x2 -> x0, local copies, waits for them, and re-layouts: 25.7 us -> none  [the longest x1 12.9 us: shards(): picked_resp = jnp.take(responsibility, component, axis=0)]
    dot_general x10 -> x0, matrix products: 21.9 us -> none  [the longest x8 11.2 us: score_one(): jnp.dot(embeddings, factor_mat, preferred_element_type=jnp.float32)]
    unnamed x1 -> x0, blocking collectives: 15.3 us -> none
    ppermute x0 -> x13, starting transfers between devices: none -> 13.1 us  [the longest x10 8.34 us: hop(): return lax.ppermute(value, 'blk', [(i, i ^ blk) for i in range(n_blk)])]
    all_gather x1 -> x0, blocking collectives: 7.99 us -> none  [shards(): lax.all_gather(centres, 'blk', axis=0, tiled=True)]
  transfers between devices with their start and end apart: 3 -> 13, of which waited for: 2 -> 7; matrix products, arithmetic and copies ran while one was open for 8% -> 0% of each run, Pallas kernels for 0% -> 8%
where the time goes in v1:
time: 52.3 us; the launch traced here: 52.1 us
  waiting for transfers between devices  28.2 us (54%)
  starting transfers between devices  13.1 us (25%)
  Pallas kernels  6.66 us (13%)
  other arithmetic  2.57 us (5%)
  between operations  1.46 us (3%)
    ppermute x10, waiting for transfers between devices, hop(): return lax.ppermute(value, 'blk', [(i, i ^ blk) for i in range(n_blk)])  15.6 us
    ppermute x2, waiting for transfers between devices, hop(): return lax.ppermute(value, 'rows', [(i, i ^ rows) for i in range(n_rows)])  9.25 us
    ppermute x10, starting transfers between devices, hop(): return lax.ppermute(value, 'blk', [(i, i ^ blk) for i in range(n_blk)])  8.34 us
    pallas_call x4, Pallas kernels, call(): pl.pallas_call(kernel, out_shape=out_shape, in_specs=specs, out_specs=jax...  6.66 us
    ppermute x1, waiting for transfers between devices, hop(): return lax.ppermute(value, ('blk', 'rows'), pairs)  3.38 us
    ppermute x2, starting transfers between devices, hop(): return lax.ppermute(value, 'rows', [(i, i ^ rows) for i in range(n_rows)])  3.15 us
    ppermute x1, starting transfers between devices, hop(): return lax.ppermute(value, ('blk', 'rows'), pairs)  1.58 us
    concatenate x1, other arithmetic, shards(): jnp.concatenate([factors.reshape(width, width), centres, jnp.broadcast_to...  1.15 us
  transfers between devices with their start and end apart: 13, of which 7 were waited for; matrix products, arithmetic and copies ran while one was open for 0% of the time, Pallas kernels for 8%

profile of v1, /device:TPU:0, one launch (start us, length us, event | category | flops | bytes accessed | tf_op | source)
XLA Modules:
  0.0 52.1 jit_solution(5273545021816089174)
XLA Ops:
  0.6 0.0 copy-start
  1.4 0.1 pad.3.clone
  1.4 0.1 pad.2.clone
  1.5 1.1 %maximum_maximum_fusion.refs_3_ = bf16[400,384]{1,0:T(8,128)(2,1)S(1)} fusion(bf16[1,384]{1,0:T(2,128)(2,1)} %param.6, bf16[384,384]{1,0:T(8,128)(2,1)} %bitcast.35, bf16[400]{0:T(512)(128)(2,1)S(1)} %pad.3.clone, bf16[400]{0:T(512)(128)(2,1)S(1)} %pad.2.clone), kind=kLoop, calls=%fused_computation.2 | loop fusion | flops 1228800 | bytes 604480 | tf_op jit(solution)/shard_map/concatenate | solution.py:224
  2.7 3.0 %collective-permute-start.2 = (bf16[400,384]{1,0:T(8,128)(2,1)S(1)}, bf16[400,384]{1,0:T(8,128)(2,1)S(1)}, u32[]{:S(2)}, u32[]{:S(2)}) collective-permute-start(bf16[400,384]{1,0:T(8,128)(2,1)S(1)} %maximum_maximum_fusion.refs_3_), channel_id=1, source_target_pairs={{0,16},{4,20},{8,24},{12,28},{16,0},{20,4},{24,8},{28,12},{1,17},{... | collective-permute-start | bytes 921608 | tf_op jit(solution)/shard_map/ppermute | solution.py:204
  5.7 0.0 copy-done
  5.7 1.5 %collective-permute-start = (bf16[512,384]{1,0:T(8,128)(2,1)S(1)}, bf16[512,384]{1,0:T(8,128)(2,1)S(1)}, u32[]{:S(2)}, u32[]{:S(2)}) collective-permute-start(bf16[512,384]{1,0:T(8,128)(2,1)S(1)} %copy-done), channel_id=1, source_target_pairs={{0,8},{4,12},{8,0},{12,4},{16,24},{20,28},{24,16},{28,20},{1,9},{5... | collective-permute-start | bytes 1179656 | tf_op jit(solution)/shard_map/ppermute | solution.py:204
  7.2 0.0 collective-permute-start.1
  7.2 5.8 %collective-permute-done.2.refs_5_ = bf16[400,384]{1,0:T(8,128)(2,1)S(1)} collective-permute-done((bf16[400,384]{1,0:T(8,128)(2,1)S(1)}, bf16[400,384]{1,0:T(8,128)(2,1)S(1)}, u32[]{:S(2)}, u32[]{:S(2)}) %collective-permute-start.2) | collective-permute-done | bytes 307232 | tf_op jit(solution)/shard_map/ppermute | solution.py:204
  13.0 0.0 collective-permute-start.3
  13.0 0.5 collective-permute-start.7
  13.5 2.8 %collective-permute-done.refs_2_.refs_6_.refs_4_ = bf16[512,384]{1,0:T(8,128)(2,1)S(1)} collective-permute-done((bf16[512,384]{1,0:T(8,128)(2,1)S(1)}, bf16[512,384]{1,0:T(8,128)(2,1)S(1)}, u32[]{:S(2)}, u32[]{:S(2)}) %collective-permute-start) | collective-permute-done | bytes 393248 | tf_op jit(solution)/shard_map/ppermute | solution.py:204
  16.3 0.0 collective-permute-start.8
  16.3 0.0 collective-permute-done.1.refs_4_
  16.3 0.0 collective-permute-done.3.refs_6_
  16.3 2.0 %shard_map.75.refs_1_ = f32[8,1024]{1,0:T(8,128)S(1)} custom-call(s32[1]{0:T(128)} %bitcast.refs_0_, bf16[512,384]{1,0:T(8,128)(2,1)S(1)} %copy-done, bf16[512,384]{1,0:T(8,128)(2,1)S(1)} %collective-permute-done.refs_2_.refs_6_.refs_4_, bf16[400,384]{1,0:T(8,128)(2,1)S(1)} %maximum_maximum_fusion.refs_3_, ...), custom_call_target="tpu_custom_call" | custom-call | flops 1207959552 | bytes 2048004 | tf_op jit(solution)/shard_map/pallas_call | solution.py:188
  18.3 1.5 %collective-permute-start.4 = (f32[8,1024]{1,0:T(8,128)S(1)}, f32[8,1024]{1,0:T(8,128)S(1)}, u32[]{:S(2)}, u32[]{:S(2)}) collective-permute-start(f32[8,1024]{1,0:T(8,128)S(1)} %shard_map.75.refs_1_), channel_id=1, source_target_pairs={{0,8},{4,12},{8,0},{12,4},{16,24},{20,28},{24,16},{28,20},{1,9},{5... | collective-permute-start | bytes 98312 | tf_op jit(solution)/shard_map/ppermute | solution.py:204
  19.9 0.2 collective-permute-start.5
  20.1 2.2 %collective-permute-done.4.refs_2_ = f32[8,1024]{1,0:T(8,128)S(1)} collective-permute-done((f32[8,1024]{1,0:T(8,128)S(1)}, f32[8,1024]{1,0:T(8,128)S(1)}, u32[]{:S(2)}, u32[]{:S(2)}) %collective-permute-start.4) | collective-permute-done | bytes 32800 | tf_op jit(solution)/shard_map/ppermute | solution.py:204
  22.3 0.0 collective-permute-start.6
  22.3 0.0 collective-permute-done.7.refs_7_.refs_5_
  22.3 0.0 collective-permute-done.5.refs_3_
  22.3 1.2 %collective-permute-done.6.refs_4_ = f32[8,1024]{1,0:T(8,128)S(1)} collective-permute-done((f32[8,1024]{1,0:T(8,128)S(1)}, f32[8,1024]{1,0:T(8,128)S(1)}, u32[]{:S(2)}, u32[]{:S(2)}) %collective-permute-start.6) | collective-permute-done | bytes 32800 | tf_op jit(solution)/shard_map/ppermute | solution.py:204
  23.5 0.0 collective-permute-done.8.refs_8_.refs_6_
  23.5 1.7 %shard_map.76 = (f32[8,2048]{1,0:T(8,128)S(1)}, f32[48,128]{1,0:T(8,128)S(1)}, f32[816,128]{1,0:T(8,128)S(1)}) custom-call(s32[1]{0:T(128)} %bitcast.refs_0_, f32[8,1024]{1,0:T(8,128)S(1)} %shard_map.75.refs_1_, f32[8,1024]{1,0:T(8,128)S(1)} %collective-permute-done.4.refs_2_, f32[8,1024]{1,0:T(8,128)S(1)} %collective-permute-done.5.refs_3_, ...), custom_call_target="tpu_custom_call" | custom-call | flops 1207959552 | bytes 2211844 | tf_op jit(solution)/shard_map/pallas_call | solution.py:188
  25.3 1.6 %collective-permute-start.11 = (f16[816,128]{1,0:T(8,128)(2,1)S(1)}, f16[816,128]{1,0:T(8,128)(2,1)S(1)}, u32[]{:S(2)}, u32[]{:S(2)}) collective-permute-start(f16[816,128]{1,0:T(8,128)(2,1)S(1)} %convert_element_type.30), channel_id=1, source_target_pairs={{0,17},{1,16},{2,19},{3,18},{4,21},{5,20},{6,23},{7,22},{8,25},{9,... | collective-permute-start | bytes 626696 | tf_op jit(solution)/shard_map/ppermute | solution.py:210
  26.8 1.5 %collective-permute-start.10 = (f16[816,128]{1,0:T(8,128)(2,1)S(1)}, f16[816,128]{1,0:T(8,128)(2,1)S(1)}, u32[]{:S(2)}, u32[]{:S(2)}) collective-permute-start(f16[816,128]{1,0:T(8,128)(2,1)S(1)} %convert_element_type.30), channel_id=1, source_target_pairs={{0,16},{4,20},{8,24},{12,28},{16,0},{20,4},{24,8},{28,12},{1,17},{... | collective-permute-start | bytes 626696 | tf_op jit(solution)/shard_map/ppermute | solution.py:204
  28.4 2.0 %shard_map.77 = (f32[816,128]{1,0:T(8,128)S(1)}, f32[8,512]{1,0:T(8,128)}) custom-call(s32[1]{0:T(128)} %bitcast.refs_0_, f32[8,2048]{1,0:T(8,128)S(1)} %get-tuple-element.12.refs_1_, f32[48,128]{1,0:T(8,128)S(1)} %get-tuple-element.13.refs_2_, bf16[512,384]{1,0:T(8,128)(2,1)S(1)} %copy-done, ...), custom_call_target="tpu_custom_call" | custom-call | flops 1207959552 | bytes 2097156 | tf_op jit(solution)/shard_map/pallas_call | solution.py:188
  30.3 0.1 fusion.9
  30.4 0.5 collective-permute-start.9
  30.9 3.4 %collective-permute-done.11 = f16[816,128]{1,0:T(8,128)(2,1)S(1)} collective-permute-done((f16[816,128]{1,0:T(8,128)(2,1)S(1)}, f16[816,128]{1,0:T(8,128)(2,1)S(1)}, u32[]{:S(2)}, u32[]{:S(2)}) %collective-permute-start.11) | collective-permute-done | bytes 208928 | tf_op jit(solution)/shard_map/ppermute | solution.py:210
  34.3 3.6 %collective-permute-done.10 = f16[816,128]{1,0:T(8,128)(2,1)S(1)} collective-permute-done((f16[816,128]{1,0:T(8,128)(2,1)S(1)}, f16[816,128]{1,0:T(8,128)(2,1)S(1)}, u32[]{:S(2)}, u32[]{:S(2)}) %collective-permute-start.10) | collective-permute-done | bytes 208928 | tf_op jit(solution)/shard_map/ppermute | solution.py:204
  38.0 0.0 collective-permute-done.9
  38.1 0.9 %fusion.8 = (f32[816,128]{1,0:T(8,128)S(1)}, f16[816,128]{1,0:T(8,128)(2,1)S(1)}) fusion(f32[128]{0:T(128)S(1)} %bitcast.37, f32[128]{0:T(128)S(1)} %bitcast.36, pred[816]{0:T(1024)(128)(4,1)S(1)} %get-tuple-element.42, f32[128]{0:T(128)S(1)} %get-tuple-element.28, f32[128]{0:T(128)S(1)} %get-tuple-element.22, f32[128]{0:T(128)S(1)} %get-tuple-element.40, ...), kind=kLoop, calls=%fused_computation.31 | loop fusion | flops 2715648 | bytes 1471680 | tf_op jit(solution)/shard_map/convert_element_type | solution.py:161
  38.9 2.6 %collective-permute-start.12 = (f16[816,128]{1,0:T(8,128)(2,1)S(1)}, f16[816,128]{1,0:T(8,128)(2,1)S(1)}, u32[]{:S(2)}, u32[]{:S(2)}) collective-permute-start(f16[816,128]{1,0:T(8,128)(2,1)S(1)} %get-tuple-element.21), channel_id=1, source_target_pairs={{0,2},{1,3},{2,0},{3,1},{4,6},{5,7},{6,4},{7,5},{8,10},{9,11},{10,... | collective-permute-start | bytes 626696 | tf_op jit(solution)/shard_map/ppermute | solution.py:206
  41.6 9.2 %collective-permute-done.12 = f16[816,128]{1,0:T(8,128)(2,1)S(1)} collective-permute-done((f16[816,128]{1,0:T(8,128)(2,1)S(1)}, f16[816,128]{1,0:T(8,128)(2,1)S(1)}, u32[]{:S(2)}, u32[]{:S(2)}) %collective-permute-start.12) | collective-permute-done | bytes 208928 | tf_op jit(solution)/shard_map/ppermute | solution.py:206
  50.9 0.3 multiply_add_fusion.packed_ref
  51.2 1.0 %shard_map.78 = (f32[384,384]{1,0:T(8,128)}, f32[8,384]{1,0:T(8,128)}, f32[1,8]{1,0:T(1,128)}) custom-call(f32[816,128]{1,0:T(8,128)S(1)} %multiply_add_fusion.packed_ref), custom_call_target="tpu_custom_call" | custom-call | bytes 1019936 | tf_op jit(solution)/shard_map/pallas_call | solution.py:188
  (11 shorter events, 0.2 us)
Async XLA Ops:
  0.6 5.1 %copy-start = (bf16[512,384]{1,0:T(8,128)(2,1)S(1)}, bf16[512,384]{1,0:T(8,128)(2,1)}, u32[]{:S(2)}) copy-start(bf16[512,384]{1,0:T(8,128)(2,1)} %refs_3_.1) | copy-start | bytes 1179652
  2.7 10.3 %collective-permute-start.2 = (bf16[400,384]{1,0:T(8,128)(2,1)S(1)}, bf16[400,384]{1,0:T(8,128)(2,1)S(1)}, u32[]{:S(2)}, u32[]{:S(2)}) collective-permute-start(bf16[400,384]{1,0:T(8,128)(2,1)S(1)} %maximum_maximum_fusion.refs_3_), channel_id=1, source_target_pairs={{0,16},{4,20},{8,24},{12,28},{16,0},{20,4},{24,8},{28,12},{1,17},{... | collective-permute-start | bytes 921608 | tf_op jit(solution)/shard_map/ppermute | solution.py:204
  5.7 10.6 %collective-permute-start = (bf16[512,384]{1,0:T(8,128)(2,1)S(1)}, bf16[512,384]{1,0:T(8,128)(2,1)S(1)}, u32[]{:S(2)}, u32[]{:S(2)}) collective-permute-start(bf16[512,384]{1,0:T(8,128)(2,1)S(1)} %copy-done), channel_id=1, source_target_pairs={{0,8},{4,12},{8,0},{12,4},{16,24},{20,28},{24,16},{28,20},{1,9},{5... | collective-permute-start | bytes 1179656 | tf_op jit(solution)/shard_map/ppermute | solution.py:204
  7.2 9.1 %collective-permute-start.1 = (bf16[400,384]{1,0:T(8,128)(2,1)S(1)}, bf16[400,384]{1,0:T(8,128)(2,1)S(1)}, u32[]{:S(2)}, u32[]{:S(2)}) collective-permute-start(bf16[400,384]{1,0:T(8,128)(2,1)S(1)} %maximum_maximum_fusion.refs_3_), channel_id=1, source_target_pairs={{0,4},{4,0},{8,12},{12,8},{16,20},{20,16},{24,28},{28,24},{1,5},{5... | collective-permute-start | bytes 921608 | tf_op jit(solution)/shard_map/ppermute | solution.py:204
  13.0 3.3 %collective-permute-start.3 = (bf16[400,384]{1,0:T(8,128)(2,1)S(1)}, bf16[400,384]{1,0:T(8,128)(2,1)S(1)}, u32[]{:S(2)}, u32[]{:S(2)}) collective-permute-start(bf16[400,384]{1,0:T(8,128)(2,1)S(1)} %collective-permute-done.2.refs_5_), channel_id=1, source_target_pairs={{0,4},{4,0},{8,12},{12,8},{16,20},{20,16},{24,28},{28,24},{1,5},{5... | collective-permute-start | bytes 921608 | tf_op jit(solution)/shard_map/ppermute | solution.py:204
  13.0 9.3 %collective-permute-start.7 = (bf16[512,384]{1,0:T(8,128)(2,1)S(1)}, bf16[512,384]{1,0:T(8,128)(2,1)S(1)}, u32[]{:S(2)}, u32[]{:S(2)}) collective-permute-start(bf16[512,384]{1,0:T(8,128)(2,1)S(1)} %copy-done), channel_id=1, source_target_pairs={{0,4},{4,0},{8,12},{12,8},{16,20},{20,16},{24,28},{28,24},{1,5},{5... | collective-permute-start | bytes 1179656 | tf_op jit(solution)/shard_map/ppermute | solution.py:204
  16.3 7.2 %collective-permute-start.8 = (bf16[512,384]{1,0:T(8,128)(2,1)S(1)}, bf16[512,384]{1,0:T(8,128)(2,1)S(1)}, u32[]{:S(2)}, u32[]{:S(2)}) collective-permute-start(bf16[512,384]{1,0:T(8,128)(2,1)S(1)} %collective-permute-done.refs_2_.refs_6_.refs_4_), channel_id=1, source_target_pairs={{0,4},{4,0},{8,12},{12,8},{16,20},{20,16},{24,28},{28,24},{1,5},{5... | collective-permute-start | bytes 1179656 | tf_op jit(solution)/shard_map/ppermute | solution.py:204
  18.3 4.0 %collective-permute-start.4 = (f32[8,1024]{1,0:T(8,128)S(1)}, f32[8,1024]{1,0:T(8,128)S(1)}, u32[]{:S(2)}, u32[]{:S(2)}) collective-permute-start(f32[8,1024]{1,0:T(8,128)S(1)} %shard_map.75.refs_1_), channel_id=1, source_target_pairs={{0,8},{4,12},{8,0},{12,4},{16,24},{20,28},{24,16},{28,20},{1,9},{5... | collective-permute-start | bytes 98312 | tf_op jit(solution)/shard_map/ppermute | solution.py:204
  19.9 2.4 %collective-permute-start.5 = (f32[8,1024]{1,0:T(8,128)S(1)}, f32[8,1024]{1,0:T(8,128)S(1)}, u32[]{:S(2)}, u32[]{:S(2)}) collective-permute-start(f32[8,1024]{1,0:T(8,128)S(1)} %shard_map.75.refs_1_), channel_id=1, source_target_pairs={{0,4},{4,0},{8,12},{12,8},{16,20},{20,16},{24,28},{28,24},{1,5},{5... | collective-permute-start | bytes 98312 | tf_op jit(solution)/shard_map/ppermute | solution.py:204
  22.3 1.2 %collective-permute-start.6 = (f32[8,1024]{1,0:T(8,128)S(1)}, f32[8,1024]{1,0:T(8,128)S(1)}, u32[]{:S(2)}, u32[]{:S(2)}) collective-permute-start(f32[8,1024]{1,0:T(8,128)S(1)} %collective-permute-done.4.refs_2_), channel_id=1, source_target_pairs={{0,4},{4,0},{8,12},{12,8},{16,20},{20,16},{24,28},{28,24},{1,5},{5... | collective-permute-start | bytes 98312 | tf_op jit(solution)/shard_map/ppermute | solution.py:204
  25.3 9.0 %collective-permute-start.11 = (f16[816,128]{1,0:T(8,128)(2,1)S(1)}, f16[816,128]{1,0:T(8,128)(2,1)S(1)}, u32[]{:S(2)}, u32[]{:S(2)}) collective-permute-start(f16[816,128]{1,0:T(8,128)(2,1)S(1)} %convert_element_type.30), channel_id=1, source_target_pairs={{0,17},{1,16},{2,19},{3,18},{4,21},{5,20},{6,23},{7,22},{8,25},{9,... | collective-permute-start | bytes 626696 | tf_op jit(solution)/shard_map/ppermute | solution.py:210
  26.8 11.1 %collective-permute-start.10 = (f16[816,128]{1,0:T(8,128)(2,1)S(1)}, f16[816,128]{1,0:T(8,128)(2,1)S(1)}, u32[]{:S(2)}, u32[]{:S(2)}) collective-permute-start(f16[816,128]{1,0:T(8,128)(2,1)S(1)} %convert_element_type.30), channel_id=1, source_target_pairs={{0,16},{4,20},{8,24},{12,28},{16,0},{20,4},{24,8},{28,12},{1,17},{... | collective-permute-start | bytes 626696 | tf_op jit(solution)/shard_map/ppermute | solution.py:204
  30.4 7.6 %collective-permute-start.9 = (f16[816,128]{1,0:T(8,128)(2,1)S(1)}, f16[816,128]{1,0:T(8,128)(2,1)S(1)}, u32[]{:S(2)}, u32[]{:S(2)}) collective-permute-start(f16[816,128]{1,0:T(8,128)(2,1)S(1)} %get-tuple-element.27), channel_id=1, source_target_pairs={{0,1},{1,0},{2,3},{3,2},{4,5},{5,4},{6,7},{7,6},{8,9},{9,8},{10,11... | collective-permute-start | bytes 626696 | tf_op jit(solution)/shard_map/ppermute | solution.py:206
  38.9 11.9 %collective-permute-start.12 = (f16[816,128]{1,0:T(8,128)(2,1)S(1)}, f16[816,128]{1,0:T(8,128)(2,1)S(1)}, u32[]{:S(2)}, u32[]{:S(2)}) collective-permute-start(f16[816,128]{1,0:T(8,128)(2,1)S(1)} %get-tuple-element.21), channel_id=1, source_target_pairs={{0,2},{1,3},{2,0},{3,1},{4,6},{5,7},{6,4},{7,5},{8,10},{9,11},{10,... | collective-permute-start | bytes 626696 | tf_op jit(solution)/shard_map/ppermute | solution.py:206

commit v2 on v1

v2 whole, which is shorter than its diff:
```python
import jax
import jax.numpy as jnp
from jax import lax
from jax.experimental import pallas as pl
from jax.experimental.pallas import tpu as pltpu
from jax.sharding import PartitionSpec as P

half_temper = 0.05
LANES = 128
TAIL = 16
EARLY_COST = 0
HEAD = 8
VMEM_LIMIT = 40 * 1024 * 1024
NT = (((1,), (1,)), ((), ()))


def split_two(value):
    high = value.astype(jnp.bfloat16)
    low = (value - high.astype(jnp.float32)).astype(jnp.bfloat16)
    return high, low


def power(exponent):
    whole = exponent.astype(jnp.int32)
    size = jnp.abs(whole)
    result = jnp.ones(exponent.shape, jnp.float32)
    for bit in range(7):
        factor = jnp.where(whole < 0, 0.5 ** (1 << bit), 2.0 ** (1 << bit))
        result = result * jnp.where((size >> bit) & 1 == 1, factor, 1.0)
    return result


def exponent_of(largest):
    bits = jnp.ceil(jnp.log(jnp.maximum(largest, 1e-35)) * 1.4426950408889634) - 12.0
    return jnp.clip(bits, -110.0, 110.0)


def score_rows(turned, tail, rows_ref):
    whitened = lax.dot_general(turned, rows_ref[...], NT, preferred_element_type=jnp.float32)
    whitened = whitened - tail.T[:, 0:1]
    return tail[1:2, 0:1] - half_temper * jnp.sum(whitened * whitened, axis=0, keepdims=True)


def own_kernel(own_ref, core_ref, matrix_ref, tail_ref, out_ref, turned_ref):
    rows = own_ref.shape[0]
    turned_ref[...] = matrix_ref[...].T
    tail = tail_ref[...].astype(jnp.float32)
    for part, rows_ref in enumerate((own_ref, core_ref)):
        out_ref[:, part * rows : (part + 1) * rows] = score_rows(turned_ref[...], tail, rows_ref)


def near_kernel(groups, own_ref, near_ref, core_ref, done_ref, turned_ref, *refs):
    tails, matrices, (out_ref, others_ref) = refs[:groups], refs[groups : 2 * groups - 1], refs[2 * groups - 1 :]
    rows = own_ref.shape[0]
    for b in range(groups):
        if b:
            others_ref[b - 1] = matrices[b - 1][...].T
        turned = others_ref[b - 1] if b else turned_ref[...]
        tail = tails[b][...].astype(jnp.float32)
        for part, rows_ref in enumerate((own_ref, near_ref, core_ref)):
            if b == 0 and part != 1:
                line = done_ref[:, part // 2 * rows : (part // 2 + 1) * rows]
            else:
                line = score_rows(turned, tail, rows_ref)
            out_ref[b : b + 1, part * rows : (part + 1) * rows] = line


def far_kernel(groups, far_ref, done_ref, turned_ref, others_ref, *refs):
    tails, out_ref = refs[:groups], refs[groups]
    rows = far_ref.shape[0]
    out_ref[:, : 3 * rows] = done_ref[...]
    for b in range(groups):
        tail = tails[b][...].astype(jnp.float32)
        turned = others_ref[b - 1] if b else turned_ref[...]
        out_ref[b : b + 1, 3 * rows :] = score_rows(turned, tail, far_ref)


def softmax(scores):
    peak = jnp.max(scores, axis=0, keepdims=True)
    unnorm = jnp.exp(scores - peak)
    return unnorm / jnp.sum(unnorm, axis=0, keepdims=True)


def moment(resp, component, blocks, extra=None):
    width = blocks[0].shape[1]
    parts = width // LANES
    total = [0.0] * parts
    products = []
    for at, (weights, block_ref) in enumerate(zip(resp, blocks, strict=True)):
        picked = lax.broadcasted_iota(jnp.int32, weights.shape, 0) == component
        row = jnp.sum(jnp.where(picked, weights, 0.0), axis=0, keepdims=True)
        block = block_ref[...]
        high, low = split_two(block.T.astype(jnp.float32) * row)
        for a in range(parts):
            left = [high[a * LANES : (a + 1) * LANES], low[a * LANES : (a + 1) * LANES]]
            if a == 0 and extra is not None:
                left.append(extra[at])
            left = jnp.concatenate(left, axis=0)
            both = jnp.dot(left, block[:, a * LANES :], preferred_element_type=jnp.float32)
            total[a] = total[a] + (both[:LANES] + both[LANES : 2 * LANES])
            if a == 0:
                products.append(both[2 * LANES :])
    return total, products


def pair_masks():
    i = lax.broadcasted_iota(jnp.int32, (LANES, LANES), 0)
    j = lax.broadcasted_iota(jnp.int32, (LANES, LANES), 1)
    return i, j


class Layout:
    def __init__(self, width, comps):
        self.parts = width // LANES
        self.comps = comps
        off = self.parts * (self.parts - 1) // 2 * LANES
        folded = self.parts // 2 * LANES + self.parts % 2 * (LANES // 2)
        self.diagonals = off + folded
        self.firsts = self.diagonals + -(-self.parts // 8) * 8
        self.counts = self.firsts + self.parts * comps
        self.half = -(-(self.counts + comps) // 16) * 8
        self.rows = self.half + HEAD

    def write(self, out_ref, flip, at, value):
        done = 0
        while done < value.shape[0]:
            side, row = divmod(at + done, self.half)
            count = min(value.shape[0] - done, self.half - row)
            out_ref[side ^ flip, row : row + count, :] = value[done : done + count]
            done += count


def store_second(total, normalizer, layout, out_ref, flip):
    parts = layout.parts
    largest = jnp.zeros((1, 1), jnp.float32)
    for band in total:
        largest = jnp.maximum(largest, jnp.max(jnp.abs(band[:, :LANES]), keepdims=True))
    exponent = exponent_of(largest * normalizer)
    factor = normalizer * power(-exponent)
    i, j = pair_masks()
    at = 0
    for a in range(parts):
        for b in range(a + 1, parts):
            block = total[a][:, (b - a) * LANES : (b - a + 1) * LANES]
            layout.write(out_ref, flip, at, block * factor)
            at += LANES
    diagonal = [band[:, :LANES] * factor for band in total]
    for a in range(0, parts - 1, 2):
        layout.write(out_ref, flip, at, jnp.where(i <= j, diagonal[a], diagonal[a + 1]))
        at += LANES
    if parts % 2:
        half = LANES // 2
        lower = pltpu.roll(diagonal[-1][half:], half, 1)
        layout.write(out_ref, flip, at, jnp.where(i <= j, diagonal[-1], 0.0)[:half] + jnp.where((i > j)[:half], lower, 0.0))
        at += half
    lines = [jnp.sum(jnp.where(i == j, d, 0.0), axis=0, keepdims=True) for d in diagonal]
    lines += [jnp.zeros((1, LANES), jnp.float32)] * (layout.firsts - at - parts)
    layout.write(out_ref, flip, at, jnp.concatenate(lines, axis=0))
    for side in range(2):
        out_ref[side, layout.half : layout.half + 1, :] = jnp.broadcast_to(exponent, (1, LANES))


def store_low(low_ref, layout, out_ref, flip):
    body = low_ref.shape[0] - HEAD
    layout.write(out_ref, flip, layout.firsts, low_ref[:body, :])
    for side in range(2):
        out_ref[side, layout.half + 1 :, :] = low_ref[body + 1 :, :]


def give_kernel(offsets, normalizer, layout, me_ref, *refs):
    scores, blocks = refs[:4], refs[4:8]
    outs, table_ref = refs[8:-1], refs[-1]
    resp_ref, low_ref, here_ref, *outs = outs
    comps, rows = here_ref.shape
    me, flip = me_ref[0], me_ref[1]
    for source, score_ref in enumerate(scores):
        for b in range(score_ref.shape[0]):
            for part in range(4):
                to = part ^ (((source & 1) << 1) | (source >> 1))
                table_ref[pl.ds(me ^ (4 * b + source), 1), to * rows : (to + 1) * rows] = score_ref[
                    b : b + 1, part * rows : (part + 1) * rows
                ]
    weights = softmax(table_ref[...])
    resp_ref[...] = weights
    here_ref[...] = weights[:, :rows]
    resp = [weights[:, part * rows : (part + 1) * rows] for part in range(4)]
    stacked, counts = [], []
    for weights in resp:
        high = weights.astype(jnp.bfloat16).astype(jnp.float32)
        rest = weights - high
        middle = rest.astype(jnp.bfloat16).astype(jnp.float32)
        pieces = [high, middle, rest - middle]
        if 3 * comps % 16:
            pieces.append(jnp.zeros((-3 * comps % 16, rows), jnp.float32))
        stacked.append(jnp.concatenate(pieces, axis=0).astype(jnp.bfloat16))
        counts.append(jnp.sum(weights, axis=1, keepdims=True))
    totals, products = [], []
    for at, offset in enumerate(offsets):
        total, product = moment(resp, me ^ offset, blocks, stacked if at == 0 else None)
        totals.append(total)
        products = products or product
    firsts = [p[:comps] + (p[comps : 2 * comps] + p[2 * comps : 3 * comps]) for p in products]
    first = ((firsts[0] + firsts[2]) + (firsts[1] + firsts[3])) * normalizer
    count = ((counts[0] + counts[2]) + (counts[1] + counts[3])) * normalizer
    exponent = exponent_of(jnp.max(jnp.abs(first), keepdims=True))
    first = first * power(-exponent)
    body = low_ref.shape[0] - HEAD
    low_ref[...] = jnp.zeros_like(low_ref)
    for a in range(layout.parts):
        low_ref[a * comps : (a + 1) * comps, :] = first[:, a * LANES : (a + 1) * LANES]
    at = layout.parts * comps
    low_ref[at : at + comps, :] = jnp.broadcast_to(count, (comps, LANES))
    low_ref[body:, :] = jnp.broadcast_to(exponent, (HEAD, LANES))
    for total, out_ref in zip(totals, outs, strict=True):
        store_second(total, normalizer, layout, out_ref, flip)
        store_low(low_ref, layout, out_ref, flip)


def keep_kernel(normalizer, layout, me_ref, resp_ref, low_ref, *refs):
    blocks, out_ref = refs[:4], refs[4]
    rows = blocks[0].shape[0]
    resp = [resp_ref[:, part * rows : (part + 1) * rows] for part in range(4)]
    flip = me_ref[1]
    store_second(moment(resp, me_ref[0], blocks)[0], normalizer, layout, out_ref, flip)
    store_low(low_ref, layout, out_ref, flip)


def tree(values):
    while len(values) > 1:
        values = [values[i] + values[i + 1] for i in range(0, len(values), 2)]
    return values[0]


def decoded_sum(refs, side, layout):
    row = lax.broadcasted_iota(jnp.int32, (layout.half, LANES), 0) + side * layout.half
    is_second, is_first = row < layout.firsts, row < layout.counts

    def at_rows(second, first):
        return jnp.where(is_second, power(second), jnp.where(is_first, power(first), 1.0))

    seconds = [r[layout.half : layout.half + 1, :] for r in refs]
    firsts = [r[layout.half + 1 : layout.half + 2, :] for r in refs]
    total = tree([r[: layout.half, :] * at_rows(s, f) for r, s, f in zip(refs, seconds, firsts, strict=True)])
    return total, seconds, firsts, at_rows


def highest(values):
    return values[0] if len(values) == 1 else jnp.maximum(values[0], highest(values[1:]))


def early_kernel(layout, count, me_ref, *refs):
    refs, out_ref = refs[:-1], refs[-1]
    total, _, _, _ = decoded_sum(refs[:count], me_ref[1], layout)
    out_ref[: layout.half, :] = total
    for line in range(2):
        out_ref[layout.half + line : layout.half + line + 1, :] = highest(
            [r[layout.half + line : layout.half + line + 1, :] for r in refs]
        )
    out_ref[layout.half + 2 :, :] = jnp.zeros((HEAD - 2, LANES), jnp.float32)


def combine_kernel(layout, early, me_ref, *refs):
    refs, out_ref = refs[:-1], refs[-1]
    total, seconds, firsts, at_rows = decoded_sum(refs[early:], me_ref[1], layout)
    if early:
        total = refs[0][: layout.half, :] + total
        seconds.append(refs[0][layout.half : layout.half + 1, :])
        firsts.append(refs[0][layout.half + 1 : layout.half + 2, :])
    grow = float((2 * len(refs) - 1).bit_length())
    second, first = highest(seconds) + grow, highest(firsts) + grow
    out_ref[: layout.half, :] = total * at_rows(-second, -first)
    out_ref[layout.half :, :] = jnp.broadcast_to(first, (HEAD, LANES))
    out_ref[layout.half : layout.half + 1, :] = second


def finish_kernel(layout, count, me_ref, *refs):
    mine, others = refs[:count], refs[count : 2 * count]
    second_ref, first_ref, count_ref, table_ref = refs[2 * count :]
    side = me_ref[1]
    for part, messages in ((0, mine), (1, others)):
        total, _, _, _ = decoded_sum(messages, side ^ part, layout)
        table_ref[pl.ds(pl.multiple_of((side ^ part) * layout.half, 8), layout.half), :] = total
    parts, comps = layout.parts, layout.comps
    i, j = pair_masks()

    def place(a, b, block):
        second_ref[a * LANES : (a + 1) * LANES, b * LANES : (b + 1) * LANES] = block

    at = 0
    for a in range(parts):
        for b in range(a + 1, parts):
            block = table_ref[at : at + LANES, :]
            place(a, b, block)
            place(b, a, block.T)
            at += LANES
    lines = [table_ref[layout.diagonals + a : layout.diagonals + a + 1, :] for a in range(parts)]
    for a in range(0, parts - 1, 2):
        block = table_ref[at : at + LANES, :]
        turned = block.T
        place(a, a, jnp.where(i <= j, block, turned))
        place(a + 1, a + 1, jnp.where(i == j, lines[a + 1], jnp.where(i > j, block, turned)))
        at += LANES
    if parts % 2:
        half = LANES // 2
        block = table_ref[at : at + half, :]
        upper = jnp.where((i <= j)[:half], block, 0.0)
        lower = pltpu.roll(jnp.where((i > j)[:half], block, 0.0), half, 1)
        whole = jnp.concatenate([upper, lower], axis=0)
        place(parts - 1, parts - 1, jnp.where(i == j, lines[-1], whole + whole.T))
    at = layout.firsts
    for a in range(parts):
        first_ref[:, a * LANES : (a + 1) * LANES] = table_ref[at : at + comps, :]
        at += comps
    count_ref[...] = table_ref[at : at + comps, :].T[0:1, :]


def call(kernel, out_shape, args, flops, scratch=()):
    specs = [pl.BlockSpec(memory_space=pltpu.VMEM)] * len(args)
    if args[0].dtype == jnp.int32:
        specs[0] = pl.BlockSpec(memory_space=pltpu.SMEM)
    moved = sum(a.size * a.dtype.itemsize for a in args) + sum(
        o.size * o.dtype.itemsize for o in jax.tree.leaves(out_shape)
    )
    return pl.pallas_call(
        kernel,
        out_shape=out_shape,
        in_specs=specs,
        out_specs=jax.tree.map(lambda _: pl.BlockSpec(memory_space=pltpu.VMEM), out_shape),
        scratch_shapes=list(scratch),
        compiler_params=pltpu.CompilerParams(vmem_limit_bytes=VMEM_LIMIT),
        cost_estimate=pl.CostEstimate(flops=flops, bytes_accessed=moved, transcendentals=0),
    )(*args)


def solution(mesh):
    n_blk, n_rows = mesh.shape["blk"], mesh.shape["rows"]
    groups = n_blk // 4

    def hop(value, blk, rows):
        if rows == 0:
            return lax.ppermute(value, "blk", [(i, i ^ blk) for i in range(n_blk)])
        if blk == 0:
            return lax.ppermute(value, "rows", [(i, i ^ rows) for i in range(n_rows)])
        pairs = [
            (i * n_rows + j, (i ^ blk) * n_rows + (j ^ rows)) for i in range(n_blk) for j in range(n_rows)
        ]
        return lax.ppermute(value, ("blk", "rows"), pairs)

    def shards(embeddings, factors, centres, log_prior):
        rows, width = embeddings.shape
        comps = factors.shape[0] * n_blk
        normalizer = comps / (rows * n_blk * n_rows)
        layout = Layout(width, comps)
        low_rows = 2 * layout.half - layout.firsts + HEAD
        me = jnp.stack([lax.axis_index("blk"), lax.axis_index("rows") & 1]).astype(jnp.int32)

        near = hop(embeddings, 2, 0)
        matrix = factors.reshape(width, width)
        tail = jnp.concatenate(
            [
                centres,
                jnp.broadcast_to(log_prior[:, None], (1, width)),
                jnp.zeros((TAIL - 2, width), jnp.bfloat16),
            ],
            axis=0,
        )
        core = hop(embeddings, 1, 0)
        matrices = [hop(matrix, 4 * b, 0) for b in range(1, groups)]
        tails = [hop(tail, 4 * b, 0) for b in range(1, groups)]
        flops = 2 * rows * width * width
        line = lambda count, lanes: jax.ShapeDtypeStruct((count, lanes * rows), jnp.float32)
        turned = jax.ShapeDtypeStruct((width, width), jnp.bfloat16)
        own_scores, own_turned = call(
            own_kernel, (line(1, 2), turned), (embeddings, core, matrix, tail), 2 * flops
        )
        near, matrices, tails, own_scores = lax.optimization_barrier((near, matrices, tails, own_scores))
        far = hop(near, 1, 0)
        blocks = (embeddings, near, core, far)
        tails = [tail] + tails
        most_scores, other_turned = call(
            lambda *refs: near_kernel(groups, *refs),
            (line(groups, 3), jax.ShapeDtypeStruct((groups - 1, width, width), jnp.bfloat16)),
            (embeddings, near, core, own_scores, own_turned, *tails, *matrices),
            (3 * groups - 2) * flops,
        )
        scores = call(
            lambda *refs: far_kernel(groups, *refs),
            line(groups, 4),
            (far, most_scores, own_turned, other_turned, *tails),
            groups * flops,
        )
        near_scores = hop(scores, 2, 0)
        core_scores = hop(scores, 1, 0)
        far_scores = hop(near_scores, 1, 0)

        sent = jax.ShapeDtypeStruct((layout.rows, LANES), jnp.float32)
        message = jax.ShapeDtypeStruct((2, layout.rows, LANES), jnp.float32)
        flops = 4 * 4 * rows * width * width
        resp, low, here, *given = call(
            lambda *refs: give_kernel([4 * b for b in range(1, groups)], normalizer, layout, *refs),
            (
                jax.ShapeDtypeStruct((comps, 4 * rows), jnp.float32),
                jax.ShapeDtypeStruct((low_rows, LANES), jnp.float32),
                jax.ShapeDtypeStruct((comps, rows), jnp.float32),
                *[message] * (groups - 1),
            ),
            (me, scores, core_scores, near_scores, far_scores, *blocks),
            flops * (groups - 1),
            [pltpu.VMEM((comps, 4 * rows), jnp.float32)],
        )
        received = {}
        for b in range(1, groups):
            for z in (1, 0):
                received[b, z] = hop(given[b - 1][z].astype(jnp.float16), 4 * b, z)
        kept = call(
            lambda *refs: keep_kernel(normalizer, layout, *refs),
            message,
            (me, resp, low, *blocks),
            flops,
        )
        received[0, 0] = lax.optimization_barrier(kept[0].astype(jnp.float16))
        received[0, 1] = hop(kept[1].astype(jnp.float16), 0, 1)
        wide = {key: value.astype(jnp.float32) for key, value in received.items()}
        same = [wide[b, 0] for b in range(groups)]
        other = [wide[b, 1] for b in range(1, groups)]
        early = call(
            lambda *refs: early_kernel(layout, groups, *refs), sent, (me, *same, *other), EARLY_COST
        )
        summed = call(
            lambda *refs: combine_kernel(layout, 1, *refs), sent, (me, early, wide[0, 1], *other), 0
        )
        summed = lax.optimization_barrier(summed.astype(jnp.float16))
        bit = 2
        while 2 * bit < n_rows:
            messages = [m.astype(jnp.float32) for m in (summed, hop(summed, 0, bit))]
            summed = call(
                lambda *refs: combine_kernel(layout, 0, *refs), sent, (me, *messages), 0
            )
            summed = lax.optimization_barrier(summed.astype(jnp.float16))
            bit *= 2
        last = [0, bit] if bit < n_rows else [0]
        others = [hop(summed, 0, 1 ^ z) for z in reversed(last)][::-1]
        mine = [summed] + [hop(summed, 0, z) for z in last[1:]]
        second, first, count = call(
            lambda *refs: finish_kernel(layout, len(last), *refs),
            (
                jax.ShapeDtypeStruct((width, width), jnp.float32),
                jax.ShapeDtypeStruct((comps, width), jnp.float32),
                jax.ShapeDtypeStruct((1, comps), jnp.float32),
            ),
            (me, *[m.astype(jnp.float32) for m in mine + others]),
            0,
            [pltpu.VMEM((2 * layout.half, LANES), jnp.float32)],
        )
        return here, count.reshape(comps), first, second.reshape(1, width, width)

    in_specs = (P(("blk", "rows"), None), P("blk", None, None), P("blk", None), P("blk"))
    out_specs = (P(None, ("blk", "rows")), P(), P(), P("blk", None, None))
    return jax.shard_map(shards, mesh=mesh, in_specs=in_specs, out_specs=out_specs, check_vma=False)
```

time: 52.3 us -> 47.3 us (0.904)
  waiting for transfers between devices: 28.2 us -> 17.5 us
  Pallas kernels: 6.66 us -> 10 us
  local copies, waits for them, and re-layouts: 0.16 us -> 2.79 us
  other arithmetic: 2.57 us -> 0.32 us
  starting transfers between devices: 13.1 us -> 15 us
    ppermute x10 -> x9, waiting for transfers between devices: 15.6 us -> 9.14 us  [hop(): return lax.ppermute(value, 'blk', [(i, i ^ blk) for i in range(n_blk)])]
    pallas_call x4 -> x8, Pallas kernels: 6.66 us -> 10 us  [call(): pl.pallas_call(kernel, out_shape=out_shape, in_specs=specs, out_specs=jax...]
    ppermute x2 -> x4, waiting for transfers between devices: 9.25 us -> 6.3 us  [hop(): return lax.ppermute(value, 'rows', [(i, i ^ rows) for i in range(n_rows)])]
    unnamed x2 -> x8, local copies, waits for them, and re-layouts: 0.01 us -> 2.56 us
    ppermute x2 -> x4, starting transfers between devices: 3.15 us -> 4.7 us  [hop(): return lax.ppermute(value, 'rows', [(i, i ^ rows) for i in range(n_rows)])]
    ppermute x1, waiting for transfers between devices: 3.38 us -> 2.05 us  [hop(): return lax.ppermute(value, ('blk', 'rows'), pairs)]
    ppermute x1, starting transfers between devices: 1.58 us -> 2.88 us  [hop(): return lax.ppermute(value, ('blk', 'rows'), pairs)]
    concatenate x1, other arithmetic: 1.15 us -> 0.07 us  [shards(): jnp.concatenate([centres, jnp.broadcast_to(log_prior[:, None], (1, width)...]
  transfers between devices with their start and end apart: 13 -> 14, of which waited for: 7 -> 10; matrix products, arithmetic and copies ran while one was open for 0% -> 1% of each run, Pallas kernels for 8% -> 5%
where the time goes in v2:
time: 47.3 us; the launch traced here: 47.1 us
  waiting for transfers between devices  17.5 us (37%)
  starting transfers between devices  15 us (32%)
  Pallas kernels  10 us (21%)
  local copies, waits for them, and re-layouts  2.79 us (6%)
  between operations  1.43 us (3%)
    pallas_call x8, Pallas kernels, call(): pl.pallas_call(kernel, out_shape=out_shape, in_specs=specs, out_specs=jax...  10 us
    ppermute x9, waiting for transfers between devices, hop(): return lax.ppermute(value, 'blk', [(i, i ^ blk) for i in range(n_blk)])  9.14 us
    ppermute x9, starting transfers between devices, hop(): return lax.ppermute(value, 'blk', [(i, i ^ blk) for i in range(n_blk)])  7.44 us
    ppermute x4, waiting for transfers between devices, hop(): return lax.ppermute(value, 'rows', [(i, i ^ rows) for i in range(n_rows)])  6.3 us
    ppermute x4, starting transfers between devices, hop(): return lax.ppermute(value, 'rows', [(i, i ^ rows) for i in range(n_rows)])  4.7 us
    ppermute x1, starting transfers between devices, hop(): return lax.ppermute(value, ('blk', 'rows'), pairs)  2.88 us
    unnamed x8, local copies, waits for them, and re-layouts  2.56 us
    ppermute x1, waiting for transfers between devices, hop(): return lax.ppermute(value, ('blk', 'rows'), pairs)  2.05 us
  transfers between devices with their start and end apart: 14, of which 10 were waited for; matrix products, arithmetic and copies ran while one was open for 1% of the time, Pallas kernels for 5%

profile of v2, /device:TPU:0, one launch (start us, length us, event | category | flops | bytes accessed | tf_op | source)
XLA Modules:
  0.0 47.1 jit_solution(16716054012387955090)
XLA Ops:
  0.6 0.5 %collective-permute-start.3 = (bf16[512,384]{1,0:T(8,128)(2,1)}, bf16[512,384]{1,0:T(8,128)(2,1)S(1)}, u32[]{:S(2)}, u32[]{:S(2)}) collective-permute-start(bf16[512,384]{1,0:T(8,128)(2,1)} %refs_3_.1), channel_id=1, source_target_pairs={{0,4},{4,0},{8,12},{12,8},{16,20},{20,16},{24,28},{28,24},{1,5},{5... | collective-permute-start | bytes 1179656 | tf_op jit(solution)/shard_map/ppermute | solution.py:341
  1.1 2.6 %collective-permute-start = (bf16[512,384]{1,0:T(8,128)(2,1)}, bf16[512,384]{1,0:T(8,128)(2,1)S(1)}, u32[]{:S(2)}, u32[]{:S(2)}) collective-permute-start(bf16[512,384]{1,0:T(8,128)(2,1)} %refs_3_.1), channel_id=1, source_target_pairs={{0,8},{4,12},{8,0},{12,4},{16,24},{20,28},{24,16},{28,20},{1,9},{5... | collective-permute-start | bytes 1179656 | tf_op jit(solution)/shard_map/ppermute | solution.py:341
  3.7 1.5 %collective-permute-start.1 = (bf16[384,384]{1,0:T(8,128)(2,1)}, bf16[384,384]{1,0:T(8,128)(2,1)S(1)}, u32[]{:S(2)}, u32[]{:S(2)}) collective-permute-start(bf16[384,384]{1,0:T(8,128)(2,1)} %bitcast.14), channel_id=1, source_target_pairs={{0,16},{4,20},{8,24},{12,28},{16,0},{20,4},{24,8},{28,12},{1,17},{... | collective-permute-start | bytes 884744 | tf_op jit(solution)/shard_map/ppermute | solution.py:341
  5.9 0.1 pad.1.clone
  6.0 0.0 copy-start.3
  6.0 0.1 pad.2.clone
  6.1 0.6 %copy-done.3 = bf16[1,384]{1,0:T(2,128)(2,1)S(1)} copy-done((bf16[1,384]{1,0:T(2,128)(2,1)S(1)}, bf16[1,384]{1,0:T(2,128)(2,1)}, u32[]{:S(2)}) %copy-start.3) | copy-done | bytes 792
  6.7 0.1 maximum_maximum_fusion.tail_ref.refs_5_.refs_4_
  6.7 0.5 %collective-permute-start.2 = (bf16[16,384]{1,0:T(8,128)(2,1)S(1)}, bf16[16,384]{1,0:T(8,128)(2,1)S(1)}, u32[]{:S(2)}, u32[]{:S(2)}) collective-permute-start(bf16[16,384]{1,0:T(8,128)(2,1)S(1)} %maximum_maximum_fusion.tail_ref.refs_5_.refs_4_), channel_id=1, source_target_pairs={{0,16},{4,20},{8,24},{12,28},{16,0},{20,4},{24,8},{28,12},{1,17},{... | collective-permute-start | bytes 36872 | tf_op jit(solution)/shard_map/ppermute | solution.py:341
  7.2 0.0 collective-permute-done.3.core_ref.refs_2_.refs_7_.refs_5_
  7.2 0.0 copy-start
  7.2 1.0 %copy-done = bf16[512,384]{1,0:T(8,128)(2,1)S(1)} copy-done((bf16[512,384]{1,0:T(8,128)(2,1)S(1)}, bf16[512,384]{1,0:T(8,128)(2,1)}, u32[]{:S(2)}) %copy-start) | copy-done | bytes 393240
  8.2 0.0 copy-start.2
  8.2 1.0 %copy-done.2 = bf16[1,384,384]{2,1,0:T(8,128)(2,1)S(1)} copy-done((bf16[1,384,384]{2,1,0:T(8,128)(2,1)S(1)}, bf16[1,384,384]{2,1,0:T(8,128)(2,1)}, u32[]{:S(2)}) %copy-start.2) | copy-done | bytes 294936
  9.2 0.7 %shard_map.75 = (f32[1,1024]{1,0:T(1,128)S(1)}, bf16[384,384]{1,0:T(8,128)(2,1)S(1)}) custom-call(bf16[512,384]{1,0:T(8,128)(2,1)S(1)} %copy-done, bf16[512,384]{1,0:T(8,128)(2,1)S(1)} %collective-permute-done.3.core_ref.refs_2_.refs_7_.refs_5_, bf16[384,384]{1,0:T(8,128)(2,1)S(1)} %bitcast.15, bf16[16,384]{1,0:T(8,128)(2,1)S(1)} %maximum_maximum_fusion.tail_ref.refs_5_.refs_4_), custom_call_target="tpu_custom_call" | custom-call | flops 301989888 | bytes 1392640 | tf_op jit(solution)/shard_map/pallas_call | solution.py:324
  9.9 3.4 %collective-permute-done.2.refs_6_.refs_5_ = bf16[16,384]{1,0:T(8,128)(2,1)S(1)} collective-permute-done((bf16[16,384]{1,0:T(8,128)(2,1)S(1)}, bf16[16,384]{1,0:T(8,128)(2,1)S(1)}, u32[]{:S(2)}, u32[]{:S(2)}) %collective-permute-start.2) | collective-permute-done | bytes 12320 | tf_op jit(solution)/shard_map/ppermute | solution.py:341
  13.3 0.0 collective-permute-done.1.refs_7_
  13.3 0.4 collective-permute-done.refs_1_.refs_6_.refs_4_
  13.6 0.0 collective-permute-start.4
  13.6 1.1 %shard_map.76 = (f32[2,1536]{1,0:T(2,128)S(1)}, bf16[1,384,384]{2,1,0:T(8,128)(2,1)S(1)}) custom-call(bf16[512,384]{1,0:T(8,128)(2,1)S(1)} %copy-done, bf16[512,384]{1,0:T(8,128)(2,1)S(1)} %collective-permute-done.refs_1_.refs_6_.refs_4_, bf16[512,384]{1,0:T(8,128)(2,1)S(1)} %collective-permute-done.3.core_ref.refs_2_.refs_7_.refs_5_, ...), custom_call_target="tpu_custom_call" | custom-call | flops 603979776 | bytes 2105344 | tf_op jit(solution)/shard_map/pallas_call | solution.py:324
  14.7 0.6 %collective-permute-done.4.refs_0_.refs_8_.refs_6_ = bf16[512,384]{1,0:T(8,128)(2,1)S(1)} collective-permute-done((bf16[512,384]{1,0:T(8,128)(2,1)S(1)}, bf16[512,384]{1,0:T(8,128)(2,1)S(1)}, u32[]{:S(2)}, u32[]{:S(2)}) %collective-permute-start.4) | collective-permute-done | bytes 393248 | tf_op jit(solution)/shard_map/ppermute | solution.py:341
  15.4 0.0 copy-start.1
  15.4 0.6 %shard_map.77.refs_1_ = f32[2,2048]{1,0:T(2,128)S(1)} custom-call(bf16[512,384]{1,0:T(8,128)(2,1)S(1)} %collective-permute-done.4.refs_0_.refs_8_.refs_6_, f32[2,1536]{1,0:T(2,128)S(1)} %get-tuple-element.25.refs_1_, bf16[384,384]{1,0:T(8,128)(2,1)S(1)} %get-tuple-element.22.refs_4_.refs_2_, bf16[1,384,384]{2,1,0:T(8,128)(2,1)S(1)} %get-tuple-element.26.refs_3_, ...), custom_call_target="tpu_custom_call" | custom-call | flops 301989888 | bytes 1036288 | tf_op jit(solution)/shard_map/pallas_call | solution.py:324
  16.0 1.8 %collective-permute-start.6 = (f32[2,2048]{1,0:T(2,128)S(1)}, f32[2,2048]{1,0:T(2,128)S(1)}, u32[]{:S(2)}, u32[]{:S(2)}) collective-permute-start(f32[2,2048]{1,0:T(2,128)S(1)} %shard_map.77.refs_1_), channel_id=1, source_target_pairs={{0,8},{4,12},{8,0},{12,4},{16,24},{20,28},{24,16},{28,20},{1,9},{5... | collective-permute-start | bytes 49160 | tf_op jit(solution)/shard_map/ppermute | solution.py:341
  17.8 0.0 collective-permute-start.5
  17.8 2.0 %collective-permute-done.6.refs_3_ = f32[2,2048]{1,0:T(2,128)S(1)} collective-permute-done((f32[2,2048]{1,0:T(2,128)S(1)}, f32[2,2048]{1,0:T(2,128)S(1)}, u32[]{:S(2)}, u32[]{:S(2)}) %collective-permute-start.6) | collective-permute-done | bytes 16416 | tf_op jit(solution)/shard_map/ppermute | solution.py:341
  19.8 0.0 collective-permute-start.7
  19.8 0.1 pad_add_fusion.refs_0_
  19.9 0.0 collective-permute-done.5.refs_2_
  19.9 1.1 %collective-permute-done.7.refs_4_ = f32[2,2048]{1,0:T(2,128)S(1)} collective-permute-done((f32[2,2048]{1,0:T(2,128)S(1)}, f32[2,2048]{1,0:T(2,128)S(1)}, u32[]{:S(2)}, u32[]{:S(2)}) %collective-permute-start.7) | collective-permute-done | bytes 16416 | tf_op jit(solution)/shard_map/ppermute | solution.py:341
  21.0 0.0 copy-done.1
  21.0 2.5 %shard_map.78 = (f32[8,2048]{1,0:T(8,128)S(1)}, f32[48,128]{1,0:T(8,128)S(1)}, f32[8,512]{1,0:T(8,128)}, f32[2,320,128]{2,1,0:T(8,128)S(1)}) custom-call(s32[2]{0:T(128)S(1)} %pad_add_fusion.refs_0_, f32[2,2048]{1,0:T(2,128)S(1)} %shard_map.77.refs_1_, f32[2,2048]{1,0:T(2,128)S(1)} %collective-permute-done.5.refs_2_, ...), custom_call_target="tpu_custom_call" | custom-call | flops 1207959552 | bytes 2072584 | tf_op jit(solution)/shard_map/pallas_call | solution.py:324
  23.5 2.1 %shard_map.79 = f32[2,320,128]{2,1,0:T(8,128)S(1)} custom-call(s32[2]{0:T(128)S(1)} %pad_add_fusion.refs_0_, f32[8,2048]{1,0:T(8,128)S(1)} %get-tuple-element.28.refs_1_, f32[48,128]{1,0:T(8,128)S(1)} %get-tuple-element.29.refs_2_, bf16[512,384]{1,0:T(8,128)(2,1)S(1)} %copy-done.1, bf16[512,384]{1,0:T(8,128)(2,1)S(1)} %collective-permute-done.refs_1_.refs_6_.refs_4_, ...), custom_call_target="tpu_custom_call" | custom-call | flops 1207959552 | bytes 1990664 | tf_op jit(solution)/shard_map/pallas_call | solution.py:324
  25.7 2.9 %collective-permute-start.9 = (f16[320,128]{1,0:T(8,128)(2,1)S(1)}, f16[320,128]{1,0:T(8,128)(2,1)S(1)}, u32[]{:S(2)}, u32[]{:S(2)}) collective-permute-start(f16[320,128]{1,0:T(8,128)(2,1)S(1)} %get-tuple-element.36), channel_id=1, source_target_pairs={{0,17},{1,16},{2,19},{3,18},{4,21},{5,20},{6,23},{7,22},{8,25},{9,... | collective-permute-start | bytes 245768 | tf_op jit(solution)/shard_map/ppermute | solution.py:347
  28.6 0.5 %collective-permute-start.8 = (f16[320,128]{1,0:T(8,128)(2,1)S(1)}, f16[320,128]{1,0:T(8,128)(2,1)S(1)}, u32[]{:S(2)}, u32[]{:S(2)}) collective-permute-start(f16[320,128]{1,0:T(8,128)(2,1)S(1)} %get-tuple-element.37), channel_id=1, source_target_pairs={{0,16},{4,20},{8,24},{12,28},{16,0},{20,4},{24,8},{28,12},{1,17},{... | collective-permute-start | bytes 245768 | tf_op jit(solution)/shard_map/ppermute | solution.py:341
  29.1 0.2 collective-permute-start.10
  29.4 2.1 %collective-permute-done.9 = f16[320,128]{1,0:T(8,128)(2,1)S(1)} collective-permute-done((f16[320,128]{1,0:T(8,128)(2,1)S(1)}, f16[320,128]{1,0:T(8,128)(2,1)S(1)}, u32[]{:S(2)}, u32[]{:S(2)}) %collective-permute-start.9) | collective-permute-done | bytes 81952 | tf_op jit(solution)/shard_map/ppermute | solution.py:347
  31.4 1.7 %collective-permute-done.8 = f16[320,128]{1,0:T(8,128)(2,1)S(1)} collective-permute-done((f16[320,128]{1,0:T(8,128)(2,1)S(1)}, f16[320,128]{1,0:T(8,128)(2,1)S(1)}, u32[]{:S(2)}, u32[]{:S(2)}) %collective-permute-start.8) | collective-permute-done | bytes 81952 | tf_op jit(solution)/shard_map/ppermute | solution.py:341
  33.1 0.6 %shard_map.80.refs_1_ = f32[320,128]{1,0:T(8,128)S(1)} custom-call(s32[2]{0:T(128)S(1)} %pad_add_fusion.refs_0_, f32[320,128]{1,0:T(8,128)S(1)} %convert_element_type.44.refs_1_, f32[320,128]{1,0:T(8,128)S(1)} %convert_element_type.46.refs_2_, f32[320,128]{1,0:T(8,128)S(1)} %convert_element_type.48.refs_3_), custom_call_target="tpu_custom_call" | custom-call | bytes 655368 | tf_op jit(solution)/shard_map/pallas_call | solution.py:324
  33.7 0.0 collective-permute-done.10
  33.8 0.7 %shard_map.81 = f32[320,128]{1,0:T(8,128)S(1)} custom-call(s32[2]{0:T(128)S(1)} %pad_add_fusion.refs_0_, f32[320,128]{1,0:T(8,128)S(1)} %shard_map.80.refs_1_, f32[320,128]{1,0:T(8,128)S(1)} %convert_element_type.50.refs_2_, f32[320,128]{1,0:T(8,128)S(1)} %convert_element_type.48.refs_3_), custom_call_target="tpu_custom_call" | custom-call | bytes 655368 | tf_op jit(solution)/shard_map/pallas_call | solution.py:324
  34.5 3.8 %collective-permute-start.13 = (f16[320,128]{1,0:T(8,128)(2,1)S(1)}, f16[320,128]{1,0:T(8,128)(2,1)S(1)}, u32[]{:S(2)}, u32[]{:S(2)}) collective-permute-start(f16[320,128]{1,0:T(8,128)(2,1)S(1)} %convert_element_type.51), channel_id=1, source_target_pairs={{0,3},{1,2},{2,1},{3,0},{4,7},{5,6},{6,5},{7,4},{8,11},{9,10},{10,... | collective-permute-start | bytes 245768 | tf_op jit(solution)/shard_map/ppermute | solution.py:343
  38.2 0.0 collective-permute-start.12
  38.2 0.7 %collective-permute-start.11 = (f16[320,128]{1,0:T(8,128)(2,1)S(1)}, f16[320,128]{1,0:T(8,128)(2,1)S(1)}, u32[]{:S(2)}, u32[]{:S(2)}) collective-permute-start(f16[320,128]{1,0:T(8,128)(2,1)S(1)} %convert_element_type.51), channel_id=1, source_target_pairs={{0,2},{1,3},{2,0},{3,1},{4,6},{5,7},{6,4},{7,5},{8,10},{9,11},{10,... | collective-permute-start | bytes 245768 | tf_op jit(solution)/shard_map/ppermute | solution.py:343
  38.9 2.8 %collective-permute-done.13 = f16[320,128]{1,0:T(8,128)(2,1)S(1)} collective-permute-done((f16[320,128]{1,0:T(8,128)(2,1)S(1)}, f16[320,128]{1,0:T(8,128)(2,1)S(1)}, u32[]{:S(2)}, u32[]{:S(2)}) %collective-permute-start.13) | collective-permute-done | bytes 81952 | tf_op jit(solution)/shard_map/ppermute | solution.py:343
  41.7 2.7 %collective-permute-done.12 = f16[320,128]{1,0:T(8,128)(2,1)S(1)} collective-permute-done((f16[320,128]{1,0:T(8,128)(2,1)S(1)}, f16[320,128]{1,0:T(8,128)(2,1)S(1)}, u32[]{:S(2)}, u32[]{:S(2)}) %collective-permute-start.12) | collective-permute-done | bytes 81952 | tf_op jit(solution)/shard_map/ppermute | solution.py:343
  44.5 0.8 %collective-permute-done.11 = f16[320,128]{1,0:T(8,128)(2,1)S(1)} collective-permute-done((f16[320,128]{1,0:T(8,128)(2,1)S(1)}, f16[320,128]{1,0:T(8,128)(2,1)S(1)}, u32[]{:S(2)}, u32[]{:S(2)}) %collective-permute-start.11) | collective-permute-done | bytes 81952 | tf_op jit(solution)/shard_map/ppermute | solution.py:343
  45.3 1.8 %shard_map.82 = (f32[384,384]{1,0:T(8,128)}, f32[8,384]{1,0:T(8,128)}, f32[1,8]{1,0:T(1,128)}) custom-call(s32[2]{0:T(128)S(1)} %pad_add_fusion.refs_0_, f32[320,128]{1,0:T(8,128)S(1)} %convert_element_type.52.refs_1_, f32[320,128]{1,0:T(8,128)S(1)} %convert_element_type.53.refs_2_, f32[320,128]{1,0:T(8,128)S(1)} %convert_element_type.54.refs_3_, ...), custom_call_target="tpu_custom_call" | custom-call | bytes 1257512 | tf_op jit(solution)/shard_map/pallas_call | solution.py:324
  (14 shorter events, 0.2 us)
Async XLA Ops:
  0.6 6.6 %collective-permute-start.3 = (bf16[512,384]{1,0:T(8,128)(2,1)}, bf16[512,384]{1,0:T(8,128)(2,1)S(1)}, u32[]{:S(2)}, u32[]{:S(2)}) collective-permute-start(bf16[512,384]{1,0:T(8,128)(2,1)} %refs_3_.1), channel_id=1, source_target_pairs={{0,4},{4,0},{8,12},{12,8},{16,20},{20,16},{24,28},{28,24},{1,5},{5... | collective-permute-start | bytes 1179656 | tf_op jit(solution)/shard_map/ppermute | solution.py:341
  1.1 12.5 %collective-permute-start = (bf16[512,384]{1,0:T(8,128)(2,1)}, bf16[512,384]{1,0:T(8,128)(2,1)S(1)}, u32[]{:S(2)}, u32[]{:S(2)}) collective-permute-start(bf16[512,384]{1,0:T(8,128)(2,1)} %refs_3_.1), channel_id=1, source_target_pairs={{0,8},{4,12},{8,0},{12,4},{16,24},{20,28},{24,16},{28,20},{1,9},{5... | collective-permute-start | bytes 1179656 | tf_op jit(solution)/shard_map/ppermute | solution.py:341
  3.7 9.6 %collective-permute-start.1 = (bf16[384,384]{1,0:T(8,128)(2,1)}, bf16[384,384]{1,0:T(8,128)(2,1)S(1)}, u32[]{:S(2)}, u32[]{:S(2)}) collective-permute-start(bf16[384,384]{1,0:T(8,128)(2,1)} %bitcast.14), channel_id=1, source_target_pairs={{0,16},{4,20},{8,24},{12,28},{16,0},{20,4},{24,8},{28,12},{1,17},{... | collective-permute-start | bytes 884744 | tf_op jit(solution)/shard_map/ppermute | solution.py:341
  6.0 0.7 %copy-start.3 = (bf16[1,384]{1,0:T(2,128)(2,1)S(1)}, bf16[1,384]{1,0:T(2,128)(2,1)}, u32[]{:S(2)}) copy-start(bf16[1,384]{1,0:T(2,128)(2,1)} %param.6) | copy-start | bytes 2308
  6.7 6.5 %collective-permute-start.2 = (bf16[16,384]{1,0:T(8,128)(2,1)S(1)}, bf16[16,384]{1,0:T(8,128)(2,1)S(1)}, u32[]{:S(2)}, u32[]{:S(2)}) collective-permute-start(bf16[16,384]{1,0:T(8,128)(2,1)S(1)} %maximum_maximum_fusion.tail_ref.refs_5_.refs_4_), channel_id=1, source_target_pairs={{0,16},{4,20},{8,24},{12,28},{16,0},{20,4},{24,8},{28,12},{1,17},{... | collective-permute-start | bytes 36872 | tf_op jit(solution)/shard_map/ppermute | solution.py:341
  7.2 1.0 %copy-start = (bf16[512,384]{1,0:T(8,128)(2,1)S(1)}, bf16[512,384]{1,0:T(8,128)(2,1)}, u32[]{:S(2)}) copy-start(bf16[512,384]{1,0:T(8,128)(2,1)} %refs_3_.1) | copy-start | bytes 1179652
  8.2 1.0 %copy-start.2 = (bf16[1,384,384]{2,1,0:T(8,128)(2,1)S(1)}, bf16[1,384,384]{2,1,0:T(8,128)(2,1)}, u32[]{:S(2)}) copy-start(bf16[1,384,384]{2,1,0:T(8,128)(2,1)} %param.5) | copy-start | bytes 884740
  13.6 1.7 %collective-permute-start.4 = (bf16[512,384]{1,0:T(8,128)(2,1)S(1)}, bf16[512,384]{1,0:T(8,128)(2,1)S(1)}, u32[]{:S(2)}, u32[]{:S(2)}) collective-permute-start(bf16[512,384]{1,0:T(8,128)(2,1)S(1)} %collective-permute-done.refs_1_.refs_6_.refs_4_), channel_id=1, source_target_pairs={{0,4},{4,0},{8,12},{12,8},{16,20},{20,16},{24,28},{28,24},{1,5},{5... | collective-permute-start | bytes 1179656 | tf_op jit(solution)/shard_map/ppermute | solution.py:341
  15.4 5.6 %copy-start.1 = (bf16[512,384]{1,0:T(8,128)(2,1)S(1)}, bf16[512,384]{1,0:T(8,128)(2,1)}, u32[]{:S(2)}) copy-start(bf16[512,384]{1,0:T(8,128)(2,1)} %refs_3_.1) | copy-start | bytes 1179652
  16.0 3.8 %collective-permute-start.6 = (f32[2,2048]{1,0:T(2,128)S(1)}, f32[2,2048]{1,0:T(2,128)S(1)}, u32[]{:S(2)}, u32[]{:S(2)}) collective-permute-start(f32[2,2048]{1,0:T(2,128)S(1)} %shard_map.77.refs_1_), channel_id=1, source_target_pairs={{0,8},{4,12},{8,0},{12,4},{16,24},{20,28},{24,16},{28,20},{1,9},{5... | collective-permute-start | bytes 49160 | tf_op jit(solution)/shard_map/ppermute | solution.py:341
  17.8 2.1 %collective-permute-start.5 = (f32[2,2048]{1,0:T(2,128)S(1)}, f32[2,2048]{1,0:T(2,128)S(1)}, u32[]{:S(2)}, u32[]{:S(2)}) collective-permute-start(f32[2,2048]{1,0:T(2,128)S(1)} %shard_map.77.refs_1_), channel_id=1, source_target_pairs={{0,4},{4,0},{8,12},{12,8},{16,20},{20,16},{24,28},{28,24},{1,5},{5... | collective-permute-start | bytes 49160 | tf_op jit(solution)/shard_map/ppermute | solution.py:341
  19.8 1.2 %collective-permute-start.7 = (f32[2,2048]{1,0:T(2,128)S(1)}, f32[2,2048]{1,0:T(2,128)S(1)}, u32[]{:S(2)}, u32[]{:S(2)}) collective-permute-start(f32[2,2048]{1,0:T(2,128)S(1)} %collective-permute-done.6.refs_3_), channel_id=1, source_target_pairs={{0,4},{4,0},{8,12},{12,8},{16,20},{20,16},{24,28},{28,24},{1,5},{5... | collective-permute-start | bytes 49160 | tf_op jit(solution)/shard_map/ppermute | solution.py:341
  25.7 5.7 %collective-permute-start.9 = (f16[320,128]{1,0:T(8,128)(2,1)S(1)}, f16[320,128]{1,0:T(8,128)(2,1)S(1)}, u32[]{:S(2)}, u32[]{:S(2)}) collective-permute-start(f16[320,128]{1,0:T(8,128)(2,1)S(1)} %get-tuple-element.36), channel_id=1, source_target_pairs={{0,17},{1,16},{2,19},{3,18},{4,21},{5,20},{6,23},{7,22},{8,25},{9,... | collective-permute-start | bytes 245768 | tf_op jit(solution)/shard_map/ppermute | solution.py:347
  28.6 4.5 %collective-permute-start.8 = (f16[320,128]{1,0:T(8,128)(2,1)S(1)}, f16[320,128]{1,0:T(8,128)(2,1)S(1)}, u32[]{:S(2)}, u32[]{:S(2)}) collective-permute-start(f16[320,128]{1,0:T(8,128)(2,1)S(1)} %get-tuple-element.37), channel_id=1, source_target_pairs={{0,16},{4,20},{8,24},{12,28},{16,0},{20,4},{24,8},{28,12},{1,17},{... | collective-permute-start | bytes 245768 | tf_op jit(solution)/shard_map/ppermute | solution.py:341
  29.1 4.7 %collective-permute-start.10 = (f16[320,128]{1,0:T(8,128)(2,1)S(1)}, f16[320,128]{1,0:T(8,128)(2,1)S(1)}, u32[]{:S(2)}, u32[]{:S(2)}) collective-permute-start(f16[320,128]{1,0:T(8,128)(2,1)S(1)} %get-tuple-element.34), channel_id=1, source_target_pairs={{0,1},{1,0},{2,3},{3,2},{4,5},{5,4},{6,7},{7,6},{8,9},{9,8},{10,11... | collective-permute-start | bytes 245768 | tf_op jit(solution)/shard_map/ppermute | solution.py:343
  34.5 7.2 %collective-permute-start.13 = (f16[320,128]{1,0:T(8,128)(2,1)S(1)}, f16[320,128]{1,0:T(8,128)(2,1)S(1)}, u32[]{:S(2)}, u32[]{:S(2)}) collective-permute-start(f16[320,128]{1,0:T(8,128)(2,1)S(1)} %convert_element_type.51), channel_id=1, source_target_pairs={{0,3},{1,2},{2,1},{3,0},{4,7},{5,6},{6,5},{7,4},{8,11},{9,10},{10,... | collective-permute-start | bytes 245768 | tf_op jit(solution)/shard_map/ppermute | solution.py:343
  38.2 6.2 %collective-permute-start.12 = (f16[320,128]{1,0:T(8,128)(2,1)S(1)}, f16[320,128]{1,0:T(8,128)(2,1)S(1)}, u32[]{:S(2)}, u32[]{:S(2)}) collective-permute-start(f16[320,128]{1,0:T(8,128)(2,1)S(1)} %convert_element_type.51), channel_id=1, source_target_pairs={{0,1},{1,0},{2,3},{3,2},{4,5},{5,4},{6,7},{7,6},{8,9},{9,8},{10,11... | collective-permute-start | bytes 245768 | tf_op jit(solution)/shard_map/ppermute | solution.py:343
  38.2 7.0 %collective-permute-start.11 = (f16[320,128]{1,0:T(8,128)(2,1)S(1)}, f16[320,128]{1,0:T(8,128)(2,1)S(1)}, u32[]{:S(2)}, u32[]{:S(2)}) collective-permute-start(f16[320,128]{1,0:T(8,128)(2,1)S(1)} %convert_element_type.51), channel_id=1, source_target_pairs={{0,2},{1,3},{2,0},{3,1},{4,6},{5,7},{6,4},{7,5},{8,10},{9,11},{10,... | collective-permute-start | bytes 245768 | tf_op jit(solution)/shard_map/ppermute | solution.py:343

commit v3 on v2

--- a/solution.py
+++ b/solution.py
@@ -8,7 +8,6 @@
 half_temper = 0.05
 LANES = 128
 TAIL = 16
-EARLY_COST = 0
 HEAD = 8
 VMEM_LIMIT = 40 * 1024 * 1024
 NT = (((1,), (1,)), ((), ()))
@@ -81,26 +80,30 @@
     return unnorm / jnp.sum(unnorm, axis=0, keepdims=True)
 
 
-def moment(resp, component, blocks, extra=None):
-    width = blocks[0].shape[1]
-    parts = width // LANES
-    total = [0.0] * parts
-    products = []
-    for at, (weights, block_ref) in enumerate(zip(resp, blocks, strict=True)):
-        picked = lax.broadcasted_iota(jnp.int32, weights.shape, 0) == component
-        row = jnp.sum(jnp.where(picked, weights, 0.0), axis=0, keepdims=True)
-        block = block_ref[...]
-        high, low = split_two(block.T.astype(jnp.float32) * row)
-        for a in range(parts):
-            left = [high[a * LANES : (a + 1) * LANES], low[a * LANES : (a + 1) * LANES]]
-            if a == 0 and extra is not None:
-                left.append(extra[at])
-            left = jnp.concatenate(left, axis=0)
-            both = jnp.dot(left, block[:, a * LANES :], preferred_element_type=jnp.float32)
-            total[a] = total[a] + (both[:LANES] + both[LANES : 2 * LANES])
-            if a == 0:
-                products.append(both[2 * LANES :])
-    return total, products
+def band_pairs(parts):
+    return [[(a + d) % parts for d in range(parts // 2 + (parts % 2 or a < parts // 2))] for a in range(parts)]
+
+
+def moment(weights, component, rows_ref, columns_ref, layout, extra=None):
+    picked = lax.broadcasted_iota(jnp.int32, weights.shape, 0) == component
+    row = jnp.sum(jnp.where(picked, weights, 0.0), axis=0, keepdims=True)
+    blocks, products = {}, {}
+    for a, bands in enumerate(band_pairs(layout.parts)):
+        left = list(split_two(columns_ref[a * LANES : (a + 1) * LANES, :] * row))
+        adds = extra is not None and any(b not in products for b in bands)
+        if adds:
+            left.append(extra)
+        both = jnp.dot(
+            jnp.concatenate(left, axis=0),
+            rows_ref[:, a * LANES : (a + len(bands)) * LANES],
+            preferred_element_type=jnp.float32,
+        )
+        for d, b in enumerate(bands):
+            part = both[:, d * LANES : (d + 1) * LANES]
+            blocks[a, b] = part[:LANES] + part[LANES : 2 * LANES]
+            if adds:
+                products[b] = part[2 * LANES :]
+    return blocks, products
 
 
 def pair_masks():
@@ -113,6 +116,7 @@
     def __init__(self, width, comps):
         self.parts = width // LANES
         self.comps = comps
+        self.pairs = [(a, b) for a, bands in enumerate(band_pairs(self.parts)) for b in bands[1:]]
         off = self.parts * (self.parts - 1) // 2 * LANES
         folded = self.parts // 2 * LANES + self.parts % 2 * (LANES // 2)
         self.diagonals = off + folded
@@ -130,21 +134,19 @@
             done += count
 
 
-def store_second(total, normalizer, layout, out_ref, flip):
+def store_second(blocks, normalizer, layout, out_ref, flip):
     parts = layout.parts
     largest = jnp.zeros((1, 1), jnp.float32)
-    for band in total:
-        largest = jnp.maximum(largest, jnp.max(jnp.abs(band[:, :LANES]), keepdims=True))
+    for a in range(parts):
+        largest = jnp.maximum(largest, jnp.max(jnp.abs(blocks[a, a]), keepdims=True))
     exponent = exponent_of(largest * normalizer)
     factor = normalizer * power(-exponent)
     i, j = pair_masks()
     at = 0
-    for a in range(parts):
-        for b in range(a + 1, parts):
-            block = total[a][:, (b - a) * LANES : (b - a + 1) * LANES]
-            layout.write(out_ref, flip, at, block * factor)
-            at += LANES
-    diagonal = [band[:, :LANES] * factor for band in total]
+    for a, b in layout.pairs:
+        layout.write(out_ref, flip, at, blocks[a, b] * factor)
+        at += LANES
+    diagonal = [blocks[a, a] * factor for a in range(parts)]
     for a in range(0, parts - 1, 2):
         layout.write(out_ref, flip, at, jnp.where(i <= j, diagonal[a], diagonal[a + 1]))
         at += LANES
@@ -160,6 +162,11 @@
         out_ref[side, layout.half : layout.half + 1, :] = jnp.broadcast_to(exponent, (1, LANES))
 
 
+def part_ways(table_ref, flip, outs):
+    outs[0][...] = table_ref[flip]
+    outs[1][...] = table_ref[1 - flip]
+
+
 def store_low(low_ref, layout, out_ref, flip):
     body = low_ref.shape[0] - HEAD
     layout.write(out_ref, flip, layout.firsts, low_ref[:body, :])
@@ -167,41 +174,60 @@
         out_ref[side, layout.half + 1 :, :] = low_ref[body + 1 :, :]
 
 
-def give_kernel(offsets, normalizer, layout, me_ref, *refs):
-    scores, blocks = refs[:4], refs[4:8]
-    outs, table_ref = refs[8:-1], refs[-1]
-    resp_ref, low_ref, here_ref, *outs = outs
+def own_place(me):
+    return ((me >> 1) & 1) | ((me & 1) << 1)
+
+
+def span(place, rows):
+    return pl.ds(pl.multiple_of(place * rows, LANES), rows)
+
+
+def place_here():
+    return lax.axis_index("blk"), lax.axis_index("rows") & 1
+
+
+def turn_kernel(*refs):
+    blocks, (rows_ref, columns_ref) = refs[:-2], refs[-2:]
+    rows, width = blocks[0].shape
+    own = own_place(place_here()[0])
+    for part, block_ref in enumerate(blocks):
+        block = block_ref[...]
+        rows_ref[span(part ^ own, rows), :width] = block
+        rows_ref[span(part ^ own, rows), width:] = block[:, : rows_ref.shape[1] - width]
+        columns_ref[:, span(part ^ own, rows)] = block.T.astype(jnp.float32)
+
+
+def give_kernel(offsets, normalizer, layout, *refs):
+    scores, (rows_ref, columns_ref), refs = refs[:4], refs[4:6], refs[6:]
+    resp_ref, low_ref, here_ref, *outs, table_ref, message_ref = refs
     comps, rows = here_ref.shape
-    me, flip = me_ref[0], me_ref[1]
+    me, flip = place_here()
+    own = own_place(me)
     for source, score_ref in enumerate(scores):
         for b in range(score_ref.shape[0]):
             for part in range(4):
-                to = part ^ (((source & 1) << 1) | (source >> 1))
-                table_ref[pl.ds(me ^ (4 * b + source), 1), to * rows : (to + 1) * rows] = score_ref[
+                to = part ^ (((source & 1) << 1) | (source >> 1)) ^ own
+                table_ref[pl.ds(me ^ (4 * b + source), 1), span(to, rows)] = score_ref[
                     b : b + 1, part * rows : (part + 1) * rows
                 ]
     weights = softmax(table_ref[...])
     resp_ref[...] = weights
-    here_ref[...] = weights[:, :rows]
-    resp = [weights[:, part * rows : (part + 1) * rows] for part in range(4)]
-    stacked, counts = [], []
-    for weights in resp:
-        high = weights.astype(jnp.bfloat16).astype(jnp.float32)
-        rest = weights - high
-        middle = rest.astype(jnp.bfloat16).astype(jnp.float32)
-        pieces = [high, middle, rest - middle]
-        if 3 * comps % 16:
-            pieces.append(jnp.zeros((-3 * comps % 16, rows), jnp.float32))
-        stacked.append(jnp.concatenate(pieces, axis=0).astype(jnp.bfloat16))
-        counts.append(jnp.sum(weights, axis=1, keepdims=True))
-    totals, products = [], []
-    for at, offset in enumerate(offsets):
-        total, product = moment(resp, me ^ offset, blocks, stacked if at == 0 else None)
+    here_ref[...] = resp_ref[:, span(own, rows)]
+    high = weights.astype(jnp.bfloat16).astype(jnp.float32)
+    rest = weights - high
+    middle = rest.astype(jnp.bfloat16).astype(jnp.float32)
+    pieces = [high, middle, rest - middle]
+    if 3 * comps % 16:
+        pieces.append(jnp.zeros((-3 * comps % 16, 4 * rows), jnp.float32))
+    stacked = jnp.concatenate(pieces, axis=0).astype(jnp.bfloat16)
+    totals, products = [], {}
+    for offset in offsets:
+        total, product = moment(weights, me ^ offset, rows_ref, columns_ref, layout, None if products else stacked)
         totals.append(total)
         products = products or product
-    firsts = [p[:comps] + (p[comps : 2 * comps] + p[2 * comps : 3 * comps]) for p in products]
-    first = ((firsts[0] + firsts[2]) + (firsts[1] + firsts[3])) * normalizer
-    count = ((counts[0] + counts[2]) + (counts[1] + counts[3])) * normalizer
+    product = jnp.concatenate([products[b] for b in range(layout.parts)], axis=1)
+    first = (product[:comps] + (product[comps : 2 * comps] + product[2 * comps : 3 * comps])) * normalizer
+    count = jnp.sum(weights, axis=1, keepdims=True) * normalizer
     exponent = exponent_of(jnp.max(jnp.abs(first), keepdims=True))
     first = first * power(-exponent)
     body = low_ref.shape[0] - HEAD
@@ -211,18 +237,18 @@
     at = layout.parts * comps
     low_ref[at : at + comps, :] = jnp.broadcast_to(count, (comps, LANES))
     low_ref[body:, :] = jnp.broadcast_to(exponent, (HEAD, LANES))
-    for total, out_ref in zip(totals, outs, strict=True):
-        store_second(total, normalizer, layout, out_ref, flip)
-        store_low(low_ref, layout, out_ref, flip)
-
-
-def keep_kernel(normalizer, layout, me_ref, resp_ref, low_ref, *refs):
-    blocks, out_ref = refs[:4], refs[4]
-    rows = blocks[0].shape[0]
-    resp = [resp_ref[:, part * rows : (part + 1) * rows] for part in range(4)]
-    flip = me_ref[1]
-    store_second(moment(resp, me_ref[0], blocks)[0], normalizer, layout, out_ref, flip)
-    store_low(low_ref, layout, out_ref, flip)
+    for at, total in enumerate(totals):
+        store_second(total, normalizer, layout, message_ref, 0)
+        store_low(low_ref, layout, message_ref, 0)
+        part_ways(message_ref, flip, outs[2 * at : 2 * at + 2])
+
+
+def keep_kernel(normalizer, layout, resp_ref, low_ref, rows_ref, columns_ref, *refs):
+    outs, message_ref = refs[:2], refs[2]
+    me, flip = place_here()
+    store_second(moment(resp_ref[...], me, rows_ref, columns_ref, layout)[0], normalizer, layout, message_ref, 0)
+    store_low(low_ref, layout, message_ref, 0)
+    part_ways(message_ref, flip, outs)
 
 
 def tree(values):
@@ -248,35 +274,20 @@
     return values[0] if len(values) == 1 else jnp.maximum(values[0], highest(values[1:]))
 
 
-def early_kernel(layout, count, me_ref, *refs):
+def combine_kernel(layout, *refs):
     refs, out_ref = refs[:-1], refs[-1]
-    total, _, _, _ = decoded_sum(refs[:count], me_ref[1], layout)
-    out_ref[: layout.half, :] = total
-    for line in range(2):
-        out_ref[layout.half + line : layout.half + line + 1, :] = highest(
-            [r[layout.half + line : layout.half + line + 1, :] for r in refs]
-        )
-    out_ref[layout.half + 2 :, :] = jnp.zeros((HEAD - 2, LANES), jnp.float32)
-
-
-def combine_kernel(layout, early, me_ref, *refs):
-    refs, out_ref = refs[:-1], refs[-1]
-    total, seconds, firsts, at_rows = decoded_sum(refs[early:], me_ref[1], layout)
-    if early:
-        total = refs[0][: layout.half, :] + total
-        seconds.append(refs[0][layout.half : layout.half + 1, :])
-        firsts.append(refs[0][layout.half + 1 : layout.half + 2, :])
-    grow = float((2 * len(refs) - 1).bit_length())
+    total, seconds, firsts, at_rows = decoded_sum(refs, place_here()[1], layout)
+    grow = float((len(refs) - 1).bit_length())
     second, first = highest(seconds) + grow, highest(firsts) + grow
     out_ref[: layout.half, :] = total * at_rows(-second, -first)
     out_ref[layout.half :, :] = jnp.broadcast_to(first, (HEAD, LANES))
     out_ref[layout.half : layout.half + 1, :] = second
 
 
-def finish_kernel(layout, count, me_ref, *refs):
+def finish_kernel(layout, count, *refs):
     mine, others = refs[:count], refs[count : 2 * count]
     second_ref, first_ref, count_ref, table_ref = refs[2 * count :]
-    side = me_ref[1]
+    side = place_here()[1]
     for part, messages in ((0, mine), (1, others)):
         total, _, _, _ = decoded_sum(messages, side ^ part, layout)
         table_ref[pl.ds(pl.multiple_of((side ^ part) * layout.half, 8), layout.half), :] = total
@@ -287,12 +298,11 @@
         second_ref[a * LANES : (a + 1) * LANES, b * LANES : (b + 1) * LANES] = block
 
     at = 0
-    for a in range(parts):
-        for b in range(a + 1, parts):
-            block = table_ref[at : at + LANES, :]
-            place(a, b, block)
-            place(b, a, block.T)
-            at += LANES
+    for a, b in layout.pairs:
+        block = table_ref[at : at + LANES, :]
+        place(a, b, block)
+        place(b, a, block.T)
+        at += LANES
     lines = [table_ref[layout.diagonals + a : layout.diagonals + a + 1, :] for a in range(parts)]
     for a in range(0, parts - 1, 2):
         block = table_ref[at : at + LANES, :]
@@ -316,8 +326,6 @@
 
 def call(kernel, out_shape, args, flops, scratch=()):
     specs = [pl.BlockSpec(memory_space=pltpu.VMEM)] * len(args)
-    if args[0].dtype == jnp.int32:
-        specs[0] = pl.BlockSpec(memory_space=pltpu.SMEM)
     moved = sum(a.size * a.dtype.itemsize for a in args) + sum(
         o.size * o.dtype.itemsize for o in jax.tree.leaves(out_shape)
     )
@@ -352,7 +360,6 @@
         normalizer = comps / (rows * n_blk * n_rows)
         layout = Layout(width, comps)
         low_rows = 2 * layout.half - layout.firsts + HEAD
-        me = jnp.stack([lax.axis_index("blk"), lax.axis_index("rows") & 1]).astype(jnp.int32)
 
         near = hop(embeddings, 2, 0)
         matrix = factors.reshape(width, width)
@@ -375,7 +382,6 @@
         )
         near, matrices, tails, own_scores = lax.optimization_barrier((near, matrices, tails, own_scores))
         far = hop(near, 1, 0)
-        blocks = (embeddings, near, core, far)
         tails = [tail] + tails
         most_scores, other_turned = call(
             lambda *refs: near_kernel(groups, *refs),
@@ -389,12 +395,23 @@
             (far, most_scores, own_turned, other_turned, *tails),
             groups * flops,
         )
+        scores, far = lax.optimization_barrier((scores, far))
+        blocks = (embeddings, near, core, far)
+        both = call(
+            turn_kernel,
+            (
+                jax.ShapeDtypeStruct((4 * rows, width + layout.parts // 2 * LANES), jnp.bfloat16),
+                jax.ShapeDtypeStruct((width, 4 * rows), jnp.float32),
+            ),
+            blocks,
+            0,
+        )
         near_scores = hop(scores, 2, 0)
         core_scores = hop(scores, 1, 0)
         far_scores = hop(near_scores, 1, 0)
 
         sent = jax.ShapeDtypeStruct((layout.rows, LANES), jnp.float32)
-        message = jax.ShapeDtypeStruct((2, layout.rows, LANES), jnp.float32)
+        whole = pltpu.VMEM((2, layout.rows, LANES), jnp.float32)
         flops = 4 * 4 * rows * width * width
         resp, low, here, *given = call(
             lambda *refs: give_kernel([4 * b for b in range(1, groups)], normalizer, layout, *refs),
@@ -402,39 +419,39 @@
                 jax.ShapeDtypeStruct((comps, 4 * rows), jnp.float32),
                 jax.ShapeDtypeStruct((low_rows, LANES), jnp.float32),
                 jax.ShapeDtypeStruct((comps, rows), jnp.float32),
-                *[message] * (groups - 1),
+                *[sent] * (2 * groups - 2),
             ),
-            (me, scores, core_scores, near_scores, far_scores, *blocks),
+            (scores, core_scores, near_scores, far_scores, *both),
             flops * (groups - 1),
-            [pltpu.VMEM((comps, 4 * rows), jnp.float32)],
+            [pltpu.VMEM((comps, 4 * rows), jnp.float32), whole],
         )
         received = {}
         for b in range(1, groups):
             for z in (1, 0):
-                received[b, z] = hop(given[b - 1][z].astype(jnp.float16), 4 * b, z)
+                received[b, z] = hop(given[2 * b - 2 + z].astype(jnp.float16), 4 * b, z)
         kept = call(
             lambda *refs: keep_kernel(normalizer, layout, *refs),
-            message,
-            (me, resp, low, *blocks),
+            (sent, sent),
+            (resp, low, *both),
             flops,
+            [whole],
         )
         received[0, 0] = lax.optimization_barrier(kept[0].astype(jnp.float16))
         received[0, 1] = hop(kept[1].astype(jnp.float16), 0, 1)
+        for b in range(1, groups):
+            received[b, 0], received[b, 1] = lax.optimization_barrier((received[b, 0], received[b, 1]))
         wide = {key: value.astype(jnp.float32) for key, value in received.items()}
         same = [wide[b, 0] for b in range(groups)]
         other = [wide[b, 1] for b in range(1, groups)]
-        early = call(
-            lambda *refs: early_kernel(layout, groups, *refs), sent, (me, *same, *other), EARLY_COST
-        )
         summed = call(
-            lambda *refs: combine_kernel(layout, 1, *refs), sent, (me, early, wide[0, 1], *other), 0
+            lambda *refs: combine_kernel(layout, *refs), sent, (*same, wide[0, 1], *other), 0
         )
         summed = lax.optimization_barrier(summed.astype(jnp.float16))
         bit = 2
         while 2 * bit < n_rows:
             messages = [m.astype(jnp.float32) for m in (summed, hop(summed, 0, bit))]
             summed = call(
-                lambda *refs: combine_kernel(layout, 0, *refs), sent, (me, *messages), 0
+                lambda *refs: combine_kernel(layout, *refs), sent, messages, 0
             )
             summed = lax.optimization_barrier(summed.astype(jnp.float16))
             bit *= 2
@@ -448,7 +465,7 @@
                 jax.ShapeDtypeStruct((comps, width), jnp.float32),
                 jax.ShapeDtypeStruct((1, comps), jnp.float32),
             ),
-            (me, *[m.astype(jnp.float32) for m in mine + others]),
+            [m.astype(jnp.float32) for m in mine + others],
             0,
             [pltpu.VMEM((2 * layout.half, LANES), jnp.float32)],
         )

time: 47.3 us -> 43.3 us (0.915)
  Pallas kernels: 10 us -> 7.59 us
  waiting for transfers between devices: 17.5 us -> 16 us
  local copies, waits for them, and re-layouts: 2.79 us -> 2.12 us
  other arithmetic: 0.32 us -> 0.93 us
    pallas_call x8, Pallas kernels: 10 us -> 7.59 us  [call(): pl.pallas_call(kernel, out_shape=out_shape, in_specs=specs, out_specs=jax...]
    ppermute x9, waiting for transfers between devices: 9.14 us -> 7.48 us  [hop(): return lax.ppermute(value, 'blk', [(i, i ^ blk) for i in range(n_blk)])]
    ppermute x9, starting transfers between devices: 7.44 us -> 8.79 us  [hop(): return lax.ppermute(value, 'blk', [(i, i ^ blk) for i in range(n_blk)])]
    ppermute x1, starting transfers between devices: 2.88 us -> 1.59 us  [hop(): return lax.ppermute(value, ('blk', 'rows'), pairs)]
    concatenate x1, other arithmetic: 0.07 us -> 0.75 us  [shards(): jnp.concatenate([centres, jnp.broadcast_to(log_prior[:, None], (1, width)...]
    unnamed x8 -> x6, local copies, waits for them, and re-layouts: 2.56 us -> 1.96 us
    ppermute x4, waiting for transfers between devices: 6.3 us -> 6.88 us  [hop(): return lax.ppermute(value, 'rows', [(i, i ^ rows) for i in range(n_rows)])]
  transfers between devices with their start and end apart: 14 -> 14, of which waited for: 10 -> 11; matrix products, arithmetic and copies ran while one was open for 1% -> 2% of each run, Pallas kernels for 5% -> 8%
where the time goes in v3:
time: 43.3 us; the launch traced here: 43.1 us
  waiting for transfers between devices  16 us (37%)
  starting transfers between devices  15.1 us (35%)
  Pallas kernels  7.59 us (18%)
  local copies, waits for them, and re-layouts  2.12 us (5%)
  between operations  1.41 us (3%)
  other arithmetic  0.93 us (2%)
    ppermute x9, starting transfers between devices, hop(): return lax.ppermute(value, 'blk', [(i, i ^ blk) for i in range(n_blk)])  8.79 us
    pallas_call x8, Pallas kernels, call(): pl.pallas_call(kernel, out_shape=out_shape, in_specs=specs, out_specs=jax...  7.59 us
    ppermute x9, waiting for transfers between devices, hop(): return lax.ppermute(value, 'blk', [(i, i ^ blk) for i in range(n_blk)])  7.48 us
    ppermute x4, waiting for transfers between devices, hop(): return lax.ppermute(value, 'rows', [(i, i ^ rows) for i in range(n_rows)])  6.88 us
    ppermute x4, starting transfers between devices, hop(): return lax.ppermute(value, 'rows', [(i, i ^ rows) for i in range(n_rows)])  4.7 us
    unnamed x6, local copies, waits for them, and re-layouts  1.96 us
    ppermute x1, waiting for transfers between devices, hop(): return lax.ppermute(value, ('blk', 'rows'), pairs)  1.6 us
    ppermute x1, starting transfers between devices, hop(): return lax.ppermute(value, ('blk', 'rows'), pairs)  1.59 us
  transfers between devices with their start and end apart: 14, of which 11 were waited for; matrix products, arithmetic and copies ran while one was open for 2% of the time, Pallas kernels for 8%

profile of v3, /device:TPU:0, one launch (start us, length us, event | category | flops | bytes accessed | tf_op | source)
XLA Modules:
  0.0 43.1 jit_solution(10140630266036692087)
XLA Ops:
  0.6 0.5 %collective-permute-start.3 = (bf16[512,384]{1,0:T(8,128)(2,1)}, bf16[512,384]{1,0:T(8,128)(2,1)S(1)}, u32[]{:S(2)}, u32[]{:S(2)}) collective-permute-start(bf16[512,384]{1,0:T(8,128)(2,1)} %refs_0_.3), channel_id=1, source_target_pairs={{0,4},{4,0},{8,12},{12,8},{16,20},{20,16},{24,28},{28,24},{1,5},{5... | collective-permute-start | bytes 1179656 | tf_op jit(solution)/shard_map/ppermute | solution.py:349
  1.1 2.6 %collective-permute-start = (bf16[512,384]{1,0:T(8,128)(2,1)}, bf16[512,384]{1,0:T(8,128)(2,1)S(1)}, u32[]{:S(2)}, u32[]{:S(2)}) collective-permute-start(bf16[512,384]{1,0:T(8,128)(2,1)} %refs_0_.3), channel_id=1, source_target_pairs={{0,8},{4,12},{8,0},{12,4},{16,24},{20,28},{24,16},{28,20},{1,9},{5... | collective-permute-start | bytes 1179656 | tf_op jit(solution)/shard_map/ppermute | solution.py:349
  3.7 1.5 %collective-permute-start.1 = (bf16[384,384]{1,0:T(8,128)(2,1)}, bf16[384,384]{1,0:T(8,128)(2,1)S(1)}, u32[]{:S(2)}, u32[]{:S(2)}) collective-permute-start(bf16[384,384]{1,0:T(8,128)(2,1)} %bitcast.4), channel_id=1, source_target_pairs={{0,16},{4,20},{8,24},{12,28},{16,0},{20,4},{24,8},{28,12},{1,17},{... | collective-permute-start | bytes 884744 | tf_op jit(solution)/shard_map/ppermute | solution.py:349
  5.9 0.1 pad.1.clone
  6.0 0.1 pad.2.clone
  6.1 0.8 %maximum_maximum_fusion.tail_ref.refs_5_.refs_4_ = bf16[16,384]{1,0:T(8,128)(2,1)S(1)} fusion(bf16[1,384]{1,0:T(2,128)(2,1)} %param.6, bf16[16]{0:T(256)(128)(2,1)S(1)} %pad.2.clone, bf16[16]{0:T(256)(128)(2,1)S(1)} %pad.1.clone), kind=kLoop, calls=%fused_computation | loop fusion | flops 36864 | bytes 13120 | tf_op jit(solution)/shard_map/concatenate | solution.py:366
  6.8 0.5 %collective-permute-start.2 = (bf16[16,384]{1,0:T(8,128)(2,1)S(1)}, bf16[16,384]{1,0:T(8,128)(2,1)S(1)}, u32[]{:S(2)}, u32[]{:S(2)}) collective-permute-start(bf16[16,384]{1,0:T(8,128)(2,1)S(1)} %maximum_maximum_fusion.tail_ref.refs_5_.refs_4_), channel_id=1, source_target_pairs={{0,16},{4,20},{8,24},{12,28},{16,0},{20,4},{24,8},{28,12},{1,17},{... | collective-permute-start | bytes 36872 | tf_op jit(solution)/shard_map/ppermute | solution.py:349
  7.3 0.0 collective-permute-done.3.core_ref.refs_2_
  7.3 0.0 copy-start
  7.3 1.0 %copy-done = bf16[512,384]{1,0:T(8,128)(2,1)S(1)} copy-done((bf16[512,384]{1,0:T(8,128)(2,1)S(1)}, bf16[512,384]{1,0:T(8,128)(2,1)}, u32[]{:S(2)}) %copy-start) | copy-done | bytes 393240
  8.3 0.0 copy-start.2
  8.3 1.0 %copy-done.2 = bf16[1,384,384]{2,1,0:T(8,128)(2,1)S(1)} copy-done((bf16[1,384,384]{2,1,0:T(8,128)(2,1)S(1)}, bf16[1,384,384]{2,1,0:T(8,128)(2,1)}, u32[]{:S(2)}) %copy-start.2) | copy-done | bytes 294936
  9.3 0.0 copy-start.1
  9.3 0.7 %shard_map.75 = (f32[1,1024]{1,0:T(1,128)S(1)}, bf16[384,384]{1,0:T(8,128)(2,1)S(1)}) custom-call(bf16[512,384]{1,0:T(8,128)(2,1)S(1)} %copy-done, bf16[512,384]{1,0:T(8,128)(2,1)S(1)} %collective-permute-done.3.core_ref.refs_2_, bf16[384,384]{1,0:T(8,128)(2,1)S(1)} %bitcast.5, bf16[16,384]{1,0:T(8,128)(2,1)S(1)} %maximum_maximum_fusion.tail_ref.refs_5_.refs_4_), custom_call_target="tpu_custom_call" | custom-call | flops 301989888 | bytes 1392640 | tf_op jit(solution)/shard_map/pallas_call | solution.py:332
  10.0 3.3 %collective-permute-done.2.refs_6_.refs_5_ = bf16[16,384]{1,0:T(8,128)(2,1)S(1)} collective-permute-done((bf16[16,384]{1,0:T(8,128)(2,1)S(1)}, bf16[16,384]{1,0:T(8,128)(2,1)S(1)}, u32[]{:S(2)}, u32[]{:S(2)}) %collective-permute-start.2) | collective-permute-done | bytes 12320 | tf_op jit(solution)/shard_map/ppermute | solution.py:349
  13.3 0.0 collective-permute-done.1.refs_7_
  13.3 0.4 collective-permute-done.refs_1_
  13.6 0.0 collective-permute-start.4
  13.6 1.1 %shard_map.76 = (f32[2,1536]{1,0:T(2,128)S(1)}, bf16[1,384,384]{2,1,0:T(8,128)(2,1)S(1)}) custom-call(bf16[512,384]{1,0:T(8,128)(2,1)S(1)} %copy-done, bf16[512,384]{1,0:T(8,128)(2,1)S(1)} %collective-permute-done.refs_1_, bf16[512,384]{1,0:T(8,128)(2,1)S(1)} %collective-permute-done.3.core_ref.refs_2_, f32[1,1024]{1,0:T(1,128)S(1)} %get-tuple-element.30.refs_3_, ...), custom_call_target="tpu_custom_call" | custom-call | flops 603979776 | bytes 2105344 | tf_op jit(solution)/shard_map/pallas_call | solution.py:332
  14.7 0.6 %collective-permute-done.4.refs_0_.refs_3_ = bf16[512,384]{1,0:T(8,128)(2,1)S(1)} collective-permute-done((bf16[512,384]{1,0:T(8,128)(2,1)S(1)}, bf16[512,384]{1,0:T(8,128)(2,1)S(1)}, u32[]{:S(2)}, u32[]{:S(2)}) %collective-permute-start.4) | collective-permute-done | bytes 393248 | tf_op jit(solution)/shard_map/ppermute | solution.py:349
  15.4 0.6 %shard_map.77.refs_0_ = f32[2,2048]{1,0:T(2,128)S(1)} custom-call(bf16[512,384]{1,0:T(8,128)(2,1)S(1)} %collective-permute-done.4.refs_0_.refs_3_, f32[2,1536]{1,0:T(2,128)S(1)} %get-tuple-element.34.refs_1_, bf16[384,384]{1,0:T(8,128)(2,1)S(1)} %get-tuple-element.31.refs_4_.refs_2_, bf16[1,384,384]{2,1,0:T(8,128)(2,1)S(1)} %get-tuple-element.35.refs_3_, ...), custom_call_target="tpu_custom_call" | custom-call | flops 301989888 | bytes 1036288 | tf_op jit(solution)/shard_map/pallas_call | solution.py:332
  16.0 1.8 %collective-permute-start.6 = (f32[2,2048]{1,0:T(2,128)S(1)}, f32[2,2048]{1,0:T(2,128)S(1)}, u32[]{:S(2)}, u32[]{:S(2)}) collective-permute-start(f32[2,2048]{1,0:T(2,128)S(1)} %shard_map.77.refs_0_), channel_id=1, source_target_pairs={{0,8},{4,12},{8,0},{12,4},{16,24},{20,28},{24,16},{28,20},{1,9},{5... | collective-permute-start | bytes 49160 | tf_op jit(solution)/shard_map/ppermute | solution.py:349
  17.8 0.0 collective-permute-start.5
  17.8 2.0 %collective-permute-done.6.refs_2_ = f32[2,2048]{1,0:T(2,128)S(1)} collective-permute-done((f32[2,2048]{1,0:T(2,128)S(1)}, f32[2,2048]{1,0:T(2,128)S(1)}, u32[]{:S(2)}, u32[]{:S(2)}) %collective-permute-start.6) | collective-permute-done | bytes 16416 | tf_op jit(solution)/shard_map/ppermute | solution.py:349
  19.8 0.0 collective-permute-start.7
  19.8 0.0 copy-done.1
  19.8 0.6 %shard_map.78 = (bf16[2048,512]{1,0:T(8,128)(2,1)S(1)}, f32[384,2048]{1,0:T(8,128)S(1)}) custom-call(bf16[512,384]{1,0:T(8,128)(2,1)S(1)} %copy-done.1, bf16[512,384]{1,0:T(8,128)(2,1)S(1)} %collective-permute-done.refs_1_, bf16[512,384]{1,0:T(8,128)(2,1)S(1)} %collective-permute-done.3.core_ref.refs_2_, ...), custom_call_target="tpu_custom_call" | custom-call | bytes 6815744 | tf_op jit(solution)/shard_map/pallas_call | solution.py:332
  20.4 0.0 collective-permute-done.5.refs_1_
  20.4 0.5 %collective-permute-done.7.refs_3_ = f32[2,2048]{1,0:T(2,128)S(1)} collective-permute-done((f32[2,2048]{1,0:T(2,128)S(1)}, f32[2,2048]{1,0:T(2,128)S(1)}, u32[]{:S(2)}, u32[]{:S(2)}) %collective-permute-start.7) | collective-permute-done | bytes 16416 | tf_op jit(solution)/shard_map/ppermute | solution.py:349
  21.0 1.9 %shard_map.79 = (f32[8,2048]{1,0:T(8,128)S(1)}, f32[48,128]{1,0:T(8,128)S(1)}, f32[8,512]{1,0:T(8,128)}, f32[320,128]{1,0:T(8,128)S(1)}, f32[320,128]{1,0:T(8,128)S(1)}) custom-call(f32[2,2048]{1,0:T(2,128)S(1)} %shard_map.77.refs_0_, f32[2,2048]{1,0:T(2,128)S(1)} %collective-permute-done.5.refs_1_, f32[2,2048]{1,0:T(2,128)S(1)} %collective-permute-done.6.refs_2_, ...), custom_call_target="tpu_custom_call" | custom-call | flops 1207959552 | bytes 5742592 | tf_op jit(solution)/shard_map/pallas_call | solution.py:332
  22.9 1.8 %collective-permute-start.8 = (f16[320,128]{1,0:T(8,128)(2,1)S(1)}, f16[320,128]{1,0:T(8,128)(2,1)S(1)}, u32[]{:S(2)}, u32[]{:S(2)}) collective-permute-start(f16[320,128]{1,0:T(8,128)(2,1)S(1)} %convert_element_type.41), channel_id=1, source_target_pairs={{0,16},{4,20},{8,24},{12,28},{16,0},{20,4},{24,8},{28,12},{1,17},{... | collective-permute-start | bytes 245768 | tf_op jit(solution)/shard_map/ppermute | solution.py:349
  24.8 1.6 %collective-permute-start.9 = (f16[320,128]{1,0:T(8,128)(2,1)S(1)}, f16[320,128]{1,0:T(8,128)(2,1)S(1)}, u32[]{:S(2)}, u32[]{:S(2)}) collective-permute-start(f16[320,128]{1,0:T(8,128)(2,1)S(1)} %convert_element_type.42), channel_id=1, source_target_pairs={{0,17},{1,16},{2,19},{3,18},{4,21},{5,20},{6,23},{7,22},{8,25},{9,... | collective-permute-start | bytes 245768 | tf_op jit(solution)/shard_map/ppermute | solution.py:355
  26.4 1.3 %shard_map.80 = (f32[320,128]{1,0:T(8,128)S(1)}, f32[320,128]{1,0:T(8,128)S(1)}) custom-call(f32[8,2048]{1,0:T(8,128)S(1)} %get-tuple-element.41.refs_0_, f32[48,128]{1,0:T(8,128)S(1)} %get-tuple-element.42.refs_1_, bf16[2048,512]{1,0:T(8,128)(2,1)S(1)} %get-tuple-element.38.refs_4_.refs_2_, f32[384,2048]{1,0:T(8,128)S(1)} %get-tuple-element.39.refs_5_.refs_3_), custom_call_target="tpu_custom_call" | custom-call | flops 1207959552 | bytes 5660672 | tf_op jit(solution)/shard_map/pallas_call | solution.py:332
  27.7 0.3 collective-permute-start.10
  28.0 0.6 %collective-permute-done.8 = f16[320,128]{1,0:T(8,128)(2,1)S(1)} collective-permute-done((f16[320,128]{1,0:T(8,128)(2,1)S(1)}, f16[320,128]{1,0:T(8,128)(2,1)S(1)}, u32[]{:S(2)}, u32[]{:S(2)}) %collective-permute-start.8) | collective-permute-done | bytes 81952 | tf_op jit(solution)/shard_map/ppermute | solution.py:349
  28.6 1.6 %collective-permute-done.9 = f16[320,128]{1,0:T(8,128)(2,1)S(1)} collective-permute-done((f16[320,128]{1,0:T(8,128)(2,1)S(1)}, f16[320,128]{1,0:T(8,128)(2,1)S(1)}, u32[]{:S(2)}, u32[]{:S(2)}) %collective-permute-start.9) | collective-permute-done | bytes 81952 | tf_op jit(solution)/shard_map/ppermute | solution.py:355
  30.2 1.9 %collective-permute-done.10 = f16[320,128]{1,0:T(8,128)(2,1)S(1)} collective-permute-done((f16[320,128]{1,0:T(8,128)(2,1)S(1)}, f16[320,128]{1,0:T(8,128)(2,1)S(1)}, u32[]{:S(2)}, u32[]{:S(2)}) %collective-permute-start.10) | collective-permute-done | bytes 81952 | tf_op jit(solution)/shard_map/ppermute | solution.py:351
  32.2 0.2 shard_map.81
  32.4 2.7 %collective-permute-start.11 = (f16[320,128]{1,0:T(8,128)(2,1)S(1)}, f16[320,128]{1,0:T(8,128)(2,1)S(1)}, u32[]{:S(2)}, u32[]{:S(2)}) collective-permute-start(f16[320,128]{1,0:T(8,128)(2,1)S(1)} %convert_element_type.47), channel_id=1, source_target_pairs={{0,2},{1,3},{2,0},{3,1},{4,6},{5,7},{6,4},{7,5},{8,10},{9,11},{10,... | collective-permute-start | bytes 245768 | tf_op jit(solution)/shard_map/ppermute | solution.py:351
  35.1 0.5 %collective-permute-start.12 = (f16[320,128]{1,0:T(8,128)(2,1)S(1)}, f16[320,128]{1,0:T(8,128)(2,1)S(1)}, u32[]{:S(2)}, u32[]{:S(2)}) collective-permute-start(f16[320,128]{1,0:T(8,128)(2,1)S(1)} %convert_element_type.47), channel_id=1, source_target_pairs={{0,1},{1,0},{2,3},{3,2},{4,5},{5,4},{6,7},{7,6},{8,9},{9,8},{10,11... | collective-permute-start | bytes 245768 | tf_op jit(solution)/shard_map/ppermute | solution.py:351
  35.5 1.3 %collective-permute-start.13 = (f16[320,128]{1,0:T(8,128)(2,1)S(1)}, f16[320,128]{1,0:T(8,128)(2,1)S(1)}, u32[]{:S(2)}, u32[]{:S(2)}) collective-permute-start(f16[320,128]{1,0:T(8,128)(2,1)S(1)} %convert_element_type.47), channel_id=1, source_target_pairs={{0,3},{1,2},{2,1},{3,0},{4,7},{5,6},{6,5},{7,4},{8,11},{9,10},{10,... | collective-permute-start | bytes 245768 | tf_op jit(solution)/shard_map/ppermute | solution.py:351
  36.9 3.5 %collective-permute-done.11 = f16[320,128]{1,0:T(8,128)(2,1)S(1)} collective-permute-done((f16[320,128]{1,0:T(8,128)(2,1)S(1)}, f16[320,128]{1,0:T(8,128)(2,1)S(1)}, u32[]{:S(2)}, u32[]{:S(2)}) %collective-permute-start.11) | collective-permute-done | bytes 81952 | tf_op jit(solution)/shard_map/ppermute | solution.py:351
  40.4 0.4 collective-permute-done.12
  40.8 1.1 %collective-permute-done.13 = f16[320,128]{1,0:T(8,128)(2,1)S(1)} collective-permute-done((f16[320,128]{1,0:T(8,128)(2,1)S(1)}, f16[320,128]{1,0:T(8,128)(2,1)S(1)}, u32[]{:S(2)}, u32[]{:S(2)}) %collective-permute-start.13) | collective-permute-done | bytes 81952 | tf_op jit(solution)/shard_map/ppermute | solution.py:351
  41.9 1.2 %shard_map.82 = (f32[384,384]{1,0:T(8,128)}, f32[8,384]{1,0:T(8,128)}, f32[1,8]{1,0:T(1,128)}) custom-call(f32[320,128]{1,0:T(8,128)S(1)} %convert_element_type.48.refs_0_, f32[320,128]{1,0:T(8,128)S(1)} %convert_element_type.49.refs_1_, f32[320,128]{1,0:T(8,128)S(1)} %convert_element_type.50.refs_2_, f32[320,128]{1,0:T(8,128)S(1)} %convert_element_type.51.refs_3_), custom_call_target="tpu_custom_call" | custom-call | bytes 1257504 | tf_op jit(solution)/shard_map/pallas_call | solution.py:332
  (14 shorter events, 0.2 us)
Async XLA Ops:
  0.6 6.7 %collective-permute-start.3 = (bf16[512,384]{1,0:T(8,128)(2,1)}, bf16[512,384]{1,0:T(8,128)(2,1)S(1)}, u32[]{:S(2)}, u32[]{:S(2)}) collective-permute-start(bf16[512,384]{1,0:T(8,128)(2,1)} %refs_0_.3), channel_id=1, source_target_pairs={{0,4},{4,0},{8,12},{12,8},{16,20},{20,16},{24,28},{28,24},{1,5},{5... | collective-permute-start | bytes 1179656 | tf_op jit(solution)/shard_map/ppermute | solution.py:349
  1.1 12.5 %collective-permute-start = (bf16[512,384]{1,0:T(8,128)(2,1)}, bf16[512,384]{1,0:T(8,128)(2,1)S(1)}, u32[]{:S(2)}, u32[]{:S(2)}) collective-permute-start(bf16[512,384]{1,0:T(8,128)(2,1)} %refs_0_.3), channel_id=1, source_target_pairs={{0,8},{4,12},{8,0},{12,4},{16,24},{20,28},{24,16},{28,20},{1,9},{5... | collective-permute-start | bytes 1179656 | tf_op jit(solution)/shard_map/ppermute | solution.py:349
  3.7 9.6 %collective-permute-start.1 = (bf16[384,384]{1,0:T(8,128)(2,1)}, bf16[384,384]{1,0:T(8,128)(2,1)S(1)}, u32[]{:S(2)}, u32[]{:S(2)}) collective-permute-start(bf16[384,384]{1,0:T(8,128)(2,1)} %bitcast.4), channel_id=1, source_target_pairs={{0,16},{4,20},{8,24},{12,28},{16,0},{20,4},{24,8},{28,12},{1,17},{... | collective-permute-start | bytes 884744 | tf_op jit(solution)/shard_map/ppermute | solution.py:349
  6.8 6.5 %collective-permute-start.2 = (bf16[16,384]{1,0:T(8,128)(2,1)S(1)}, bf16[16,384]{1,0:T(8,128)(2,1)S(1)}, u32[]{:S(2)}, u32[]{:S(2)}) collective-permute-start(bf16[16,384]{1,0:T(8,128)(2,1)S(1)} %maximum_maximum_fusion.tail_ref.refs_5_.refs_4_), channel_id=1, source_target_pairs={{0,16},{4,20},{8,24},{12,28},{16,0},{20,4},{24,8},{28,12},{1,17},{... | collective-permute-start | bytes 36872 | tf_op jit(solution)/shard_map/ppermute | solution.py:349
  7.3 1.0 %copy-start = (bf16[512,384]{1,0:T(8,128)(2,1)S(1)}, bf16[512,384]{1,0:T(8,128)(2,1)}, u32[]{:S(2)}) copy-start(bf16[512,384]{1,0:T(8,128)(2,1)} %refs_0_.3) | copy-start | bytes 1179652
  8.3 1.0 %copy-start.2 = (bf16[1,384,384]{2,1,0:T(8,128)(2,1)S(1)}, bf16[1,384,384]{2,1,0:T(8,128)(2,1)}, u32[]{:S(2)}) copy-start(bf16[1,384,384]{2,1,0:T(8,128)(2,1)} %param.5) | copy-start | bytes 884740
  9.3 10.5 %copy-start.1 = (bf16[512,384]{1,0:T(8,128)(2,1)S(1)}, bf16[512,384]{1,0:T(8,128)(2,1)}, u32[]{:S(2)}) copy-start(bf16[512,384]{1,0:T(8,128)(2,1)} %refs_0_.3) | copy-start | bytes 1179652
  13.6 1.7 %collective-permute-start.4 = (bf16[512,384]{1,0:T(8,128)(2,1)S(1)}, bf16[512,384]{1,0:T(8,128)(2,1)S(1)}, u32[]{:S(2)}, u32[]{:S(2)}) collective-permute-start(bf16[512,384]{1,0:T(8,128)(2,1)S(1)} %collective-permute-done.refs_1_), channel_id=1, source_target_pairs={{0,4},{4,0},{8,12},{12,8},{16,20},{20,16},{24,28},{28,24},{1,5},{5... | collective-permute-start | bytes 1179656 | tf_op jit(solution)/shard_map/ppermute | solution.py:349
  16.0 3.8 %collective-permute-start.6 = (f32[2,2048]{1,0:T(2,128)S(1)}, f32[2,2048]{1,0:T(2,128)S(1)}, u32[]{:S(2)}, u32[]{:S(2)}) collective-permute-start(f32[2,2048]{1,0:T(2,128)S(1)} %shard_map.77.refs_0_), channel_id=1, source_target_pairs={{0,8},{4,12},{8,0},{12,4},{16,24},{20,28},{24,16},{28,20},{1,9},{5... | collective-permute-start | bytes 49160 | tf_op jit(solution)/shard_map/ppermute | solution.py:349
  17.8 2.6 %collective-permute-start.5 = (f32[2,2048]{1,0:T(2,128)S(1)}, f32[2,2048]{1,0:T(2,128)S(1)}, u32[]{:S(2)}, u32[]{:S(2)}) collective-permute-start(f32[2,2048]{1,0:T(2,128)S(1)} %shard_map.77.refs_0_), channel_id=1, source_target_pairs={{0,4},{4,0},{8,12},{12,8},{16,20},{20,16},{24,28},{28,24},{1,5},{5... | collective-permute-start | bytes 49160 | tf_op jit(solution)/shard_map/ppermute | solution.py:349
  19.8 1.2 %collective-permute-start.7 = (f32[2,2048]{1,0:T(2,128)S(1)}, f32[2,2048]{1,0:T(2,128)S(1)}, u32[]{:S(2)}, u32[]{:S(2)}) collective-permute-start(f32[2,2048]{1,0:T(2,128)S(1)} %collective-permute-done.6.refs_2_), channel_id=1, source_target_pairs={{0,4},{4,0},{8,12},{12,8},{16,20},{20,16},{24,28},{28,24},{1,5},{5... | collective-permute-start | bytes 49160 | tf_op jit(solution)/shard_map/ppermute | solution.py:349
  22.9 5.7 %collective-permute-start.8 = (f16[320,128]{1,0:T(8,128)(2,1)S(1)}, f16[320,128]{1,0:T(8,128)(2,1)S(1)}, u32[]{:S(2)}, u32[]{:S(2)}) collective-permute-start(f16[320,128]{1,0:T(8,128)(2,1)S(1)} %convert_element_type.41), channel_id=1, source_target_pairs={{0,16},{4,20},{8,24},{12,28},{16,0},{20,4},{24,8},{28,12},{1,17},{... | collective-permute-start | bytes 245768 | tf_op jit(solution)/shard_map/ppermute | solution.py:349
  24.8 5.4 %collective-permute-start.9 = (f16[320,128]{1,0:T(8,128)(2,1)S(1)}, f16[320,128]{1,0:T(8,128)(2,1)S(1)}, u32[]{:S(2)}, u32[]{:S(2)}) collective-permute-start(f16[320,128]{1,0:T(8,128)(2,1)S(1)} %convert_element_type.42), channel_id=1, source_target_pairs={{0,17},{1,16},{2,19},{3,18},{4,21},{5,20},{6,23},{7,22},{8,25},{9,... | collective-permute-start | bytes 245768 | tf_op jit(solution)/shard_map/ppermute | solution.py:355
  27.7 4.5 %collective-permute-start.10 = (f16[320,128]{1,0:T(8,128)(2,1)S(1)}, f16[320,128]{1,0:T(8,128)(2,1)S(1)}, u32[]{:S(2)}, u32[]{:S(2)}) collective-permute-start(f16[320,128]{1,0:T(8,128)(2,1)S(1)} %convert_element_type.44), channel_id=1, source_target_pairs={{0,1},{1,0},{2,3},{3,2},{4,5},{5,4},{6,7},{7,6},{8,9},{9,8},{10,11... | collective-permute-start | bytes 245768 | tf_op jit(solution)/shard_map/ppermute | solution.py:351
  32.4 8.0 %collective-permute-start.11 = (f16[320,128]{1,0:T(8,128)(2,1)S(1)}, f16[320,128]{1,0:T(8,128)(2,1)S(1)}, u32[]{:S(2)}, u32[]{:S(2)}) collective-permute-start(f16[320,128]{1,0:T(8,128)(2,1)S(1)} %convert_element_type.47), channel_id=1, source_target_pairs={{0,2},{1,3},{2,0},{3,1},{4,6},{5,7},{6,4},{7,5},{8,10},{9,11},{10,... | collective-permute-start | bytes 245768 | tf_op jit(solution)/shard_map/ppermute | solution.py:351
  35.1 5.7 %collective-permute-start.12 = (f16[320,128]{1,0:T(8,128)(2,1)S(1)}, f16[320,128]{1,0:T(8,128)(2,1)S(1)}, u32[]{:S(2)}, u32[]{:S(2)}) collective-permute-start(f16[320,128]{1,0:T(8,128)(2,1)S(1)} %convert_element_type.47), channel_id=1, source_target_pairs={{0,1},{1,0},{2,3},{3,2},{4,5},{5,4},{6,7},{7,6},{8,9},{9,8},{10,11... | collective-permute-start | bytes 245768 | tf_op jit(solution)/shard_map/ppermute | solution.py:351
  35.5 6.3 %collective-permute-start.13 = (f16[320,128]{1,0:T(8,128)(2,1)S(1)}, f16[320,128]{1,0:T(8,128)(2,1)S(1)}, u32[]{:S(2)}, u32[]{:S(2)}) collective-permute-start(f16[320,128]{1,0:T(8,128)(2,1)S(1)} %convert_element_type.47), channel_id=1, source_target_pairs={{0,3},{1,2},{2,1},{3,0},{4,7},{5,6},{6,5},{7,4},{8,11},{9,10},{10,... | collective-permute-start | bytes 245768 | tf_op jit(solution)/shard_map/ppermute | solution.py:351

commit v4 on v3

--- a/solution.py
+++ b/solution.py
@@ -199,20 +199,22 @@
 
 def give_kernel(offsets, normalizer, layout, *refs):
     scores, (rows_ref, columns_ref), refs = refs[:4], refs[4:6], refs[6:]
-    resp_ref, low_ref, here_ref, *outs, table_ref, message_ref = refs
+    resp_ref, low_ref, here_ref, *outs, message_ref = refs
     comps, rows = here_ref.shape
     me, flip = place_here()
     own = own_place(me)
+    index = lax.broadcasted_iota(jnp.int32, (comps, 4 * rows), 0)
+    table = jnp.zeros((comps, 4 * rows), jnp.float32)
     for source, score_ref in enumerate(scores):
+        turn = ((source & 1) << 1) | (source >> 1)
         for b in range(score_ref.shape[0]):
-            for part in range(4):
-                to = part ^ (((source & 1) << 1) | (source >> 1)) ^ own
-                table_ref[pl.ds(me ^ (4 * b + source), 1), span(to, rows)] = score_ref[
-                    b : b + 1, part * rows : (part + 1) * rows
-                ]
-    weights = softmax(table_ref[...])
-    resp_ref[...] = weights
-    here_ref[...] = resp_ref[:, span(own, rows)]
+            pieces = [score_ref[b : b + 1, (part ^ turn) * rows : ((part ^ turn) + 1) * rows] for part in range(4)]
+            table = jnp.where(index == (me ^ (4 * b + source)), jnp.concatenate(pieces, axis=1), table)
+    weights = softmax(table)
+    here_ref[...] = weights[:, :rows]
+    for part in range(4):
+        resp_ref[:, span(part ^ own, rows)] = weights[:, part * rows : (part + 1) * rows]
+    weights = resp_ref[...]
     high = weights.astype(jnp.bfloat16).astype(jnp.float32)
     rest = weights - high
     middle = rest.astype(jnp.bfloat16).astype(jnp.float32)
@@ -423,7 +425,7 @@
             ),
             (scores, core_scores, near_scores, far_scores, *both),
             flops * (groups - 1),
-            [pltpu.VMEM((comps, 4 * rows), jnp.float32), whole],
+            [whole],
         )
         received = {}
         for b in range(1, groups):

time: 43.3 us -> 42.8 us (0.988)
  Pallas kernels: 7.59 us -> 7.06 us
    pallas_call x8, Pallas kernels: 7.59 us -> 7.06 us  [call(): pl.pallas_call(kernel, out_shape=out_shape, in_specs=specs, out_specs=jax...]
  transfers between devices with their start and end apart: 14 -> 14, of which waited for: 11 -> 11; matrix products, arithmetic and copies ran while one was open for 2% -> 2% of each run, Pallas kernels for 8% -> 9%
where the time goes in v4:
time: 42.8 us; the launch traced here: 42.6 us
  waiting for transfers between devices  16 us (37%)
  starting transfers between devices  15.1 us (35%)
  Pallas kernels  7.06 us (16%)
  local copies, waits for them, and re-layouts  2.12 us (5%)
  between operations  1.42 us (3%)
  other arithmetic  0.93 us (2%)
    ppermute x9, starting transfers between devices, hop(): return lax.ppermute(value, 'blk', [(i, i ^ blk) for i in range(n_blk)])  8.79 us
    ppermute x9, waiting for transfers between devices, hop(): return lax.ppermute(value, 'blk', [(i, i ^ blk) for i in range(n_blk)])  7.49 us
    pallas_call x8, Pallas kernels, call(): pl.pallas_call(kernel, out_shape=out_shape, in_specs=specs, out_specs=jax...  7.06 us
    ppermute x4, waiting for transfers between devices, hop(): return lax.ppermute(value, 'rows', [(i, i ^ rows) for i in range(n_rows)])  6.89 us
    ppermute x4, starting transfers between devices, hop(): return lax.ppermute(value, 'rows', [(i, i ^ rows) for i in range(n_rows)])  4.7 us
    unnamed x6, local copies, waits for them, and re-layouts  1.96 us
    ppermute x1, waiting for transfers between devices, hop(): return lax.ppermute(value, ('blk', 'rows'), pairs)  1.6 us
    ppermute x1, starting transfers between devices, hop(): return lax.ppermute(value, ('blk', 'rows'), pairs)  1.59 us
  transfers between devices with their start and end apart: 14, of which 11 were waited for; matrix products, arithmetic and copies ran while one was open for 2% of the time, Pallas kernels for 9%

profile of v4, /device:TPU:0, one launch (start us, length us, event | category | flops | bytes accessed | tf_op | source)
XLA Modules:
  0.0 42.6 jit_solution(15810439116754985502)
XLA Ops:
  0.6 0.5 %collective-permute-start.3 = (bf16[512,384]{1,0:T(8,128)(2,1)}, bf16[512,384]{1,0:T(8,128)(2,1)S(1)}, u32[]{:S(2)}, u32[]{:S(2)}) collective-permute-start(bf16[512,384]{1,0:T(8,128)(2,1)} %refs_0_.3), channel_id=1, source_target_pairs={{0,4},{4,0},{8,12},{12,8},{16,20},{20,16},{24,28},{28,24},{1,5},{5... | collective-permute-start | bytes 1179656 | tf_op jit(solution)/shard_map/ppermute | solution.py:351
  1.1 2.6 %collective-permute-start = (bf16[512,384]{1,0:T(8,128)(2,1)}, bf16[512,384]{1,0:T(8,128)(2,1)S(1)}, u32[]{:S(2)}, u32[]{:S(2)}) collective-permute-start(bf16[512,384]{1,0:T(8,128)(2,1)} %refs_0_.3), channel_id=1, source_target_pairs={{0,8},{4,12},{8,0},{12,4},{16,24},{20,28},{24,16},{28,20},{1,9},{5... | collective-permute-start | bytes 1179656 | tf_op jit(solution)/shard_map/ppermute | solution.py:351
  3.7 1.5 %collective-permute-start.1 = (bf16[384,384]{1,0:T(8,128)(2,1)}, bf16[384,384]{1,0:T(8,128)(2,1)S(1)}, u32[]{:S(2)}, u32[]{:S(2)}) collective-permute-start(bf16[384,384]{1,0:T(8,128)(2,1)} %bitcast.4), channel_id=1, source_target_pairs={{0,16},{4,20},{8,24},{12,28},{16,0},{20,4},{24,8},{28,12},{1,17},{... | collective-permute-start | bytes 884744 | tf_op jit(solution)/shard_map/ppermute | solution.py:351
  5.9 0.1 pad.1.clone
  6.0 0.1 pad.2.clone
  6.1 0.8 %maximum_maximum_fusion.tail_ref.refs_5_.refs_4_ = bf16[16,384]{1,0:T(8,128)(2,1)S(1)} fusion(bf16[1,384]{1,0:T(2,128)(2,1)} %param.6, bf16[16]{0:T(256)(128)(2,1)S(1)} %pad.2.clone, bf16[16]{0:T(256)(128)(2,1)S(1)} %pad.1.clone), kind=kLoop, calls=%fused_computation | loop fusion | flops 36864 | bytes 13120 | tf_op jit(solution)/shard_map/concatenate | solution.py:368
  6.8 0.5 %collective-permute-start.2 = (bf16[16,384]{1,0:T(8,128)(2,1)S(1)}, bf16[16,384]{1,0:T(8,128)(2,1)S(1)}, u32[]{:S(2)}, u32[]{:S(2)}) collective-permute-start(bf16[16,384]{1,0:T(8,128)(2,1)S(1)} %maximum_maximum_fusion.tail_ref.refs_5_.refs_4_), channel_id=1, source_target_pairs={{0,16},{4,20},{8,24},{12,28},{16,0},{20,4},{24,8},{28,12},{1,17},{... | collective-permute-start | bytes 36872 | tf_op jit(solution)/shard_map/ppermute | solution.py:351
  7.3 0.0 collective-permute-done.3.core_ref.refs_2_
  7.3 0.0 copy-start
  7.3 1.0 %copy-done = bf16[512,384]{1,0:T(8,128)(2,1)S(1)} copy-done((bf16[512,384]{1,0:T(8,128)(2,1)S(1)}, bf16[512,384]{1,0:T(8,128)(2,1)}, u32[]{:S(2)}) %copy-start) | copy-done | bytes 393240
  8.3 0.0 copy-start.2
  8.3 1.0 %copy-done.2 = bf16[1,384,384]{2,1,0:T(8,128)(2,1)S(1)} copy-done((bf16[1,384,384]{2,1,0:T(8,128)(2,1)S(1)}, bf16[1,384,384]{2,1,0:T(8,128)(2,1)}, u32[]{:S(2)}) %copy-start.2) | copy-done | bytes 294936
  9.3 0.0 copy-start.1
  9.3 0.7 %shard_map.75 = (f32[1,1024]{1,0:T(1,128)S(1)}, bf16[384,384]{1,0:T(8,128)(2,1)S(1)}) custom-call(bf16[512,384]{1,0:T(8,128)(2,1)S(1)} %copy-done, bf16[512,384]{1,0:T(8,128)(2,1)S(1)} %collective-permute-done.3.core_ref.refs_2_, bf16[384,384]{1,0:T(8,128)(2,1)S(1)} %bitcast.5, bf16[16,384]{1,0:T(8,128)(2,1)S(1)} %maximum_maximum_fusion.tail_ref.refs_5_.refs_4_), custom_call_target="tpu_custom_call" | custom-call | flops 301989888 | bytes 1392640 | tf_op jit(solution)/shard_map/pallas_call | solution.py:334
  10.0 3.3 %collective-permute-done.2.refs_6_.refs_5_ = bf16[16,384]{1,0:T(8,128)(2,1)S(1)} collective-permute-done((bf16[16,384]{1,0:T(8,128)(2,1)S(1)}, bf16[16,384]{1,0:T(8,128)(2,1)S(1)}, u32[]{:S(2)}, u32[]{:S(2)}) %collective-permute-start.2) | collective-permute-done | bytes 12320 | tf_op jit(solution)/shard_map/ppermute | solution.py:351
  13.3 0.0 collective-permute-done.1.refs_7_
  13.3 0.4 collective-permute-done.refs_1_
  13.6 0.0 collective-permute-start.4
  13.6 1.1 %shard_map.76 = (f32[2,1536]{1,0:T(2,128)S(1)}, bf16[1,384,384]{2,1,0:T(8,128)(2,1)S(1)}) custom-call(bf16[512,384]{1,0:T(8,128)(2,1)S(1)} %copy-done, bf16[512,384]{1,0:T(8,128)(2,1)S(1)} %collective-permute-done.refs_1_, bf16[512,384]{1,0:T(8,128)(2,1)S(1)} %collective-permute-done.3.core_ref.refs_2_, f32[1,1024]{1,0:T(1,128)S(1)} %get-tuple-element.30.refs_3_, ...), custom_call_target="tpu_custom_call" | custom-call | flops 603979776 | bytes 2105344 | tf_op jit(solution)/shard_map/pallas_call | solution.py:334
  14.7 0.6 %collective-permute-done.4.refs_0_.refs_3_ = bf16[512,384]{1,0:T(8,128)(2,1)S(1)} collective-permute-done((bf16[512,384]{1,0:T(8,128)(2,1)S(1)}, bf16[512,384]{1,0:T(8,128)(2,1)S(1)}, u32[]{:S(2)}, u32[]{:S(2)}) %collective-permute-start.4) | collective-permute-done | bytes 393248 | tf_op jit(solution)/shard_map/ppermute | solution.py:351
  15.4 0.6 %shard_map.77.refs_0_ = f32[2,2048]{1,0:T(2,128)S(1)} custom-call(bf16[512,384]{1,0:T(8,128)(2,1)S(1)} %collective-permute-done.4.refs_0_.refs_3_, f32[2,1536]{1,0:T(2,128)S(1)} %get-tuple-element.34.refs_1_, bf16[384,384]{1,0:T(8,128)(2,1)S(1)} %get-tuple-element.31.refs_4_.refs_2_, bf16[1,384,384]{2,1,0:T(8,128)(2,1)S(1)} %get-tuple-element.35.refs_3_, ...), custom_call_target="tpu_custom_call" | custom-call | flops 301989888 | bytes 1036288 | tf_op jit(solution)/shard_map/pallas_call | solution.py:334
  16.0 1.8 %collective-permute-start.6 = (f32[2,2048]{1,0:T(2,128)S(1)}, f32[2,2048]{1,0:T(2,128)S(1)}, u32[]{:S(2)}, u32[]{:S(2)}) collective-permute-start(f32[2,2048]{1,0:T(2,128)S(1)} %shard_map.77.refs_0_), channel_id=1, source_target_pairs={{0,8},{4,12},{8,0},{12,4},{16,24},{20,28},{24,16},{28,20},{1,9},{5... | collective-permute-start | bytes 49160 | tf_op jit(solution)/shard_map/ppermute | solution.py:351
  17.8 0.0 collective-permute-start.5
  17.8 2.0 %collective-permute-done.6.refs_2_ = f32[2,2048]{1,0:T(2,128)S(1)} collective-permute-done((f32[2,2048]{1,0:T(2,128)S(1)}, f32[2,2048]{1,0:T(2,128)S(1)}, u32[]{:S(2)}, u32[]{:S(2)}) %collective-permute-start.6) | collective-permute-done | bytes 16416 | tf_op jit(solution)/shard_map/ppermute | solution.py:351
  19.8 0.0 collective-permute-start.7
  19.8 0.0 copy-done.1
  19.8 0.6 %shard_map.78 = (bf16[2048,512]{1,0:T(8,128)(2,1)S(1)}, f32[384,2048]{1,0:T(8,128)S(1)}) custom-call(bf16[512,384]{1,0:T(8,128)(2,1)S(1)} %copy-done.1, bf16[512,384]{1,0:T(8,128)(2,1)S(1)} %collective-permute-done.refs_1_, bf16[512,384]{1,0:T(8,128)(2,1)S(1)} %collective-permute-done.3.core_ref.refs_2_, ...), custom_call_target="tpu_custom_call" | custom-call | bytes 6815744 | tf_op jit(solution)/shard_map/pallas_call | solution.py:334
  20.4 0.0 collective-permute-done.5.refs_1_
  20.4 0.5 %collective-permute-done.7.refs_3_ = f32[2,2048]{1,0:T(2,128)S(1)} collective-permute-done((f32[2,2048]{1,0:T(2,128)S(1)}, f32[2,2048]{1,0:T(2,128)S(1)}, u32[]{:S(2)}, u32[]{:S(2)}) %collective-permute-start.7) | collective-permute-done | bytes 16416 | tf_op jit(solution)/shard_map/ppermute | solution.py:351
  21.0 1.4 %shard_map.79 = (f32[8,2048]{1,0:T(8,128)S(1)}, f32[48,128]{1,0:T(8,128)S(1)}, f32[8,512]{1,0:T(8,128)}, f32[320,128]{1,0:T(8,128)S(1)}, f32[320,128]{1,0:T(8,128)S(1)}) custom-call(f32[2,2048]{1,0:T(2,128)S(1)} %shard_map.77.refs_0_, f32[2,2048]{1,0:T(2,128)S(1)} %collective-permute-done.5.refs_1_, f32[2,2048]{1,0:T(2,128)S(1)} %collective-permute-done.6.refs_2_, ...), custom_call_target="tpu_custom_call" | custom-call | flops 1207959552 | bytes 5742592 | tf_op jit(solution)/shard_map/pallas_call | solution.py:334
  22.4 1.8 %collective-permute-start.8 = (f16[320,128]{1,0:T(8,128)(2,1)S(1)}, f16[320,128]{1,0:T(8,128)(2,1)S(1)}, u32[]{:S(2)}, u32[]{:S(2)}) collective-permute-start(f16[320,128]{1,0:T(8,128)(2,1)S(1)} %convert_element_type.41), channel_id=1, source_target_pairs={{0,16},{4,20},{8,24},{12,28},{16,0},{20,4},{24,8},{28,12},{1,17},{... | collective-permute-start | bytes 245768 | tf_op jit(solution)/shard_map/ppermute | solution.py:351
  24.3 1.6 %collective-permute-start.9 = (f16[320,128]{1,0:T(8,128)(2,1)S(1)}, f16[320,128]{1,0:T(8,128)(2,1)S(1)}, u32[]{:S(2)}, u32[]{:S(2)}) collective-permute-start(f16[320,128]{1,0:T(8,128)(2,1)S(1)} %convert_element_type.42), channel_id=1, source_target_pairs={{0,17},{1,16},{2,19},{3,18},{4,21},{5,20},{6,23},{7,22},{8,25},{9,... | collective-permute-start | bytes 245768 | tf_op jit(solution)/shard_map/ppermute | solution.py:357
  25.9 1.3 %shard_map.80 = (f32[320,128]{1,0:T(8,128)S(1)}, f32[320,128]{1,0:T(8,128)S(1)}) custom-call(f32[8,2048]{1,0:T(8,128)S(1)} %get-tuple-element.41.refs_0_, f32[48,128]{1,0:T(8,128)S(1)} %get-tuple-element.42.refs_1_, bf16[2048,512]{1,0:T(8,128)(2,1)S(1)} %get-tuple-element.38.refs_4_.refs_2_, f32[384,2048]{1,0:T(8,128)S(1)} %get-tuple-element.39.refs_5_.refs_3_), custom_call_target="tpu_custom_call" | custom-call | flops 1207959552 | bytes 5660672 | tf_op jit(solution)/shard_map/pallas_call | solution.py:334
  27.2 0.2 collective-permute-start.10
  27.4 0.6 %collective-permute-done.8 = f16[320,128]{1,0:T(8,128)(2,1)S(1)} collective-permute-done((f16[320,128]{1,0:T(8,128)(2,1)S(1)}, f16[320,128]{1,0:T(8,128)(2,1)S(1)}, u32[]{:S(2)}, u32[]{:S(2)}) %collective-permute-start.8) | collective-permute-done | bytes 81952 | tf_op jit(solution)/shard_map/ppermute | solution.py:351
  28.1 1.6 %collective-permute-done.9 = f16[320,128]{1,0:T(8,128)(2,1)S(1)} collective-permute-done((f16[320,128]{1,0:T(8,128)(2,1)S(1)}, f16[320,128]{1,0:T(8,128)(2,1)S(1)}, u32[]{:S(2)}, u32[]{:S(2)}) %collective-permute-start.9) | collective-permute-done | bytes 81952 | tf_op jit(solution)/shard_map/ppermute | solution.py:357
  29.7 1.9 %collective-permute-done.10 = f16[320,128]{1,0:T(8,128)(2,1)S(1)} collective-permute-done((f16[320,128]{1,0:T(8,128)(2,1)S(1)}, f16[320,128]{1,0:T(8,128)(2,1)S(1)}, u32[]{:S(2)}, u32[]{:S(2)}) %collective-permute-start.10) | collective-permute-done | bytes 81952 | tf_op jit(solution)/shard_map/ppermute | solution.py:353
  31.7 0.2 shard_map.81
  31.9 2.7 %collective-permute-start.11 = (f16[320,128]{1,0:T(8,128)(2,1)S(1)}, f16[320,128]{1,0:T(8,128)(2,1)S(1)}, u32[]{:S(2)}, u32[]{:S(2)}) collective-permute-start(f16[320,128]{1,0:T(8,128)(2,1)S(1)} %convert_element_type.47), channel_id=1, source_target_pairs={{0,2},{1,3},{2,0},{3,1},{4,6},{5,7},{6,4},{7,5},{8,10},{9,11},{10,... | collective-permute-start | bytes 245768 | tf_op jit(solution)/shard_map/ppermute | solution.py:353
  34.5 0.4 %collective-permute-start.12 = (f16[320,128]{1,0:T(8,128)(2,1)S(1)}, f16[320,128]{1,0:T(8,128)(2,1)S(1)}, u32[]{:S(2)}, u32[]{:S(2)}) collective-permute-start(f16[320,128]{1,0:T(8,128)(2,1)S(1)} %convert_element_type.47), channel_id=1, source_target_pairs={{0,1},{1,0},{2,3},{3,2},{4,5},{5,4},{6,7},{7,6},{8,9},{9,8},{10,11... | collective-permute-start | bytes 245768 | tf_op jit(solution)/shard_map/ppermute | solution.py:353
  35.0 1.3 %collective-permute-start.13 = (f16[320,128]{1,0:T(8,128)(2,1)S(1)}, f16[320,128]{1,0:T(8,128)(2,1)S(1)}, u32[]{:S(2)}, u32[]{:S(2)}) collective-permute-start(f16[320,128]{1,0:T(8,128)(2,1)S(1)} %convert_element_type.47), channel_id=1, source_target_pairs={{0,3},{1,2},{2,1},{3,0},{4,7},{5,6},{6,5},{7,4},{8,11},{9,10},{10,... | collective-permute-start | bytes 245768 | tf_op jit(solution)/shard_map/ppermute | solution.py:353
  36.4 3.5 %collective-permute-done.11 = f16[320,128]{1,0:T(8,128)(2,1)S(1)} collective-permute-done((f16[320,128]{1,0:T(8,128)(2,1)S(1)}, f16[320,128]{1,0:T(8,128)(2,1)S(1)}, u32[]{:S(2)}, u32[]{:S(2)}) %collective-permute-start.11) | collective-permute-done | bytes 81952 | tf_op jit(solution)/shard_map/ppermute | solution.py:353
  39.9 0.4 collective-permute-done.12
  40.3 1.1 %collective-permute-done.13 = f16[320,128]{1,0:T(8,128)(2,1)S(1)} collective-permute-done((f16[320,128]{1,0:T(8,128)(2,1)S(1)}, f16[320,128]{1,0:T(8,128)(2,1)S(1)}, u32[]{:S(2)}, u32[]{:S(2)}) %collective-permute-start.13) | collective-permute-done | bytes 81952 | tf_op jit(solution)/shard_map/ppermute | solution.py:353
  41.4 1.2 %shard_map.82 = (f32[384,384]{1,0:T(8,128)}, f32[8,384]{1,0:T(8,128)}, f32[1,8]{1,0:T(1,128)}) custom-call(f32[320,128]{1,0:T(8,128)S(1)} %convert_element_type.48.refs_0_, f32[320,128]{1,0:T(8,128)S(1)} %convert_element_type.49.refs_1_, f32[320,128]{1,0:T(8,128)S(1)} %convert_element_type.50.refs_2_, f32[320,128]{1,0:T(8,128)S(1)} %convert_element_type.51.refs_3_), custom_call_target="tpu_custom_call" | custom-call | bytes 1257504 | tf_op jit(solution)/shard_map/pallas_call | solution.py:334
  (14 shorter events, 0.2 us)
Async XLA Ops:
  0.6 6.7 %collective-permute-start.3 = (bf16[512,384]{1,0:T(8,128)(2,1)}, bf16[512,384]{1,0:T(8,128)(2,1)S(1)}, u32[]{:S(2)}, u32[]{:S(2)}) collective-permute-start(bf16[512,384]{1,0:T(8,128)(2,1)} %refs_0_.3), channel_id=1, source_target_pairs={{0,4},{4,0},{8,12},{12,8},{16,20},{20,16},{24,28},{28,24},{1,5},{5... | collective-permute-start | bytes 1179656 | tf_op jit(solution)/shard_map/ppermute | solution.py:351
  1.1 12.5 %collective-permute-start = (bf16[512,384]{1,0:T(8,128)(2,1)}, bf16[512,384]{1,0:T(8,128)(2,1)S(1)}, u32[]{:S(2)}, u32[]{:S(2)}) collective-permute-start(bf16[512,384]{1,0:T(8,128)(2,1)} %refs_0_.3), channel_id=1, source_target_pairs={{0,8},{4,12},{8,0},{12,4},{16,24},{20,28},{24,16},{28,20},{1,9},{5... | collective-permute-start | bytes 1179656 | tf_op jit(solution)/shard_map/ppermute | solution.py:351
  3.7 9.6 %collective-permute-start.1 = (bf16[384,384]{1,0:T(8,128)(2,1)}, bf16[384,384]{1,0:T(8,128)(2,1)S(1)}, u32[]{:S(2)}, u32[]{:S(2)}) collective-permute-start(bf16[384,384]{1,0:T(8,128)(2,1)} %bitcast.4), channel_id=1, source_target_pairs={{0,16},{4,20},{8,24},{12,28},{16,0},{20,4},{24,8},{28,12},{1,17},{... | collective-permute-start | bytes 884744 | tf_op jit(solution)/shard_map/ppermute | solution.py:351
  6.8 6.5 %collective-permute-start.2 = (bf16[16,384]{1,0:T(8,128)(2,1)S(1)}, bf16[16,384]{1,0:T(8,128)(2,1)S(1)}, u32[]{:S(2)}, u32[]{:S(2)}) collective-permute-start(bf16[16,384]{1,0:T(8,128)(2,1)S(1)} %maximum_maximum_fusion.tail_ref.refs_5_.refs_4_), channel_id=1, source_target_pairs={{0,16},{4,20},{8,24},{12,28},{16,0},{20,4},{24,8},{28,12},{1,17},{... | collective-permute-start | bytes 36872 | tf_op jit(solution)/shard_map/ppermute | solution.py:351
  7.3 1.0 %copy-start = (bf16[512,384]{1,0:T(8,128)(2,1)S(1)}, bf16[512,384]{1,0:T(8,128)(2,1)}, u32[]{:S(2)}) copy-start(bf16[512,384]{1,0:T(8,128)(2,1)} %refs_0_.3) | copy-start | bytes 1179652
  8.3 1.0 %copy-start.2 = (bf16[1,384,384]{2,1,0:T(8,128)(2,1)S(1)}, bf16[1,384,384]{2,1,0:T(8,128)(2,1)}, u32[]{:S(2)}) copy-start(bf16[1,384,384]{2,1,0:T(8,128)(2,1)} %param.5) | copy-start | bytes 884740
  9.3 10.5 %copy-start.1 = (bf16[512,384]{1,0:T(8,128)(2,1)S(1)}, bf16[512,384]{1,0:T(8,128)(2,1)}, u32[]{:S(2)}) copy-start(bf16[512,384]{1,0:T(8,128)(2,1)} %refs_0_.3) | copy-start | bytes 1179652
  13.6 1.7 %collective-permute-start.4 = (bf16[512,384]{1,0:T(8,128)(2,1)S(1)}, bf16[512,384]{1,0:T(8,128)(2,1)S(1)}, u32[]{:S(2)}, u32[]{:S(2)}) collective-permute-start(bf16[512,384]{1,0:T(8,128)(2,1)S(1)} %collective-permute-done.refs_1_), channel_id=1, source_target_pairs={{0,4},{4,0},{8,12},{12,8},{16,20},{20,16},{24,28},{28,24},{1,5},{5... | collective-permute-start | bytes 1179656 | tf_op jit(solution)/shard_map/ppermute | solution.py:351
  16.0 3.8 %collective-permute-start.6 = (f32[2,2048]{1,0:T(2,128)S(1)}, f32[2,2048]{1,0:T(2,128)S(1)}, u32[]{:S(2)}, u32[]{:S(2)}) collective-permute-start(f32[2,2048]{1,0:T(2,128)S(1)} %shard_map.77.refs_0_), channel_id=1, source_target_pairs={{0,8},{4,12},{8,0},{12,4},{16,24},{20,28},{24,16},{28,20},{1,9},{5... | collective-permute-start | bytes 49160 | tf_op jit(solution)/shard_map/ppermute | solution.py:351
  17.8 2.6 %collective-permute-start.5 = (f32[2,2048]{1,0:T(2,128)S(1)}, f32[2,2048]{1,0:T(2,128)S(1)}, u32[]{:S(2)}, u32[]{:S(2)}) collective-permute-start(f32[2,2048]{1,0:T(2,128)S(1)} %shard_map.77.refs_0_), channel_id=1, source_target_pairs={{0,4},{4,0},{8,12},{12,8},{16,20},{20,16},{24,28},{28,24},{1,5},{5... | collective-permute-start | bytes 49160 | tf_op jit(solution)/shard_map/ppermute | solution.py:351
  19.8 1.2 %collective-permute-start.7 = (f32[2,2048]{1,0:T(2,128)S(1)}, f32[2,2048]{1,0:T(2,128)S(1)}, u32[]{:S(2)}, u32[]{:S(2)}) collective-permute-start(f32[2,2048]{1,0:T(2,128)S(1)} %collective-permute-done.6.refs_2_), channel_id=1, source_target_pairs={{0,4},{4,0},{8,12},{12,8},{16,20},{20,16},{24,28},{28,24},{1,5},{5... | collective-permute-start | bytes 49160 | tf_op jit(solution)/shard_map/ppermute | solution.py:351
  22.4 5.7 %collective-permute-start.8 = (f16[320,128]{1,0:T(8,128)(2,1)S(1)}, f16[320,128]{1,0:T(8,128)(2,1)S(1)}, u32[]{:S(2)}, u32[]{:S(2)}) collective-permute-start(f16[320,128]{1,0:T(8,128)(2,1)S(1)} %convert_element_type.41), channel_id=1, source_target_pairs={{0,16},{4,20},{8,24},{12,28},{16,0},{20,4},{24,8},{28,12},{1,17},{... | collective-permute-start | bytes 245768 | tf_op jit(solution)/shard_map/ppermute | solution.py:351
  24.3 5.4 %collective-permute-start.9 = (f16[320,128]{1,0:T(8,128)(2,1)S(1)}, f16[320,128]{1,0:T(8,128)(2,1)S(1)}, u32[]{:S(2)}, u32[]{:S(2)}) collective-permute-start(f16[320,128]{1,0:T(8,128)(2,1)S(1)} %convert_element_type.42), channel_id=1, source_target_pairs={{0,17},{1,16},{2,19},{3,18},{4,21},{5,20},{6,23},{7,22},{8,25},{9,... | collective-permute-start | bytes 245768 | tf_op jit(solution)/shard_map/ppermute | solution.py:357
  27.2 4.5 %collective-permute-start.10 = (f16[320,128]{1,0:T(8,128)(2,1)S(1)}, f16[320,128]{1,0:T(8,128)(2,1)S(1)}, u32[]{:S(2)}, u32[]{:S(2)}) collective-permute-start(f16[320,128]{1,0:T(8,128)(2,1)S(1)} %convert_element_type.44), channel_id=1, source_target_pairs={{0,1},{1,0},{2,3},{3,2},{4,5},{5,4},{6,7},{7,6},{8,9},{9,8},{10,11... | collective-permute-start | bytes 245768 | tf_op jit(solution)/shard_map/ppermute | solution.py:353
  31.9 8.0 %collective-permute-start.11 = (f16[320,128]{1,0:T(8,128)(2,1)S(1)}, f16[320,128]{1,0:T(8,128)(2,1)S(1)}, u32[]{:S(2)}, u32[]{:S(2)}) collective-permute-start(f16[320,128]{1,0:T(8,128)(2,1)S(1)} %convert_element_type.47), channel_id=1, source_target_pairs={{0,2},{1,3},{2,0},{3,1},{4,6},{5,7},{6,4},{7,5},{8,10},{9,11},{10,... | collective-permute-start | bytes 245768 | tf_op jit(solution)/shard_map/ppermute | solution.py:353
  34.5 5.7 %collective-permute-start.12 = (f16[320,128]{1,0:T(8,128)(2,1)S(1)}, f16[320,128]{1,0:T(8,128)(2,1)S(1)}, u32[]{:S(2)}, u32[]{:S(2)}) collective-permute-start(f16[320,128]{1,0:T(8,128)(2,1)S(1)} %convert_element_type.47), channel_id=1, source_target_pairs={{0,1},{1,0},{2,3},{3,2},{4,5},{5,4},{6,7},{7,6},{8,9},{9,8},{10,11... | collective-permute-start | bytes 245768 | tf_op jit(solution)/shard_map/ppermute | solution.py:353
  35.0 6.3 %collective-permute-start.13 = (f16[320,128]{1,0:T(8,128)(2,1)S(1)}, f16[320,128]{1,0:T(8,128)(2,1)S(1)}, u32[]{:S(2)}, u32[]{:S(2)}) collective-permute-start(f16[320,128]{1,0:T(8,128)(2,1)S(1)} %convert_element_type.47), channel_id=1, source_target_pairs={{0,3},{1,2},{2,1},{3,0},{4,7},{5,6},{6,5},{7,4},{8,11},{9,10},{10,... | collective-permute-start | bytes 245768 | tf_op jit(solution)/shard_map/ppermute | solution.py:353

commit v5 on v4

--- a/solution.py
+++ b/solution.py
@@ -40,12 +40,9 @@
     return tail[1:2, 0:1] - half_temper * jnp.sum(whitened * whitened, axis=0, keepdims=True)
 
 
-def own_kernel(own_ref, core_ref, matrix_ref, tail_ref, out_ref, turned_ref):
-    rows = own_ref.shape[0]
+def own_kernel(own_ref, matrix_ref, tail_ref, out_ref, turned_ref):
     turned_ref[...] = matrix_ref[...].T
-    tail = tail_ref[...].astype(jnp.float32)
-    for part, rows_ref in enumerate((own_ref, core_ref)):
-        out_ref[:, part * rows : (part + 1) * rows] = score_rows(turned_ref[...], tail, rows_ref)
+    out_ref[...] = score_rows(turned_ref[...], tail_ref[...].astype(jnp.float32), own_ref)
 
 
 def near_kernel(groups, own_ref, near_ref, core_ref, done_ref, turned_ref, *refs):
@@ -57,8 +54,8 @@
         turned = others_ref[b - 1] if b else turned_ref[...]
         tail = tails[b][...].astype(jnp.float32)
         for part, rows_ref in enumerate((own_ref, near_ref, core_ref)):
-            if b == 0 and part != 1:
-                line = done_ref[:, part // 2 * rows : (part // 2 + 1) * rows]
+            if b == 0 and part == 0:
+                line = done_ref[...]
             else:
                 line = score_rows(turned, tail, rows_ref)
             out_ref[b : b + 1, part * rows : (part + 1) * rows] = line
@@ -380,9 +377,9 @@
         line = lambda count, lanes: jax.ShapeDtypeStruct((count, lanes * rows), jnp.float32)
         turned = jax.ShapeDtypeStruct((width, width), jnp.bfloat16)
         own_scores, own_turned = call(
-            own_kernel, (line(1, 2), turned), (embeddings, core, matrix, tail), 2 * flops
-        )
-        near, matrices, tails, own_scores = lax.optimization_barrier((near, matrices, tails, own_scores))
+            own_kernel, (line(1, 1), turned), (embeddings, matrix, tail), flops
+        )
+        near, matrices, tails, own_scores, core = lax.optimization_barrier((near, matrices, tails, own_scores, core))
         far = hop(near, 1, 0)
         tails = [tail] + tails
         most_scores, other_turned = call(
@@ -458,8 +455,12 @@
             summed = lax.optimization_barrier(summed.astype(jnp.float16))
             bit *= 2
         last = [0, bit] if bit < n_rows else [0]
-        others = [hop(summed, 0, 1 ^ z) for z in reversed(last)][::-1]
-        mine = [summed] + [hop(summed, 0, z) for z in last[1:]]
+        arrived = {z: hop(summed, 0, z) for z in (last[-1], last[-1] ^ 1, 1)}
+        if len(last) > 1:
+            arrived[bit], arrived[bit ^ 1] = lax.optimization_barrier((arrived[bit], arrived[bit ^ 1]))
+        arrived[0] = summed
+        mine = [arrived[z] for z in last]
+        others = [arrived[z ^ 1] for z in last]
         second, first, count = call(
             lambda *refs: finish_kernel(layout, len(last), *refs),
             (

time: 42.8 us -> 42.1 us (0.984)
  starting transfers between devices: 15.1 us -> 13.5 us
  waiting for transfers between devices: 16 us -> 16.8 us
    ppermute x9, starting transfers between devices: 8.79 us -> 7.85 us  [hop(): return lax.ppermute(value, 'blk', [(i, i ^ blk) for i in range(n_blk)])]
    ppermute x4, starting transfers between devices: 4.7 us -> 4.06 us  [hop(): return lax.ppermute(value, 'rows', [(i, i ^ rows) for i in range(n_rows)])]
    ppermute x4, waiting for transfers between devices: 6.89 us -> 7.36 us  [hop(): return lax.ppermute(value, 'rows', [(i, i ^ rows) for i in range(n_rows)])]
  transfers between devices with their start and end apart: 14 -> 14, of which waited for: 11 -> 9; matrix products, arithmetic and copies ran while one was open for 2% -> 2% of each run, Pallas kernels for 9% -> 9%
where the time goes in v5:
time: 42.1 us; the launch traced here: 41.9 us
  waiting for transfers between devices  16.8 us (40%)
  starting transfers between devices  13.5 us (32%)
  Pallas kernels  7.07 us (17%)
  local copies, waits for them, and re-layouts  2.12 us (5%)
  between operations  1.44 us (3%)
  other arithmetic  0.93 us (2%)
    ppermute x9, waiting for transfers between devices, hop(): return lax.ppermute(value, 'blk', [(i, i ^ blk) for i in range(n_blk)])  7.86 us
    ppermute x9, starting transfers between devices, hop(): return lax.ppermute(value, 'blk', [(i, i ^ blk) for i in range(n_blk)])  7.85 us
    ppermute x4, waiting for transfers between devices, hop(): return lax.ppermute(value, 'rows', [(i, i ^ rows) for i in range(n_rows)])  7.36 us
    pallas_call x8, Pallas kernels, call(): pl.pallas_call(kernel, out_shape=out_shape, in_specs=specs, out_specs=jax...  7.07 us
    ppermute x4, starting transfers between devices, hop(): return lax.ppermute(value, 'rows', [(i, i ^ rows) for i in range(n_rows)])  4.06 us
    unnamed x6, local copies, waits for them, and re-layouts  1.96 us
    ppermute x1, waiting for transfers between devices, hop(): return lax.ppermute(value, ('blk', 'rows'), pairs)  1.6 us
    ppermute x1, starting transfers between devices, hop(): return lax.ppermute(value, ('blk', 'rows'), pairs)  1.59 us
  transfers between devices with their start and end apart: 14, of which 9 were waited for; matrix products, arithmetic and copies ran while one was open for 2% of the time, Pallas kernels for 9%

profile of v5, /device:TPU:0, one launch (start us, length us, event | category | flops | bytes accessed | tf_op | source)
XLA Modules:
  0.0 41.9 jit_solution(1421937529633456416)
XLA Ops:
  0.6 3.0 %collective-permute-start = (bf16[512,384]{1,0:T(8,128)(2,1)}, bf16[512,384]{1,0:T(8,128)(2,1)S(1)}, u32[]{:S(2)}, u32[]{:S(2)}) collective-permute-start(bf16[512,384]{1,0:T(8,128)(2,1)} %refs_0_.3), channel_id=1, source_target_pairs={{0,8},{4,12},{8,0},{12,4},{16,24},{20,28},{24,16},{28,20},{1,9},{5... | collective-permute-start | bytes 1179656 | tf_op jit(solution)/shard_map/ppermute | solution.py:348
  3.6 0.0 collective-permute-start.3
  3.6 1.5 %collective-permute-start.1 = (bf16[384,384]{1,0:T(8,128)(2,1)}, bf16[384,384]{1,0:T(8,128)(2,1)S(1)}, u32[]{:S(2)}, u32[]{:S(2)}) collective-permute-start(bf16[384,384]{1,0:T(8,128)(2,1)} %bitcast.4), channel_id=1, source_target_pairs={{0,16},{4,20},{8,24},{12,28},{16,0},{20,4},{24,8},{28,12},{1,17},{... | collective-permute-start | bytes 884744 | tf_op jit(solution)/shard_map/ppermute | solution.py:348
  5.8 0.1 pad.1.clone
  5.9 0.1 pad.2.clone
  6.0 0.8 %maximum_maximum_fusion.tail_ref.refs_5_.refs_4_ = bf16[16,384]{1,0:T(8,128)(2,1)S(1)} fusion(bf16[1,384]{1,0:T(2,128)(2,1)} %param.6, bf16[16]{0:T(256)(128)(2,1)S(1)} %pad.2.clone, bf16[16]{0:T(256)(128)(2,1)S(1)} %pad.1.clone), kind=kLoop, calls=%fused_computation | loop fusion | flops 36864 | bytes 13120 | tf_op jit(solution)/shard_map/concatenate | solution.py:365
  6.7 0.5 %collective-permute-start.2 = (bf16[16,384]{1,0:T(8,128)(2,1)S(1)}, bf16[16,384]{1,0:T(8,128)(2,1)S(1)}, u32[]{:S(2)}, u32[]{:S(2)}) collective-permute-start(bf16[16,384]{1,0:T(8,128)(2,1)S(1)} %maximum_maximum_fusion.tail_ref.refs_5_.refs_4_), channel_id=1, source_target_pairs={{0,16},{4,20},{8,24},{12,28},{16,0},{20,4},{24,8},{28,12},{1,17},{... | collective-permute-start | bytes 36872 | tf_op jit(solution)/shard_map/ppermute | solution.py:348
  7.2 0.0 copy-start
  7.2 1.0 %copy-done = bf16[512,384]{1,0:T(8,128)(2,1)S(1)} copy-done((bf16[512,384]{1,0:T(8,128)(2,1)S(1)}, bf16[512,384]{1,0:T(8,128)(2,1)}, u32[]{:S(2)}) %copy-start) | copy-done | bytes 393240
  8.2 0.0 copy-start.2
  8.2 1.0 %copy-done.2 = bf16[1,384,384]{2,1,0:T(8,128)(2,1)S(1)} copy-done((bf16[1,384,384]{2,1,0:T(8,128)(2,1)S(1)}, bf16[1,384,384]{2,1,0:T(8,128)(2,1)}, u32[]{:S(2)}) %copy-start.2) | copy-done | bytes 294936
  9.2 0.0 copy-start.1
  9.2 0.5 %shard_map.75 = (f32[1,512]{1,0:T(1,128)S(1)}, bf16[384,384]{1,0:T(8,128)(2,1)S(1)}) custom-call(bf16[512,384]{1,0:T(8,128)(2,1)S(1)} %copy-done, bf16[384,384]{1,0:T(8,128)(2,1)S(1)} %bitcast.5, bf16[16,384]{1,0:T(8,128)(2,1)S(1)} %maximum_maximum_fusion.tail_ref.refs_5_.refs_4_), custom_call_target="tpu_custom_call" | custom-call | flops 150994944 | bytes 997376 | tf_op jit(solution)/shard_map/pallas_call | solution.py:331
  9.7 3.9 %collective-permute-done.2.refs_6_.refs_5_ = bf16[16,384]{1,0:T(8,128)(2,1)S(1)} collective-permute-done((bf16[16,384]{1,0:T(8,128)(2,1)S(1)}, bf16[16,384]{1,0:T(8,128)(2,1)S(1)}, u32[]{:S(2)}, u32[]{:S(2)}) %collective-permute-start.2) | collective-permute-done | bytes 12320 | tf_op jit(solution)/shard_map/ppermute | solution.py:348
  13.5 0.0 collective-permute-done.1.refs_7_
  13.5 0.0 collective-permute-done.refs_1_
  13.5 0.0 collective-permute-done.3.refs_2_
  13.5 0.1 collective-permute-start.4
  13.6 1.3 %shard_map.76 = (f32[2,1536]{1,0:T(2,128)S(1)}, bf16[1,384,384]{2,1,0:T(8,128)(2,1)S(1)}) custom-call(bf16[512,384]{1,0:T(8,128)(2,1)S(1)} %copy-done, bf16[512,384]{1,0:T(8,128)(2,1)S(1)} %collective-permute-done.refs_1_, bf16[512,384]{1,0:T(8,128)(2,1)S(1)} %collective-permute-done.3.refs_2_, f32[1,512]{1,0:T(1,128)S(1)} %get-tuple-element.34.refs_3_, ...), custom_call_target="tpu_custom_call" | custom-call | flops 603979776 | bytes 2103296 | tf_op jit(solution)/shard_map/pallas_call | solution.py:331
  14.9 0.4 collective-permute-done.4.refs_0_.refs_3_
  15.3 0.6 %shard_map.77.refs_0_ = f32[2,2048]{1,0:T(2,128)S(1)} custom-call(bf16[512,384]{1,0:T(8,128)(2,1)S(1)} %collective-permute-done.4.refs_0_.refs_3_, f32[2,1536]{1,0:T(2,128)S(1)} %get-tuple-element.38.refs_1_, bf16[384,384]{1,0:T(8,128)(2,1)S(1)} %get-tuple-element.35.refs_4_.refs_2_, bf16[1,384,384]{2,1,0:T(8,128)(2,1)S(1)} %get-tuple-element.39.refs_3_, ...), custom_call_target="tpu_custom_call" | custom-call | flops 301989888 | bytes 1036288 | tf_op jit(solution)/shard_map/pallas_call | solution.py:331
  16.0 1.2 %collective-permute-start.6 = (f32[2,2048]{1,0:T(2,128)S(1)}, f32[2,2048]{1,0:T(2,128)S(1)}, u32[]{:S(2)}, u32[]{:S(2)}) collective-permute-start(f32[2,2048]{1,0:T(2,128)S(1)} %shard_map.77.refs_0_), channel_id=1, source_target_pairs={{0,8},{4,12},{8,0},{12,4},{16,24},{20,28},{24,16},{28,20},{1,9},{5... | collective-permute-start | bytes 49160 | tf_op jit(solution)/shard_map/ppermute | solution.py:348
  17.1 0.0 collective-permute-start.5
  17.1 2.6 %collective-permute-done.6.refs_2_ = f32[2,2048]{1,0:T(2,128)S(1)} collective-permute-done((f32[2,2048]{1,0:T(2,128)S(1)}, f32[2,2048]{1,0:T(2,128)S(1)}, u32[]{:S(2)}, u32[]{:S(2)}) %collective-permute-start.6) | collective-permute-done | bytes 16416 | tf_op jit(solution)/shard_map/ppermute | solution.py:348
  19.8 0.0 collective-permute-start.7
  19.8 0.0 copy-done.1
  19.8 0.6 %shard_map.78 = (bf16[2048,512]{1,0:T(8,128)(2,1)S(1)}, f32[384,2048]{1,0:T(8,128)S(1)}) custom-call(bf16[512,384]{1,0:T(8,128)(2,1)S(1)} %copy-done.1, bf16[512,384]{1,0:T(8,128)(2,1)S(1)} %collective-permute-done.refs_1_, bf16[512,384]{1,0:T(8,128)(2,1)S(1)} %collective-permute-done.3.refs_2_, bf16[512,384]{1,0:T(8,128)(2,1)S(1)} %collective-permute-done.4.refs_0_.refs_3_), custom_call_target="tpu_custom_call" | custom-call | bytes 6815744 | tf_op jit(solution)/shard_map/pallas_call | solution.py:331
  20.4 0.0 collective-permute-done.5.refs_1_
  20.4 0.5 %collective-permute-done.7.refs_3_ = f32[2,2048]{1,0:T(2,128)S(1)} collective-permute-done((f32[2,2048]{1,0:T(2,128)S(1)}, f32[2,2048]{1,0:T(2,128)S(1)}, u32[]{:S(2)}, u32[]{:S(2)}) %collective-permute-start.7) | collective-permute-done | bytes 16416 | tf_op jit(solution)/shard_map/ppermute | solution.py:348
  21.0 1.4 %shard_map.79 = (f32[8,2048]{1,0:T(8,128)S(1)}, f32[48,128]{1,0:T(8,128)S(1)}, f32[8,512]{1,0:T(8,128)}, f32[320,128]{1,0:T(8,128)S(1)}, f32[320,128]{1,0:T(8,128)S(1)}) custom-call(f32[2,2048]{1,0:T(2,128)S(1)} %shard_map.77.refs_0_, f32[2,2048]{1,0:T(2,128)S(1)} %collective-permute-done.5.refs_1_, f32[2,2048]{1,0:T(2,128)S(1)} %collective-permute-done.6.refs_2_, ...), custom_call_target="tpu_custom_call" | custom-call | flops 1207959552 | bytes 5742592 | tf_op jit(solution)/shard_map/pallas_call | solution.py:331
  22.4 1.6 %collective-permute-start.8 = (f16[320,128]{1,0:T(8,128)(2,1)S(1)}, f16[320,128]{1,0:T(8,128)(2,1)S(1)}, u32[]{:S(2)}, u32[]{:S(2)}) collective-permute-start(f16[320,128]{1,0:T(8,128)(2,1)S(1)} %convert_element_type.41), channel_id=1, source_target_pairs={{0,16},{4,20},{8,24},{12,28},{16,0},{20,4},{24,8},{28,12},{1,17},{... | collective-permute-start | bytes 245768 | tf_op jit(solution)/shard_map/ppermute | solution.py:348
  24.0 1.6 %collective-permute-start.9 = (f16[320,128]{1,0:T(8,128)(2,1)S(1)}, f16[320,128]{1,0:T(8,128)(2,1)S(1)}, u32[]{:S(2)}, u32[]{:S(2)}) collective-permute-start(f16[320,128]{1,0:T(8,128)(2,1)S(1)} %convert_element_type.42), channel_id=1, source_target_pairs={{0,17},{1,16},{2,19},{3,18},{4,21},{5,20},{6,23},{7,22},{8,25},{9,... | collective-permute-start | bytes 245768 | tf_op jit(solution)/shard_map/ppermute | solution.py:354
  25.6 1.3 %shard_map.80 = (f32[320,128]{1,0:T(8,128)S(1)}, f32[320,128]{1,0:T(8,128)S(1)}) custom-call(f32[8,2048]{1,0:T(8,128)S(1)} %get-tuple-element.45.refs_0_, f32[48,128]{1,0:T(8,128)S(1)} %get-tuple-element.46.refs_1_, bf16[2048,512]{1,0:T(8,128)(2,1)S(1)} %get-tuple-element.42.refs_4_.refs_2_, f32[384,2048]{1,0:T(8,128)S(1)} %get-tuple-element.43.refs_5_.refs_3_), custom_call_target="tpu_custom_call" | custom-call | flops 1207959552 | bytes 5660672 | tf_op jit(solution)/shard_map/pallas_call | solution.py:331
  26.9 0.5 %collective-permute-start.10 = (f16[320,128]{1,0:T(8,128)(2,1)S(1)}, f16[320,128]{1,0:T(8,128)(2,1)S(1)}, u32[]{:S(2)}, u32[]{:S(2)}) collective-permute-start(f16[320,128]{1,0:T(8,128)(2,1)S(1)} %convert_element_type.44), channel_id=1, source_target_pairs={{0,1},{1,0},{2,3},{3,2},{4,5},{5,4},{6,7},{7,6},{8,9},{9,8},{10,11... | collective-permute-start | bytes 245768 | tf_op jit(solution)/shard_map/ppermute | solution.py:350
  27.4 0.4 collective-permute-done.8
  27.8 1.6 %collective-permute-done.9 = f16[320,128]{1,0:T(8,128)(2,1)S(1)} collective-permute-done((f16[320,128]{1,0:T(8,128)(2,1)S(1)}, f16[320,128]{1,0:T(8,128)(2,1)S(1)}, u32[]{:S(2)}, u32[]{:S(2)}) %collective-permute-start.9) | collective-permute-done | bytes 81952 | tf_op jit(solution)/shard_map/ppermute | solution.py:354
  29.4 1.9 %collective-permute-done.10 = f16[320,128]{1,0:T(8,128)(2,1)S(1)} collective-permute-done((f16[320,128]{1,0:T(8,128)(2,1)S(1)}, f16[320,128]{1,0:T(8,128)(2,1)S(1)}, u32[]{:S(2)}, u32[]{:S(2)}) %collective-permute-start.10) | collective-permute-done | bytes 81952 | tf_op jit(solution)/shard_map/ppermute | solution.py:350
  31.4 0.2 shard_map.81
  31.6 2.7 %collective-permute-start.11 = (f16[320,128]{1,0:T(8,128)(2,1)S(1)}, f16[320,128]{1,0:T(8,128)(2,1)S(1)}, u32[]{:S(2)}, u32[]{:S(2)}) collective-permute-start(f16[320,128]{1,0:T(8,128)(2,1)S(1)} %convert_element_type.47), channel_id=1, source_target_pairs={{0,2},{1,3},{2,0},{3,1},{4,6},{5,7},{6,4},{7,5},{8,10},{9,11},{10,... | collective-permute-start | bytes 245768 | tf_op jit(solution)/shard_map/ppermute | solution.py:350
  34.3 0.2 collective-permute-start.12
  34.5 0.7 %collective-permute-start.13 = (f16[320,128]{1,0:T(8,128)(2,1)S(1)}, f16[320,128]{1,0:T(8,128)(2,1)S(1)}, u32[]{:S(2)}, u32[]{:S(2)}) collective-permute-start(f16[320,128]{1,0:T(8,128)(2,1)S(1)} %convert_element_type.47), channel_id=1, source_target_pairs={{0,1},{1,0},{2,3},{3,2},{4,5},{5,4},{6,7},{7,6},{8,9},{9,8},{10,11... | collective-permute-start | bytes 245768 | tf_op jit(solution)/shard_map/ppermute | solution.py:350
  35.2 4.1 %collective-permute-done.11 = f16[320,128]{1,0:T(8,128)(2,1)S(1)} collective-permute-done((f16[320,128]{1,0:T(8,128)(2,1)S(1)}, f16[320,128]{1,0:T(8,128)(2,1)S(1)}, u32[]{:S(2)}, u32[]{:S(2)}) %collective-permute-start.11) | collective-permute-done | bytes 81952 | tf_op jit(solution)/shard_map/ppermute | solution.py:350
  39.3 1.3 %collective-permute-done.12 = f16[320,128]{1,0:T(8,128)(2,1)S(1)} collective-permute-done((f16[320,128]{1,0:T(8,128)(2,1)S(1)}, f16[320,128]{1,0:T(8,128)(2,1)S(1)}, u32[]{:S(2)}, u32[]{:S(2)}) %collective-permute-start.12) | collective-permute-done | bytes 81952 | tf_op jit(solution)/shard_map/ppermute | solution.py:350
  40.6 0.0 collective-permute-done.13
  40.7 1.2 %shard_map.82 = (f32[384,384]{1,0:T(8,128)}, f32[8,384]{1,0:T(8,128)}, f32[1,8]{1,0:T(1,128)}) custom-call(f32[320,128]{1,0:T(8,128)S(1)} %convert_element_type.48.refs_0_, f32[320,128]{1,0:T(8,128)S(1)} %convert_element_type.49.refs_1_, f32[320,128]{1,0:T(8,128)S(1)} %convert_element_type.50.refs_2_, f32[320,128]{1,0:T(8,128)S(1)} %convert_element_type.51.refs_3_), custom_call_target="tpu_custom_call" | custom-call | bytes 1257504 | tf_op jit(solution)/shard_map/pallas_call | solution.py:331
  (14 shorter events, 0.2 us)
Async XLA Ops:
  0.6 12.9 %collective-permute-start = (bf16[512,384]{1,0:T(8,128)(2,1)}, bf16[512,384]{1,0:T(8,128)(2,1)S(1)}, u32[]{:S(2)}, u32[]{:S(2)}) collective-permute-start(bf16[512,384]{1,0:T(8,128)(2,1)} %refs_0_.3), channel_id=1, source_target_pairs={{0,8},{4,12},{8,0},{12,4},{16,24},{20,28},{24,16},{28,20},{1,9},{5... | collective-permute-start | bytes 1179656 | tf_op jit(solution)/shard_map/ppermute | solution.py:348
  3.6 9.9 %collective-permute-start.3 = (bf16[512,384]{1,0:T(8,128)(2,1)}, bf16[512,384]{1,0:T(8,128)(2,1)S(1)}, u32[]{:S(2)}, u32[]{:S(2)}) collective-permute-start(bf16[512,384]{1,0:T(8,128)(2,1)} %refs_0_.3), channel_id=1, source_target_pairs={{0,4},{4,0},{8,12},{12,8},{16,20},{20,16},{24,28},{28,24},{1,5},{5... | collective-permute-start | bytes 1179656 | tf_op jit(solution)/shard_map/ppermute | solution.py:348
  3.6 9.9 %collective-permute-start.1 = (bf16[384,384]{1,0:T(8,128)(2,1)}, bf16[384,384]{1,0:T(8,128)(2,1)S(1)}, u32[]{:S(2)}, u32[]{:S(2)}) collective-permute-start(bf16[384,384]{1,0:T(8,128)(2,1)} %bitcast.4), channel_id=1, source_target_pairs={{0,16},{4,20},{8,24},{12,28},{16,0},{20,4},{24,8},{28,12},{1,17},{... | collective-permute-start | bytes 884744 | tf_op jit(solution)/shard_map/ppermute | solution.py:348
  6.7 6.8 %collective-permute-start.2 = (bf16[16,384]{1,0:T(8,128)(2,1)S(1)}, bf16[16,384]{1,0:T(8,128)(2,1)S(1)}, u32[]{:S(2)}, u32[]{:S(2)}) collective-permute-start(bf16[16,384]{1,0:T(8,128)(2,1)S(1)} %maximum_maximum_fusion.tail_ref.refs_5_.refs_4_), channel_id=1, source_target_pairs={{0,16},{4,20},{8,24},{12,28},{16,0},{20,4},{24,8},{28,12},{1,17},{... | collective-permute-start | bytes 36872 | tf_op jit(solution)/shard_map/ppermute | solution.py:348
  7.2 1.0 %copy-start = (bf16[512,384]{1,0:T(8,128)(2,1)S(1)}, bf16[512,384]{1,0:T(8,128)(2,1)}, u32[]{:S(2)}) copy-start(bf16[512,384]{1,0:T(8,128)(2,1)} %refs_0_.3) | copy-start | bytes 1179652
  8.2 1.0 %copy-start.2 = (bf16[1,384,384]{2,1,0:T(8,128)(2,1)S(1)}, bf16[1,384,384]{2,1,0:T(8,128)(2,1)}, u32[]{:S(2)}) copy-start(bf16[1,384,384]{2,1,0:T(8,128)(2,1)} %param.5) | copy-start | bytes 884740
  9.2 10.6 %copy-start.1 = (bf16[512,384]{1,0:T(8,128)(2,1)S(1)}, bf16[512,384]{1,0:T(8,128)(2,1)}, u32[]{:S(2)}) copy-start(bf16[512,384]{1,0:T(8,128)(2,1)} %refs_0_.3) | copy-start | bytes 1179652
  13.5 1.8 %collective-permute-start.4 = (bf16[512,384]{1,0:T(8,128)(2,1)S(1)}, bf16[512,384]{1,0:T(8,128)(2,1)S(1)}, u32[]{:S(2)}, u32[]{:S(2)}) collective-permute-start(bf16[512,384]{1,0:T(8,128)(2,1)S(1)} %collective-permute-done.refs_1_), channel_id=1, source_target_pairs={{0,4},{4,0},{8,12},{12,8},{16,20},{20,16},{24,28},{28,24},{1,5},{5... | collective-permute-start | bytes 1179656 | tf_op jit(solution)/shard_map/ppermute | solution.py:348
  16.0 3.8 %collective-permute-start.6 = (f32[2,2048]{1,0:T(2,128)S(1)}, f32[2,2048]{1,0:T(2,128)S(1)}, u32[]{:S(2)}, u32[]{:S(2)}) collective-permute-start(f32[2,2048]{1,0:T(2,128)S(1)} %shard_map.77.refs_0_), channel_id=1, source_target_pairs={{0,8},{4,12},{8,0},{12,4},{16,24},{20,28},{24,16},{28,20},{1,9},{5... | collective-permute-start | bytes 49160 | tf_op jit(solution)/shard_map/ppermute | solution.py:348
  17.1 3.3 %collective-permute-start.5 = (f32[2,2048]{1,0:T(2,128)S(1)}, f32[2,2048]{1,0:T(2,128)S(1)}, u32[]{:S(2)}, u32[]{:S(2)}) collective-permute-start(f32[2,2048]{1,0:T(2,128)S(1)} %shard_map.77.refs_0_), channel_id=1, source_target_pairs={{0,4},{4,0},{8,12},{12,8},{16,20},{20,16},{24,28},{28,24},{1,5},{5... | collective-permute-start | bytes 49160 | tf_op jit(solution)/shard_map/ppermute | solution.py:348
  19.8 1.2 %collective-permute-start.7 = (f32[2,2048]{1,0:T(2,128)S(1)}, f32[2,2048]{1,0:T(2,128)S(1)}, u32[]{:S(2)}, u32[]{:S(2)}) collective-permute-start(f32[2,2048]{1,0:T(2,128)S(1)} %collective-permute-done.6.refs_2_), channel_id=1, source_target_pairs={{0,4},{4,0},{8,12},{12,8},{16,20},{20,16},{24,28},{28,24},{1,5},{5... | collective-permute-start | bytes 49160 | tf_op jit(solution)/shard_map/ppermute | solution.py:348
  22.4 5.4 %collective-permute-start.8 = (f16[320,128]{1,0:T(8,128)(2,1)S(1)}, f16[320,128]{1,0:T(8,128)(2,1)S(1)}, u32[]{:S(2)}, u32[]{:S(2)}) collective-permute-start(f16[320,128]{1,0:T(8,128)(2,1)S(1)} %convert_element_type.41), channel_id=1, source_target_pairs={{0,16},{4,20},{8,24},{12,28},{16,0},{20,4},{24,8},{28,12},{1,17},{... | collective-permute-start | bytes 245768 | tf_op jit(solution)/shard_map/ppermute | solution.py:348
  24.0 5.4 %collective-permute-start.9 = (f16[320,128]{1,0:T(8,128)(2,1)S(1)}, f16[320,128]{1,0:T(8,128)(2,1)S(1)}, u32[]{:S(2)}, u32[]{:S(2)}) collective-permute-start(f16[320,128]{1,0:T(8,128)(2,1)S(1)} %convert_element_type.42), channel_id=1, source_target_pairs={{0,17},{1,16},{2,19},{3,18},{4,21},{5,20},{6,23},{7,22},{8,25},{9,... | collective-permute-start | bytes 245768 | tf_op jit(solution)/shard_map/ppermute | solution.py:354
  26.9 4.5 %collective-permute-start.10 = (f16[320,128]{1,0:T(8,128)(2,1)S(1)}, f16[320,128]{1,0:T(8,128)(2,1)S(1)}, u32[]{:S(2)}, u32[]{:S(2)}) collective-permute-start(f16[320,128]{1,0:T(8,128)(2,1)S(1)} %convert_element_type.44), channel_id=1, source_target_pairs={{0,1},{1,0},{2,3},{3,2},{4,5},{5,4},{6,7},{7,6},{8,9},{9,8},{10,11... | collective-permute-start | bytes 245768 | tf_op jit(solution)/shard_map/ppermute | solution.py:350
  31.6 7.7 %collective-permute-start.11 = (f16[320,128]{1,0:T(8,128)(2,1)S(1)}, f16[320,128]{1,0:T(8,128)(2,1)S(1)}, u32[]{:S(2)}, u32[]{:S(2)}) collective-permute-start(f16[320,128]{1,0:T(8,128)(2,1)S(1)} %convert_element_type.47), channel_id=1, source_target_pairs={{0,2},{1,3},{2,0},{3,1},{4,6},{5,7},{6,4},{7,5},{8,10},{9,11},{10,... | collective-permute-start | bytes 245768 | tf_op jit(solution)/shard_map/ppermute | solution.py:350
  34.3 6.3 %collective-permute-start.12 = (f16[320,128]{1,0:T(8,128)(2,1)S(1)}, f16[320,128]{1,0:T(8,128)(2,1)S(1)}, u32[]{:S(2)}, u32[]{:S(2)}) collective-permute-start(f16[320,128]{1,0:T(8,128)(2,1)S(1)} %convert_element_type.47), channel_id=1, source_target_pairs={{0,3},{1,2},{2,1},{3,0},{4,7},{5,6},{6,5},{7,4},{8,11},{9,10},{10,... | collective-permute-start | bytes 245768 | tf_op jit(solution)/shard_map/ppermute | solution.py:350
  34.5 6.2 %collective-permute-start.13 = (f16[320,128]{1,0:T(8,128)(2,1)S(1)}, f16[320,128]{1,0:T(8,128)(2,1)S(1)}, u32[]{:S(2)}, u32[]{:S(2)}) collective-permute-start(f16[320,128]{1,0:T(8,128)(2,1)S(1)} %convert_element_type.47), channel_id=1, source_target_pairs={{0,1},{1,0},{2,3},{3,2},{4,5},{5,4},{6,7},{7,6},{8,9},{9,8},{10,11... | collective-permute-start | bytes 245768 | tf_op jit(solution)/shard_map/ppermute | solution.py:350

commit v6 on v5

--- a/solution.py
+++ b/solution.py
@@ -122,53 +122,47 @@
         self.half = -(-(self.counts + comps) // 16) * 8
         self.rows = self.half + HEAD
 
-    def write(self, out_ref, flip, at, value):
+    def write(self, outs, at, value):
         done = 0
         while done < value.shape[0]:
             side, row = divmod(at + done, self.half)
             count = min(value.shape[0] - done, self.half - row)
-            out_ref[side ^ flip, row : row + count, :] = value[done : done + count]
+            outs[side][row : row + count, :] = value[done : done + count]
             done += count
 
 
-def store_second(blocks, normalizer, layout, out_ref, flip):
+def store_second(blocks, normalizer, layout, outs):
     parts = layout.parts
-    largest = jnp.zeros((1, 1), jnp.float32)
-    for a in range(parts):
-        largest = jnp.maximum(largest, jnp.max(jnp.abs(blocks[a, a]), keepdims=True))
+    i, j = pair_masks()
+    lines = [jnp.sum(jnp.where(i == j, blocks[a, a], 0.0), axis=0, keepdims=True) for a in range(parts)]
+    largest = jnp.max(highest(lines), keepdims=True)
     exponent = exponent_of(largest * normalizer)
     factor = normalizer * power(-exponent)
-    i, j = pair_masks()
     at = 0
     for a, b in layout.pairs:
-        layout.write(out_ref, flip, at, blocks[a, b] * factor)
+        layout.write(outs, at, blocks[a, b] * factor)
         at += LANES
     diagonal = [blocks[a, a] * factor for a in range(parts)]
     for a in range(0, parts - 1, 2):
-        layout.write(out_ref, flip, at, jnp.where(i <= j, diagonal[a], diagonal[a + 1]))
+        layout.write(outs, at, jnp.where(i <= j, diagonal[a], diagonal[a + 1]))
         at += LANES
     if parts % 2:
         half = LANES // 2
         lower = pltpu.roll(diagonal[-1][half:], half, 1)
-        layout.write(out_ref, flip, at, jnp.where(i <= j, diagonal[-1], 0.0)[:half] + jnp.where((i > j)[:half], lower, 0.0))
+        layout.write(outs, at, jnp.where(i <= j, diagonal[-1], 0.0)[:half] + jnp.where((i > j)[:half], lower, 0.0))
         at += half
-    lines = [jnp.sum(jnp.where(i == j, d, 0.0), axis=0, keepdims=True) for d in diagonal]
+    lines = [line * factor for line in lines]
     lines += [jnp.zeros((1, LANES), jnp.float32)] * (layout.firsts - at - parts)
-    layout.write(out_ref, flip, at, jnp.concatenate(lines, axis=0))
+    layout.write(outs, at, jnp.concatenate(lines, axis=0))
     for side in range(2):
-        out_ref[side, layout.half : layout.half + 1, :] = jnp.broadcast_to(exponent, (1, LANES))
-
-
-def part_ways(table_ref, flip, outs):
-    outs[0][...] = table_ref[flip]
-    outs[1][...] = table_ref[1 - flip]
-
-
-def store_low(low_ref, layout, out_ref, flip):
+        outs[side][layout.half : layout.half + 1, :] = jnp.broadcast_to(exponent, (1, LANES))
+
+
+def store_low(low_ref, layout, outs):
     body = low_ref.shape[0] - HEAD
-    layout.write(out_ref, flip, layout.firsts, low_ref[:body, :])
+    layout.write(outs, layout.firsts, low_ref[:body, :])
     for side in range(2):
-        out_ref[side, layout.half + 1 :, :] = low_ref[body + 1 :, :]
+        outs[side][layout.half + 1 :, :] = low_ref[body + 1 :, :]
 
 
 def own_place(me):
@@ -196,9 +190,9 @@
 
 def give_kernel(offsets, normalizer, layout, *refs):
     scores, (rows_ref, columns_ref), refs = refs[:4], refs[4:6], refs[6:]
-    resp_ref, low_ref, here_ref, *outs, message_ref = refs
+    resp_ref, low_ref, here_ref, *outs = refs
     comps, rows = here_ref.shape
-    me, flip = place_here()
+    me, _ = place_here()
     own = own_place(me)
     index = lax.broadcasted_iota(jnp.int32, (comps, 4 * rows), 0)
     table = jnp.zeros((comps, 4 * rows), jnp.float32)
@@ -237,17 +231,15 @@
     low_ref[at : at + comps, :] = jnp.broadcast_to(count, (comps, LANES))
     low_ref[body:, :] = jnp.broadcast_to(exponent, (HEAD, LANES))
     for at, total in enumerate(totals):
-        store_second(total, normalizer, layout, message_ref, 0)
-        store_low(low_ref, layout, message_ref, 0)
-        part_ways(message_ref, flip, outs[2 * at : 2 * at + 2])
+        store_second(total, normalizer, layout, outs[2 * at : 2 * at + 2])
+        store_low(low_ref, layout, outs[2 * at : 2 * at + 2])
 
 
 def keep_kernel(normalizer, layout, resp_ref, low_ref, rows_ref, columns_ref, *refs):
-    outs, message_ref = refs[:2], refs[2]
-    me, flip = place_here()
-    store_second(moment(resp_ref[...], me, rows_ref, columns_ref, layout)[0], normalizer, layout, message_ref, 0)
-    store_low(low_ref, layout, message_ref, 0)
-    part_ways(message_ref, flip, outs)
+    outs = refs
+    me, _ = place_here()
+    store_second(moment(resp_ref[...], me, rows_ref, columns_ref, layout)[0], normalizer, layout, outs)
+    store_low(low_ref, layout, outs)
 
 
 def tree(values):
@@ -410,7 +402,7 @@
         far_scores = hop(near_scores, 1, 0)
 
         sent = jax.ShapeDtypeStruct((layout.rows, LANES), jnp.float32)
-        whole = pltpu.VMEM((2, layout.rows, LANES), jnp.float32)
+        odd = (lax.axis_index("rows") & 1) == 1
         flops = 4 * 4 * rows * width * width
         resp, low, here, *given = call(
             lambda *refs: give_kernel([4 * b for b in range(1, groups)], normalizer, layout, *refs),
@@ -422,21 +414,19 @@
             ),
             (scores, core_scores, near_scores, far_scores, *both),
             flops * (groups - 1),
-            [whole],
         )
         received = {}
         for b in range(1, groups):
             for z in (1, 0):
-                received[b, z] = hop(given[2 * b - 2 + z].astype(jnp.float16), 4 * b, z)
+                received[b, z] = hop(jnp.where(odd, given[2 * b - 1 - z], given[2 * b - 2 + z]).astype(jnp.float16), 4 * b, z)
         kept = call(
             lambda *refs: keep_kernel(normalizer, layout, *refs),
             (sent, sent),
             (resp, low, *both),
             flops,
-            [whole],
-        )
-        received[0, 0] = lax.optimization_barrier(kept[0].astype(jnp.float16))
-        received[0, 1] = hop(kept[1].astype(jnp.float16), 0, 1)
+        )
+        received[0, 0] = lax.optimization_barrier(jnp.where(odd, kept[1], kept[0]).astype(jnp.float16))
+        received[0, 1] = hop(jnp.where(odd, kept[0], kept[1]).astype(jnp.float16), 0, 1)
         for b in range(1, groups):
             received[b, 0], received[b, 1] = lax.optimization_barrier((received[b, 0], received[b, 1]))
         wide = {key: value.astype(jnp.float32) for key, value in received.items()}

time: 42.1 us -> 42 us (level)
  no operation moved by 1% of the time
where the time goes in v6:
time: 42 us; the launch traced here: 41.8 us
  waiting for transfers between devices  16.8 us (40%)
  starting transfers between devices  13.4 us (32%)
  Pallas kernels  7.02 us (17%)
  local copies, waits for them, and re-layouts  2.12 us (5%)
  between operations  1.44 us (3%)
  other arithmetic  0.96 us (2%)
    ppermute x9, waiting for transfers between devices, hop(): return lax.ppermute(value, 'blk', [(i, i ^ blk) for i in range(n_blk)])  7.96 us
    ppermute x9, starting transfers between devices, hop(): return lax.ppermute(value, 'blk', [(i, i ^ blk) for i in range(n_blk)])  7.85 us
    ppermute x4, waiting for transfers between devices, hop(): return lax.ppermute(value, 'rows', [(i, i ^ rows) for i in range(n_rows)])  7.36 us
    pallas_call x8, Pallas kernels, call(): pl.pallas_call(kernel, out_shape=out_shape, in_specs=specs, out_specs=jax...  7.02 us
    ppermute x4, starting transfers between devices, hop(): return lax.ppermute(value, 'rows', [(i, i ^ rows) for i in range(n_rows)])  4.07 us
    unnamed x6, local copies, waits for them, and re-layouts  1.96 us
    ppermute x1, starting transfers between devices, hop(): return lax.ppermute(value, ('blk', 'rows'), pairs)  1.52 us
    ppermute x1, waiting for transfers between devices, hop(): return lax.ppermute(value, ('blk', 'rows'), pairs)  1.52 us
  transfers between devices with their start and end apart: 14, of which 9 were waited for; matrix products, arithmetic and copies ran while one was open for 2% of the time, Pallas kernels for 9%

profile of v6, /device:TPU:0, one launch (start us, length us, event | category | flops | bytes accessed | tf_op | source)
XLA Modules:
  0.0 41.8 jit_solution(1965680745157590163)
XLA Ops:
  0.6 3.0 %collective-permute-start = (bf16[512,384]{1,0:T(8,128)(2,1)}, bf16[512,384]{1,0:T(8,128)(2,1)S(1)}, u32[]{:S(2)}, u32[]{:S(2)}) collective-permute-start(bf16[512,384]{1,0:T(8,128)(2,1)} %refs_0_.3), channel_id=1, source_target_pairs={{0,8},{4,12},{8,0},{12,4},{16,24},{20,28},{24,16},{28,20},{1,9},{5... | collective-permute-start | bytes 1179656 | tf_op jit(solution)/shard_map/ppermute | solution.py:340
  3.6 0.0 collective-permute-start.3
  3.6 1.5 %collective-permute-start.1 = (bf16[384,384]{1,0:T(8,128)(2,1)}, bf16[384,384]{1,0:T(8,128)(2,1)S(1)}, u32[]{:S(2)}, u32[]{:S(2)}) collective-permute-start(bf16[384,384]{1,0:T(8,128)(2,1)} %bitcast.4), channel_id=1, source_target_pairs={{0,16},{4,20},{8,24},{12,28},{16,0},{20,4},{24,8},{28,12},{1,17},{... | collective-permute-start | bytes 884744 | tf_op jit(solution)/shard_map/ppermute | solution.py:340
  5.8 0.1 pad.1.clone
  5.9 0.1 pad.2.clone
  6.0 0.8 %maximum_maximum_fusion.tail_ref.refs_5_.refs_4_ = bf16[16,384]{1,0:T(8,128)(2,1)S(1)} fusion(bf16[1,384]{1,0:T(2,128)(2,1)} %param.6, bf16[16]{0:T(256)(128)(2,1)S(1)} %pad.2.clone, bf16[16]{0:T(256)(128)(2,1)S(1)} %pad.1.clone), kind=kLoop, calls=%fused_computation.4 | loop fusion | flops 36864 | bytes 13120 | tf_op jit(solution)/shard_map/concatenate | solution.py:357
  6.7 0.5 %collective-permute-start.2 = (bf16[16,384]{1,0:T(8,128)(2,1)S(1)}, bf16[16,384]{1,0:T(8,128)(2,1)S(1)}, u32[]{:S(2)}, u32[]{:S(2)}) collective-permute-start(bf16[16,384]{1,0:T(8,128)(2,1)S(1)} %maximum_maximum_fusion.tail_ref.refs_5_.refs_4_), channel_id=1, source_target_pairs={{0,16},{4,20},{8,24},{12,28},{16,0},{20,4},{24,8},{28,12},{1,17},{... | collective-permute-start | bytes 36872 | tf_op jit(solution)/shard_map/ppermute | solution.py:340
  7.2 0.0 copy-start
  7.2 1.0 %copy-done = bf16[512,384]{1,0:T(8,128)(2,1)S(1)} copy-done((bf16[512,384]{1,0:T(8,128)(2,1)S(1)}, bf16[512,384]{1,0:T(8,128)(2,1)}, u32[]{:S(2)}) %copy-start) | copy-done | bytes 393240
  8.2 0.0 copy-start.2
  8.2 1.0 %copy-done.2 = bf16[1,384,384]{2,1,0:T(8,128)(2,1)S(1)} copy-done((bf16[1,384,384]{2,1,0:T(8,128)(2,1)S(1)}, bf16[1,384,384]{2,1,0:T(8,128)(2,1)}, u32[]{:S(2)}) %copy-start.2) | copy-done | bytes 294936
  9.2 0.0 copy-start.1
  9.2 0.5 %shard_map.75 = (f32[1,512]{1,0:T(1,128)S(1)}, bf16[384,384]{1,0:T(8,128)(2,1)S(1)}) custom-call(bf16[512,384]{1,0:T(8,128)(2,1)S(1)} %copy-done, bf16[384,384]{1,0:T(8,128)(2,1)S(1)} %bitcast.5, bf16[16,384]{1,0:T(8,128)(2,1)S(1)} %maximum_maximum_fusion.tail_ref.refs_5_.refs_4_), custom_call_target="tpu_custom_call" | custom-call | flops 150994944 | bytes 997376 | tf_op jit(solution)/shard_map/pallas_call | solution.py:323
  9.7 3.9 %collective-permute-done.2.refs_6_.refs_5_ = bf16[16,384]{1,0:T(8,128)(2,1)S(1)} collective-permute-done((bf16[16,384]{1,0:T(8,128)(2,1)S(1)}, bf16[16,384]{1,0:T(8,128)(2,1)S(1)}, u32[]{:S(2)}, u32[]{:S(2)}) %collective-permute-start.2) | collective-permute-done | bytes 12320 | tf_op jit(solution)/shard_map/ppermute | solution.py:340
  13.5 0.0 collective-permute-done.1.refs_7_
  13.5 0.0 collective-permute-done.refs_1_
  13.5 0.0 collective-permute-done.3.refs_2_
  13.5 0.1 collective-permute-start.4
  13.6 1.3 %shard_map.76 = (f32[2,1536]{1,0:T(2,128)S(1)}, bf16[1,384,384]{2,1,0:T(8,128)(2,1)S(1)}) custom-call(bf16[512,384]{1,0:T(8,128)(2,1)S(1)} %copy-done, bf16[512,384]{1,0:T(8,128)(2,1)S(1)} %collective-permute-done.refs_1_, bf16[512,384]{1,0:T(8,128)(2,1)S(1)} %collective-permute-done.3.refs_2_, f32[1,512]{1,0:T(1,128)S(1)} %get-tuple-element.34.refs_3_, ...), custom_call_target="tpu_custom_call" | custom-call | flops 603979776 | bytes 2103296 | tf_op jit(solution)/shard_map/pallas_call | solution.py:323
  14.9 0.4 collective-permute-done.4.refs_0_.refs_3_
  15.3 0.6 %shard_map.77.refs_0_ = f32[2,2048]{1,0:T(2,128)S(1)} custom-call(bf16[512,384]{1,0:T(8,128)(2,1)S(1)} %collective-permute-done.4.refs_0_.refs_3_, f32[2,1536]{1,0:T(2,128)S(1)} %get-tuple-element.38.refs_1_, bf16[384,384]{1,0:T(8,128)(2,1)S(1)} %get-tuple-element.35.refs_4_.refs_2_, bf16[1,384,384]{2,1,0:T(8,128)(2,1)S(1)} %get-tuple-element.39.refs_3_, ...), custom_call_target="tpu_custom_call" | custom-call | flops 301989888 | bytes 1036288 | tf_op jit(solution)/shard_map/pallas_call | solution.py:323
  16.0 1.2 %collective-permute-start.6 = (f32[2,2048]{1,0:T(2,128)S(1)}, f32[2,2048]{1,0:T(2,128)S(1)}, u32[]{:S(2)}, u32[]{:S(2)}) collective-permute-start(f32[2,2048]{1,0:T(2,128)S(1)} %shard_map.77.refs_0_), channel_id=1, source_target_pairs={{0,8},{4,12},{8,0},{12,4},{16,24},{20,28},{24,16},{28,20},{1,9},{5... | collective-permute-start | bytes 49160 | tf_op jit(solution)/shard_map/ppermute | solution.py:340
  17.1 0.0 collective-permute-start.5
  17.1 2.6 %collective-permute-done.6.refs_2_ = f32[2,2048]{1,0:T(2,128)S(1)} collective-permute-done((f32[2,2048]{1,0:T(2,128)S(1)}, f32[2,2048]{1,0:T(2,128)S(1)}, u32[]{:S(2)}, u32[]{:S(2)}) %collective-permute-start.6) | collective-permute-done | bytes 16416 | tf_op jit(solution)/shard_map/ppermute | solution.py:340
  19.8 0.0 collective-permute-start.7
  19.8 0.0 copy-done.1
  19.8 0.6 %shard_map.78 = (bf16[2048,512]{1,0:T(8,128)(2,1)S(1)}, f32[384,2048]{1,0:T(8,128)S(1)}) custom-call(bf16[512,384]{1,0:T(8,128)(2,1)S(1)} %copy-done.1, bf16[512,384]{1,0:T(8,128)(2,1)S(1)} %collective-permute-done.refs_1_, bf16[512,384]{1,0:T(8,128)(2,1)S(1)} %collective-permute-done.3.refs_2_, bf16[512,384]{1,0:T(8,128)(2,1)S(1)} %collective-permute-done.4.refs_0_.refs_3_), custom_call_target="tpu_custom_call" | custom-call | bytes 6815744 | tf_op jit(solution)/shard_map/pallas_call | solution.py:323
  20.4 0.0 collective-permute-done.5.refs_1_
  20.4 0.5 %collective-permute-done.7.refs_3_ = f32[2,2048]{1,0:T(2,128)S(1)} collective-permute-done((f32[2,2048]{1,0:T(2,128)S(1)}, f32[2,2048]{1,0:T(2,128)S(1)}, u32[]{:S(2)}, u32[]{:S(2)}) %collective-permute-start.7) | collective-permute-done | bytes 16416 | tf_op jit(solution)/shard_map/ppermute | solution.py:340
  21.0 1.4 %shard_map.79 = (f32[8,2048]{1,0:T(8,128)S(1)}, f32[48,128]{1,0:T(8,128)S(1)}, f32[8,512]{1,0:T(8,128)}, f32[320,128]{1,0:T(8,128)S(1)}, f32[320,128]{1,0:T(8,128)S(1)}) custom-call(f32[2,2048]{1,0:T(2,128)S(1)} %shard_map.77.refs_0_, f32[2,2048]{1,0:T(2,128)S(1)} %collective-permute-done.5.refs_1_, f32[2,2048]{1,0:T(2,128)S(1)} %collective-permute-done.6.refs_2_, ...), custom_call_target="tpu_custom_call" | custom-call | flops 1207959552 | bytes 5742592 | tf_op jit(solution)/shard_map/pallas_call | solution.py:323
  22.4 1.6 %collective-permute-start.8 = (f16[320,128]{1,0:T(8,128)(2,1)S(1)}, f16[320,128]{1,0:T(8,128)(2,1)S(1)}, u32[]{:S(2)}, u32[]{:S(2)}) collective-permute-start(f16[320,128]{1,0:T(8,128)(2,1)S(1)} %get-tuple-element.61), channel_id=1, source_target_pairs={{0,16},{4,20},{8,24},{12,28},{16,0},{20,4},{24,8},{28,12},{1,17},{... | collective-permute-start | bytes 245768 | tf_op jit(solution)/shard_map/ppermute | solution.py:340
  24.0 1.5 %collective-permute-start.9 = (f16[320,128]{1,0:T(8,128)(2,1)S(1)}, f16[320,128]{1,0:T(8,128)(2,1)S(1)}, u32[]{:S(2)}, u32[]{:S(2)}) collective-permute-start(f16[320,128]{1,0:T(8,128)(2,1)S(1)} %get-tuple-element.60), channel_id=1, source_target_pairs={{0,17},{1,16},{2,19},{3,18},{4,21},{5,20},{6,23},{7,22},{8,25},{9,... | collective-permute-start | bytes 245768 | tf_op jit(solution)/shard_map/ppermute | solution.py:346
  25.5 1.2 %shard_map.80 = (f32[320,128]{1,0:T(8,128)S(1)}, f32[320,128]{1,0:T(8,128)S(1)}) custom-call(f32[8,2048]{1,0:T(8,128)S(1)} %get-tuple-element.45.refs_0_, f32[48,128]{1,0:T(8,128)S(1)} %get-tuple-element.46.refs_1_, bf16[2048,512]{1,0:T(8,128)(2,1)S(1)} %get-tuple-element.42.refs_4_.refs_2_, f32[384,2048]{1,0:T(8,128)S(1)} %get-tuple-element.43.refs_5_.refs_3_), custom_call_target="tpu_custom_call" | custom-call | flops 1207959552 | bytes 5660672 | tf_op jit(solution)/shard_map/pallas_call | solution.py:323
  26.8 0.5 %collective-permute-start.10 = (f16[320,128]{1,0:T(8,128)(2,1)S(1)}, f16[320,128]{1,0:T(8,128)(2,1)S(1)}, u32[]{:S(2)}, u32[]{:S(2)}) collective-permute-start(f16[320,128]{1,0:T(8,128)(2,1)S(1)} %get-tuple-element.58), channel_id=1, source_target_pairs={{0,1},{1,0},{2,3},{3,2},{4,5},{5,4},{6,7},{7,6},{8,9},{9,8},{10,11... | collective-permute-start | bytes 245768 | tf_op jit(solution)/shard_map/ppermute | solution.py:342
  27.3 0.5 %collective-permute-done.8 = f16[320,128]{1,0:T(8,128)(2,1)S(1)} collective-permute-done((f16[320,128]{1,0:T(8,128)(2,1)S(1)}, f16[320,128]{1,0:T(8,128)(2,1)S(1)}, u32[]{:S(2)}, u32[]{:S(2)}) %collective-permute-start.8) | collective-permute-done | bytes 81952 | tf_op jit(solution)/shard_map/ppermute | solution.py:340
  27.8 1.5 %collective-permute-done.9 = f16[320,128]{1,0:T(8,128)(2,1)S(1)} collective-permute-done((f16[320,128]{1,0:T(8,128)(2,1)S(1)}, f16[320,128]{1,0:T(8,128)(2,1)S(1)}, u32[]{:S(2)}, u32[]{:S(2)}) %collective-permute-start.9) | collective-permute-done | bytes 81952 | tf_op jit(solution)/shard_map/ppermute | solution.py:346
  29.4 1.9 %collective-permute-done.10 = f16[320,128]{1,0:T(8,128)(2,1)S(1)} collective-permute-done((f16[320,128]{1,0:T(8,128)(2,1)S(1)}, f16[320,128]{1,0:T(8,128)(2,1)S(1)}, u32[]{:S(2)}, u32[]{:S(2)}) %collective-permute-start.10) | collective-permute-done | bytes 81952 | tf_op jit(solution)/shard_map/ppermute | solution.py:342
  31.3 0.2 shard_map.81
  31.5 2.7 %collective-permute-start.11 = (f16[320,128]{1,0:T(8,128)(2,1)S(1)}, f16[320,128]{1,0:T(8,128)(2,1)S(1)}, u32[]{:S(2)}, u32[]{:S(2)}) collective-permute-start(f16[320,128]{1,0:T(8,128)(2,1)S(1)} %convert_element_type.47), channel_id=1, source_target_pairs={{0,2},{1,3},{2,0},{3,1},{4,6},{5,7},{6,4},{7,5},{8,10},{9,11},{10,... | collective-permute-start | bytes 245768 | tf_op jit(solution)/shard_map/ppermute | solution.py:342
  34.2 0.2 collective-permute-start.12
  34.4 0.7 %collective-permute-start.13 = (f16[320,128]{1,0:T(8,128)(2,1)S(1)}, f16[320,128]{1,0:T(8,128)(2,1)S(1)}, u32[]{:S(2)}, u32[]{:S(2)}) collective-permute-start(f16[320,128]{1,0:T(8,128)(2,1)S(1)} %convert_element_type.47), channel_id=1, source_target_pairs={{0,1},{1,0},{2,3},{3,2},{4,5},{5,4},{6,7},{7,6},{8,9},{9,8},{10,11... | collective-permute-start | bytes 245768 | tf_op jit(solution)/shard_map/ppermute | solution.py:342
  35.1 4.1 %collective-permute-done.11 = f16[320,128]{1,0:T(8,128)(2,1)S(1)} collective-permute-done((f16[320,128]{1,0:T(8,128)(2,1)S(1)}, f16[320,128]{1,0:T(8,128)(2,1)S(1)}, u32[]{:S(2)}, u32[]{:S(2)}) %collective-permute-start.11) | collective-permute-done | bytes 81952 | tf_op jit(solution)/shard_map/ppermute | solution.py:342
  39.2 1.3 %collective-permute-done.12 = f16[320,128]{1,0:T(8,128)(2,1)S(1)} collective-permute-done((f16[320,128]{1,0:T(8,128)(2,1)S(1)}, f16[320,128]{1,0:T(8,128)(2,1)S(1)}, u32[]{:S(2)}, u32[]{:S(2)}) %collective-permute-start.12) | collective-permute-done | bytes 81952 | tf_op jit(solution)/shard_map/ppermute | solution.py:342
  40.6 0.0 collective-permute-done.13
  40.6 1.2 %shard_map.82 = (f32[384,384]{1,0:T(8,128)}, f32[8,384]{1,0:T(8,128)}, f32[1,8]{1,0:T(1,128)}) custom-call(f32[320,128]{1,0:T(8,128)S(1)} %convert_element_type.48.refs_0_, f32[320,128]{1,0:T(8,128)S(1)} %convert_element_type.49.refs_1_, f32[320,128]{1,0:T(8,128)S(1)} %convert_element_type.50.refs_2_, f32[320,128]{1,0:T(8,128)S(1)} %convert_element_type.51.refs_3_), custom_call_target="tpu_custom_call" | custom-call | bytes 1257504 | tf_op jit(solution)/shard_map/pallas_call | solution.py:323
  (12 shorter events, 0.2 us)
Async XLA Ops:
  0.6 12.9 %collective-permute-start = (bf16[512,384]{1,0:T(8,128)(2,1)}, bf16[512,384]{1,0:T(8,128)(2,1)S(1)}, u32[]{:S(2)}, u32[]{:S(2)}) collective-permute-start(bf16[512,384]{1,0:T(8,128)(2,1)} %refs_0_.3), channel_id=1, source_target_pairs={{0,8},{4,12},{8,0},{12,4},{16,24},{20,28},{24,16},{28,20},{1,9},{5... | collective-permute-start | bytes 1179656 | tf_op jit(solution)/shard_map/ppermute | solution.py:340
  3.6 9.9 %collective-permute-start.3 = (bf16[512,384]{1,0:T(8,128)(2,1)}, bf16[512,384]{1,0:T(8,128)(2,1)S(1)}, u32[]{:S(2)}, u32[]{:S(2)}) collective-permute-start(bf16[512,384]{1,0:T(8,128)(2,1)} %refs_0_.3), channel_id=1, source_target_pairs={{0,4},{4,0},{8,12},{12,8},{16,20},{20,16},{24,28},{28,24},{1,5},{5... | collective-permute-start | bytes 1179656 | tf_op jit(solution)/shard_map/ppermute | solution.py:340
  3.6 9.9 %collective-permute-start.1 = (bf16[384,384]{1,0:T(8,128)(2,1)}, bf16[384,384]{1,0:T(8,128)(2,1)S(1)}, u32[]{:S(2)}, u32[]{:S(2)}) collective-permute-start(bf16[384,384]{1,0:T(8,128)(2,1)} %bitcast.4), channel_id=1, source_target_pairs={{0,16},{4,20},{8,24},{12,28},{16,0},{20,4},{24,8},{28,12},{1,17},{... | collective-permute-start | bytes 884744 | tf_op jit(solution)/shard_map/ppermute | solution.py:340
  6.7 6.8 %collective-permute-start.2 = (bf16[16,384]{1,0:T(8,128)(2,1)S(1)}, bf16[16,384]{1,0:T(8,128)(2,1)S(1)}, u32[]{:S(2)}, u32[]{:S(2)}) collective-permute-start(bf16[16,384]{1,0:T(8,128)(2,1)S(1)} %maximum_maximum_fusion.tail_ref.refs_5_.refs_4_), channel_id=1, source_target_pairs={{0,16},{4,20},{8,24},{12,28},{16,0},{20,4},{24,8},{28,12},{1,17},{... | collective-permute-start | bytes 36872 | tf_op jit(solution)/shard_map/ppermute | solution.py:340
  7.2 1.0 %copy-start = (bf16[512,384]{1,0:T(8,128)(2,1)S(1)}, bf16[512,384]{1,0:T(8,128)(2,1)}, u32[]{:S(2)}) copy-start(bf16[512,384]{1,0:T(8,128)(2,1)} %refs_0_.3) | copy-start | bytes 1179652
  8.2 1.0 %copy-start.2 = (bf16[1,384,384]{2,1,0:T(8,128)(2,1)S(1)}, bf16[1,384,384]{2,1,0:T(8,128)(2,1)}, u32[]{:S(2)}) copy-start(bf16[1,384,384]{2,1,0:T(8,128)(2,1)} %param.5) | copy-start | bytes 884740
  9.2 10.6 %copy-start.1 = (bf16[512,384]{1,0:T(8,128)(2,1)S(1)}, bf16[512,384]{1,0:T(8,128)(2,1)}, u32[]{:S(2)}) copy-start(bf16[512,384]{1,0:T(8,128)(2,1)} %refs_0_.3) | copy-start | bytes 1179652
  13.5 1.8 %collective-permute-start.4 = (bf16[512,384]{1,0:T(8,128)(2,1)S(1)}, bf16[512,384]{1,0:T(8,128)(2,1)S(1)}, u32[]{:S(2)}, u32[]{:S(2)}) collective-permute-start(bf16[512,384]{1,0:T(8,128)(2,1)S(1)} %collective-permute-done.refs_1_), channel_id=1, source_target_pairs={{0,4},{4,0},{8,12},{12,8},{16,20},{20,16},{24,28},{28,24},{1,5},{5... | collective-permute-start | bytes 1179656 | tf_op jit(solution)/shard_map/ppermute | solution.py:340
  16.0 3.8 %collective-permute-start.6 = (f32[2,2048]{1,0:T(2,128)S(1)}, f32[2,2048]{1,0:T(2,128)S(1)}, u32[]{:S(2)}, u32[]{:S(2)}) collective-permute-start(f32[2,2048]{1,0:T(2,128)S(1)} %shard_map.77.refs_0_), channel_id=1, source_target_pairs={{0,8},{4,12},{8,0},{12,4},{16,24},{20,28},{24,16},{28,20},{1,9},{5... | collective-permute-start | bytes 49160 | tf_op jit(solution)/shard_map/ppermute | solution.py:340
  17.1 3.3 %collective-permute-start.5 = (f32[2,2048]{1,0:T(2,128)S(1)}, f32[2,2048]{1,0:T(2,128)S(1)}, u32[]{:S(2)}, u32[]{:S(2)}) collective-permute-start(f32[2,2048]{1,0:T(2,128)S(1)} %shard_map.77.refs_0_), channel_id=1, source_target_pairs={{0,4},{4,0},{8,12},{12,8},{16,20},{20,16},{24,28},{28,24},{1,5},{5... | collective-permute-start | bytes 49160 | tf_op jit(solution)/shard_map/ppermute | solution.py:340
  19.8 1.2 %collective-permute-start.7 = (f32[2,2048]{1,0:T(2,128)S(1)}, f32[2,2048]{1,0:T(2,128)S(1)}, u32[]{:S(2)}, u32[]{:S(2)}) collective-permute-start(f32[2,2048]{1,0:T(2,128)S(1)} %collective-permute-done.6.refs_2_), channel_id=1, source_target_pairs={{0,4},{4,0},{8,12},{12,8},{16,20},{20,16},{24,28},{28,24},{1,5},{5... | collective-permute-start | bytes 49160 | tf_op jit(solution)/shard_map/ppermute | solution.py:340
  22.4 5.4 %collective-permute-start.8 = (f16[320,128]{1,0:T(8,128)(2,1)S(1)}, f16[320,128]{1,0:T(8,128)(2,1)S(1)}, u32[]{:S(2)}, u32[]{:S(2)}) collective-permute-start(f16[320,128]{1,0:T(8,128)(2,1)S(1)} %get-tuple-element.61), channel_id=1, source_target_pairs={{0,16},{4,20},{8,24},{12,28},{16,0},{20,4},{24,8},{28,12},{1,17},{... | collective-permute-start | bytes 245768 | tf_op jit(solution)/shard_map/ppermute | solution.py:340
  24.0 5.3 %collective-permute-start.9 = (f16[320,128]{1,0:T(8,128)(2,1)S(1)}, f16[320,128]{1,0:T(8,128)(2,1)S(1)}, u32[]{:S(2)}, u32[]{:S(2)}) collective-permute-start(f16[320,128]{1,0:T(8,128)(2,1)S(1)} %get-tuple-element.60), channel_id=1, source_target_pairs={{0,17},{1,16},{2,19},{3,18},{4,21},{5,20},{6,23},{7,22},{8,25},{9,... | collective-permute-start | bytes 245768 | tf_op jit(solution)/shard_map/ppermute | solution.py:346
  26.8 4.5 %collective-permute-start.10 = (f16[320,128]{1,0:T(8,128)(2,1)S(1)}, f16[320,128]{1,0:T(8,128)(2,1)S(1)}, u32[]{:S(2)}, u32[]{:S(2)}) collective-permute-start(f16[320,128]{1,0:T(8,128)(2,1)S(1)} %get-tuple-element.58), channel_id=1, source_target_pairs={{0,1},{1,0},{2,3},{3,2},{4,5},{5,4},{6,7},{7,6},{8,9},{9,8},{10,11... | collective-permute-start | bytes 245768 | tf_op jit(solution)/shard_map/ppermute | solution.py:342
  31.5 7.7 %collective-permute-start.11 = (f16[320,128]{1,0:T(8,128)(2,1)S(1)}, f16[320,128]{1,0:T(8,128)(2,1)S(1)}, u32[]{:S(2)}, u32[]{:S(2)}) collective-permute-start(f16[320,128]{1,0:T(8,128)(2,1)S(1)} %convert_element_type.47), channel_id=1, source_target_pairs={{0,2},{1,3},{2,0},{3,1},{4,6},{5,7},{6,4},{7,5},{8,10},{9,11},{10,... | collective-permute-start | bytes 245768 | tf_op jit(solution)/shard_map/ppermute | solution.py:342
  34.2 6.3 %collective-permute-start.12 = (f16[320,128]{1,0:T(8,128)(2,1)S(1)}, f16[320,128]{1,0:T(8,128)(2,1)S(1)}, u32[]{:S(2)}, u32[]{:S(2)}) collective-permute-start(f16[320,128]{1,0:T(8,128)(2,1)S(1)} %convert_element_type.47), channel_id=1, source_target_pairs={{0,3},{1,2},{2,1},{3,0},{4,7},{5,6},{6,5},{7,4},{8,11},{9,10},{10,... | collective-permute-start | bytes 245768 | tf_op jit(solution)/shard_map/ppermute | solution.py:342
  34.4 6.2 %collective-permute-start.13 = (f16[320,128]{1,0:T(8,128)(2,1)S(1)}, f16[320,128]{1,0:T(8,128)(2,1)S(1)}, u32[]{:S(2)}, u32[]{:S(2)}) collective-permute-start(f16[320,128]{1,0:T(8,128)(2,1)S(1)} %convert_element_type.47), channel_id=1, source_target_pairs={{0,1},{1,0},{2,3},{3,2},{4,5},{5,4},{6,7},{7,6},{8,9},{9,8},{10,11... | collective-permute-start | bytes 245768 | tf_op jit(solution)/shard_map/ppermute | solution.py:342

commit v7 on v6

--- a/solution.py
+++ b/solution.py
@@ -417,7 +417,7 @@
         )
         received = {}
         for b in range(1, groups):
-            for z in (1, 0):
+            for z in (0, 1):
                 received[b, z] = hop(jnp.where(odd, given[2 * b - 1 - z], given[2 * b - 2 + z]).astype(jnp.float16), 4 * b, z)
         kept = call(
             lambda *refs: keep_kernel(normalizer, layout, *refs),
@@ -428,7 +428,7 @@
         received[0, 0] = lax.optimization_barrier(jnp.where(odd, kept[1], kept[0]).astype(jnp.float16))
         received[0, 1] = hop(jnp.where(odd, kept[0], kept[1]).astype(jnp.float16), 0, 1)
         for b in range(1, groups):
-            received[b, 0], received[b, 1] = lax.optimization_barrier((received[b, 0], received[b, 1]))
+            received[b, 1], received[b, 0] = lax.optimization_barrier((received[b, 1], received[b, 0]))
         wide = {key: value.astype(jnp.float32) for key, value in received.items()}
         same = [wide[b, 0] for b in range(groups)]
         other = [wide[b, 1] for b in range(1, groups)]

time: 42 us -> 42 us (level)
    ppermute x9, waiting for transfers between devices: 7.96 us -> 9.19 us  [hop(): return lax.ppermute(value, 'blk', [(i, i ^ blk) for i in range(n_blk)])]
    ppermute x1, starting transfers between devices: 1.52 us -> 2.6 us  [hop(): return lax.ppermute(value, ('blk', 'rows'), pairs)]
    ppermute x9, starting transfers between devices: 7.85 us -> 6.78 us  [hop(): return lax.ppermute(value, 'blk', [(i, i ^ blk) for i in range(n_blk)])]
    ppermute x1, waiting for transfers between devices: 1.52 us -> 0.6 us  [hop(): return lax.ppermute(value, ('blk', 'rows'), pairs)]
where the time goes in v7:
time: 42 us; the launch traced here: 41.8 us
  waiting for transfers between devices  16.8 us (40%)
  starting transfers between devices  13.4 us (32%)
  Pallas kernels  7.02 us (17%)
  local copies, waits for them, and re-layouts  2.12 us (5%)
  between operations  1.44 us (3%)
  other arithmetic  0.96 us (2%)
    ppermute x9, waiting for transfers between devices, hop(): return lax.ppermute(value, 'blk', [(i, i ^ blk) for i in range(n_blk)])  9.19 us
    ppermute x4, waiting for transfers between devices, hop(): return lax.ppermute(value, 'rows', [(i, i ^ rows) for i in range(n_rows)])  7.05 us
    pallas_call x8, Pallas kernels, call(): pl.pallas_call(kernel, out_shape=out_shape, in_specs=specs, out_specs=jax...  7.02 us
    ppermute x9, starting transfers between devices, hop(): return lax.ppermute(value, 'blk', [(i, i ^ blk) for i in range(n_blk)])  6.78 us
    ppermute x4, starting transfers between devices, hop(): return lax.ppermute(value, 'rows', [(i, i ^ rows) for i in range(n_rows)])  4.07 us
    ppermute x1, starting transfers between devices, hop(): return lax.ppermute(value, ('blk', 'rows'), pairs)  2.6 us
    unnamed x6, local copies, waits for them, and re-layouts  1.96 us
  transfers between devices with their start and end apart: 14, of which 9 were waited for; matrix products, arithmetic and copies ran while one was open for 2% of the time, Pallas kernels for 9%

profile of v7, /device:TPU:0, one launch (start us, length us, event | category | flops | bytes accessed | tf_op | source)
XLA Modules:
  0.0 41.8 jit_solution(723777926432999214)
XLA Ops:
  0.6 3.0 %collective-permute-start = (bf16[512,384]{1,0:T(8,128)(2,1)}, bf16[512,384]{1,0:T(8,128)(2,1)S(1)}, u32[]{:S(2)}, u32[]{:S(2)}) collective-permute-start(bf16[512,384]{1,0:T(8,128)(2,1)} %refs_0_.3), channel_id=1, source_target_pairs={{0,8},{4,12},{8,0},{12,4},{16,24},{20,28},{24,16},{28,20},{1,9},{5... | collective-permute-start | bytes 1179656 | tf_op jit(solution)/shard_map/ppermute | solution.py:340
  3.6 0.0 collective-permute-start.3
  3.6 1.5 %collective-permute-start.1 = (bf16[384,384]{1,0:T(8,128)(2,1)}, bf16[384,384]{1,0:T(8,128)(2,1)S(1)}, u32[]{:S(2)}, u32[]{:S(2)}) collective-permute-start(bf16[384,384]{1,0:T(8,128)(2,1)} %bitcast.4), channel_id=1, source_target_pairs={{0,16},{4,20},{8,24},{12,28},{16,0},{20,4},{24,8},{28,12},{1,17},{... | collective-permute-start | bytes 884744 | tf_op jit(solution)/shard_map/ppermute | solution.py:340
  5.8 0.1 pad.1.clone
  5.9 0.1 pad.2.clone
  6.0 0.8 %maximum_maximum_fusion.tail_ref.refs_5_.refs_4_ = bf16[16,384]{1,0:T(8,128)(2,1)S(1)} fusion(bf16[1,384]{1,0:T(2,128)(2,1)} %param.6, bf16[16]{0:T(256)(128)(2,1)S(1)} %pad.2.clone, bf16[16]{0:T(256)(128)(2,1)S(1)} %pad.1.clone), kind=kLoop, calls=%fused_computation.4 | loop fusion | flops 36864 | bytes 13120 | tf_op jit(solution)/shard_map/concatenate | solution.py:357
  6.7 0.5 %collective-permute-start.2 = (bf16[16,384]{1,0:T(8,128)(2,1)S(1)}, bf16[16,384]{1,0:T(8,128)(2,1)S(1)}, u32[]{:S(2)}, u32[]{:S(2)}) collective-permute-start(bf16[16,384]{1,0:T(8,128)(2,1)S(1)} %maximum_maximum_fusion.tail_ref.refs_5_.refs_4_), channel_id=1, source_target_pairs={{0,16},{4,20},{8,24},{12,28},{16,0},{20,4},{24,8},{28,12},{1,17},{... | collective-permute-start | bytes 36872 | tf_op jit(solution)/shard_map/ppermute | solution.py:340
  7.2 0.0 copy-start
  7.2 1.0 %copy-done = bf16[512,384]{1,0:T(8,128)(2,1)S(1)} copy-done((bf16[512,384]{1,0:T(8,128)(2,1)S(1)}, bf16[512,384]{1,0:T(8,128)(2,1)}, u32[]{:S(2)}) %copy-start) | copy-done | bytes 393240
  8.2 0.0 copy-start.2
  8.2 1.0 %copy-done.2 = bf16[1,384,384]{2,1,0:T(8,128)(2,1)S(1)} copy-done((bf16[1,384,384]{2,1,0:T(8,128)(2,1)S(1)}, bf16[1,384,384]{2,1,0:T(8,128)(2,1)}, u32[]{:S(2)}) %copy-start.2) | copy-done | bytes 294936
  9.2 0.0 copy-start.1
  9.2 0.5 %shard_map.75 = (f32[1,512]{1,0:T(1,128)S(1)}, bf16[384,384]{1,0:T(8,128)(2,1)S(1)}) custom-call(bf16[512,384]{1,0:T(8,128)(2,1)S(1)} %copy-done, bf16[384,384]{1,0:T(8,128)(2,1)S(1)} %bitcast.5, bf16[16,384]{1,0:T(8,128)(2,1)S(1)} %maximum_maximum_fusion.tail_ref.refs_5_.refs_4_), custom_call_target="tpu_custom_call" | custom-call | flops 150994944 | bytes 997376 | tf_op jit(solution)/shard_map/pallas_call | solution.py:323
  9.7 3.9 %collective-permute-done.2.refs_6_.refs_5_ = bf16[16,384]{1,0:T(8,128)(2,1)S(1)} collective-permute-done((bf16[16,384]{1,0:T(8,128)(2,1)S(1)}, bf16[16,384]{1,0:T(8,128)(2,1)S(1)}, u32[]{:S(2)}, u32[]{:S(2)}) %collective-permute-start.2) | collective-permute-done | bytes 12320 | tf_op jit(solution)/shard_map/ppermute | solution.py:340
  13.5 0.0 collective-permute-done.1.refs_7_
  13.5 0.0 collective-permute-done.refs_1_
  13.5 0.0 collective-permute-done.3.refs_2_
  13.5 0.1 collective-permute-start.4
  13.6 1.3 %shard_map.76 = (f32[2,1536]{1,0:T(2,128)S(1)}, bf16[1,384,384]{2,1,0:T(8,128)(2,1)S(1)}) custom-call(bf16[512,384]{1,0:T(8,128)(2,1)S(1)} %copy-done, bf16[512,384]{1,0:T(8,128)(2,1)S(1)} %collective-permute-done.refs_1_, bf16[512,384]{1,0:T(8,128)(2,1)S(1)} %collective-permute-done.3.refs_2_, f32[1,512]{1,0:T(1,128)S(1)} %get-tuple-element.34.refs_3_, ...), custom_call_target="tpu_custom_call" | custom-call | flops 603979776 | bytes 2103296 | tf_op jit(solution)/shard_map/pallas_call | solution.py:323
  14.9 0.4 collective-permute-done.4.refs_0_.refs_3_
  15.3 0.6 %shard_map.77.refs_0_ = f32[2,2048]{1,0:T(2,128)S(1)} custom-call(bf16[512,384]{1,0:T(8,128)(2,1)S(1)} %collective-permute-done.4.refs_0_.refs_3_, f32[2,1536]{1,0:T(2,128)S(1)} %get-tuple-element.38.refs_1_, bf16[384,384]{1,0:T(8,128)(2,1)S(1)} %get-tuple-element.35.refs_4_.refs_2_, bf16[1,384,384]{2,1,0:T(8,128)(2,1)S(1)} %get-tuple-element.39.refs_3_, ...), custom_call_target="tpu_custom_call" | custom-call | flops 301989888 | bytes 1036288 | tf_op jit(solution)/shard_map/pallas_call | solution.py:323
  16.0 1.2 %collective-permute-start.6 = (f32[2,2048]{1,0:T(2,128)S(1)}, f32[2,2048]{1,0:T(2,128)S(1)}, u32[]{:S(2)}, u32[]{:S(2)}) collective-permute-start(f32[2,2048]{1,0:T(2,128)S(1)} %shard_map.77.refs_0_), channel_id=1, source_target_pairs={{0,8},{4,12},{8,0},{12,4},{16,24},{20,28},{24,16},{28,20},{1,9},{5... | collective-permute-start | bytes 49160 | tf_op jit(solution)/shard_map/ppermute | solution.py:340
  17.1 0.0 collective-permute-start.5
  17.1 2.6 %collective-permute-done.6.refs_2_ = f32[2,2048]{1,0:T(2,128)S(1)} collective-permute-done((f32[2,2048]{1,0:T(2,128)S(1)}, f32[2,2048]{1,0:T(2,128)S(1)}, u32[]{:S(2)}, u32[]{:S(2)}) %collective-permute-start.6) | collective-permute-done | bytes 16416 | tf_op jit(solution)/shard_map/ppermute | solution.py:340
  19.8 0.0 collective-permute-start.7
  19.8 0.0 copy-done.1
  19.8 0.6 %shard_map.78 = (bf16[2048,512]{1,0:T(8,128)(2,1)S(1)}, f32[384,2048]{1,0:T(8,128)S(1)}) custom-call(bf16[512,384]{1,0:T(8,128)(2,1)S(1)} %copy-done.1, bf16[512,384]{1,0:T(8,128)(2,1)S(1)} %collective-permute-done.refs_1_, bf16[512,384]{1,0:T(8,128)(2,1)S(1)} %collective-permute-done.3.refs_2_, bf16[512,384]{1,0:T(8,128)(2,1)S(1)} %collective-permute-done.4.refs_0_.refs_3_), custom_call_target="tpu_custom_call" | custom-call | bytes 6815744 | tf_op jit(solution)/shard_map/pallas_call | solution.py:323
  20.4 0.0 collective-permute-done.5.refs_1_
  20.4 0.5 %collective-permute-done.7.refs_3_ = f32[2,2048]{1,0:T(2,128)S(1)} collective-permute-done((f32[2,2048]{1,0:T(2,128)S(1)}, f32[2,2048]{1,0:T(2,128)S(1)}, u32[]{:S(2)}, u32[]{:S(2)}) %collective-permute-start.7) | collective-permute-done | bytes 16416 | tf_op jit(solution)/shard_map/ppermute | solution.py:340
  21.0 1.4 %shard_map.79 = (f32[8,2048]{1,0:T(8,128)S(1)}, f32[48,128]{1,0:T(8,128)S(1)}, f32[8,512]{1,0:T(8,128)}, f32[320,128]{1,0:T(8,128)S(1)}, f32[320,128]{1,0:T(8,128)S(1)}) custom-call(f32[2,2048]{1,0:T(2,128)S(1)} %shard_map.77.refs_0_, f32[2,2048]{1,0:T(2,128)S(1)} %collective-permute-done.5.refs_1_, f32[2,2048]{1,0:T(2,128)S(1)} %collective-permute-done.6.refs_2_, ...), custom_call_target="tpu_custom_call" | custom-call | flops 1207959552 | bytes 5742592 | tf_op jit(solution)/shard_map/pallas_call | solution.py:323
  22.4 2.6 %collective-permute-start.8 = (f16[320,128]{1,0:T(8,128)(2,1)S(1)}, f16[320,128]{1,0:T(8,128)(2,1)S(1)}, u32[]{:S(2)}, u32[]{:S(2)}) collective-permute-start(f16[320,128]{1,0:T(8,128)(2,1)S(1)} %get-tuple-element.61), channel_id=1, source_target_pairs={{0,17},{1,16},{2,19},{3,18},{4,21},{5,20},{6,23},{7,22},{8,25},{9,... | collective-permute-start | bytes 245768 | tf_op jit(solution)/shard_map/ppermute | solution.py:346
  25.0 0.5 %collective-permute-start.9 = (f16[320,128]{1,0:T(8,128)(2,1)S(1)}, f16[320,128]{1,0:T(8,128)(2,1)S(1)}, u32[]{:S(2)}, u32[]{:S(2)}) collective-permute-start(f16[320,128]{1,0:T(8,128)(2,1)S(1)} %get-tuple-element.60), channel_id=1, source_target_pairs={{0,16},{4,20},{8,24},{12,28},{16,0},{20,4},{24,8},{28,12},{1,17},{... | collective-permute-start | bytes 245768 | tf_op jit(solution)/shard_map/ppermute | solution.py:340
  25.5 1.2 %shard_map.80 = (f32[320,128]{1,0:T(8,128)S(1)}, f32[320,128]{1,0:T(8,128)S(1)}) custom-call(f32[8,2048]{1,0:T(8,128)S(1)} %get-tuple-element.45.refs_0_, f32[48,128]{1,0:T(8,128)S(1)} %get-tuple-element.46.refs_1_, bf16[2048,512]{1,0:T(8,128)(2,1)S(1)} %get-tuple-element.42.refs_4_.refs_2_, f32[384,2048]{1,0:T(8,128)S(1)} %get-tuple-element.43.refs_5_.refs_3_), custom_call_target="tpu_custom_call" | custom-call | flops 1207959552 | bytes 5660672 | tf_op jit(solution)/shard_map/pallas_call | solution.py:323
  26.8 0.5 %collective-permute-start.10 = (f16[320,128]{1,0:T(8,128)(2,1)S(1)}, f16[320,128]{1,0:T(8,128)(2,1)S(1)}, u32[]{:S(2)}, u32[]{:S(2)}) collective-permute-start(f16[320,128]{1,0:T(8,128)(2,1)S(1)} %get-tuple-element.58), channel_id=1, source_target_pairs={{0,1},{1,0},{2,3},{3,2},{4,5},{5,4},{6,7},{7,6},{8,9},{9,8},{10,11... | collective-permute-start | bytes 245768 | tf_op jit(solution)/shard_map/ppermute | solution.py:342
  27.3 0.6 %collective-permute-done.8 = f16[320,128]{1,0:T(8,128)(2,1)S(1)} collective-permute-done((f16[320,128]{1,0:T(8,128)(2,1)S(1)}, f16[320,128]{1,0:T(8,128)(2,1)S(1)}, u32[]{:S(2)}, u32[]{:S(2)}) %collective-permute-start.8) | collective-permute-done | bytes 81952 | tf_op jit(solution)/shard_map/ppermute | solution.py:346
  27.9 1.7 %collective-permute-done.9 = f16[320,128]{1,0:T(8,128)(2,1)S(1)} collective-permute-done((f16[320,128]{1,0:T(8,128)(2,1)S(1)}, f16[320,128]{1,0:T(8,128)(2,1)S(1)}, u32[]{:S(2)}, u32[]{:S(2)}) %collective-permute-start.9) | collective-permute-done | bytes 81952 | tf_op jit(solution)/shard_map/ppermute | solution.py:340
  29.7 1.6 %collective-permute-done.10 = f16[320,128]{1,0:T(8,128)(2,1)S(1)} collective-permute-done((f16[320,128]{1,0:T(8,128)(2,1)S(1)}, f16[320,128]{1,0:T(8,128)(2,1)S(1)}, u32[]{:S(2)}, u32[]{:S(2)}) %collective-permute-start.10) | collective-permute-done | bytes 81952 | tf_op jit(solution)/shard_map/ppermute | solution.py:342
  31.3 0.2 shard_map.81
  31.5 2.6 %collective-permute-start.11 = (f16[320,128]{1,0:T(8,128)(2,1)S(1)}, f16[320,128]{1,0:T(8,128)(2,1)S(1)}, u32[]{:S(2)}, u32[]{:S(2)}) collective-permute-start(f16[320,128]{1,0:T(8,128)(2,1)S(1)} %convert_element_type.47), channel_id=1, source_target_pairs={{0,2},{1,3},{2,0},{3,1},{4,6},{5,7},{6,4},{7,5},{8,10},{9,11},{10,... | collective-permute-start | bytes 245768 | tf_op jit(solution)/shard_map/ppermute | solution.py:342
  34.2 0.2 collective-permute-start.12
  34.4 0.7 %collective-permute-start.13 = (f16[320,128]{1,0:T(8,128)(2,1)S(1)}, f16[320,128]{1,0:T(8,128)(2,1)S(1)}, u32[]{:S(2)}, u32[]{:S(2)}) collective-permute-start(f16[320,128]{1,0:T(8,128)(2,1)S(1)} %convert_element_type.47), channel_id=1, source_target_pairs={{0,1},{1,0},{2,3},{3,2},{4,5},{5,4},{6,7},{7,6},{8,9},{9,8},{10,11... | collective-permute-start | bytes 245768 | tf_op jit(solution)/shard_map/ppermute | solution.py:342
  35.1 4.3 %collective-permute-done.11 = f16[320,128]{1,0:T(8,128)(2,1)S(1)} collective-permute-done((f16[320,128]{1,0:T(8,128)(2,1)S(1)}, f16[320,128]{1,0:T(8,128)(2,1)S(1)}, u32[]{:S(2)}, u32[]{:S(2)}) %collective-permute-start.11) | collective-permute-done | bytes 81952 | tf_op jit(solution)/shard_map/ppermute | solution.py:342
  39.4 1.1 %collective-permute-done.12 = f16[320,128]{1,0:T(8,128)(2,1)S(1)} collective-permute-done((f16[320,128]{1,0:T(8,128)(2,1)S(1)}, f16[320,128]{1,0:T(8,128)(2,1)S(1)}, u32[]{:S(2)}, u32[]{:S(2)}) %collective-permute-start.12) | collective-permute-done | bytes 81952 | tf_op jit(solution)/shard_map/ppermute | solution.py:342
  40.6 0.0 collective-permute-done.13
  40.6 1.2 %shard_map.82 = (f32[384,384]{1,0:T(8,128)}, f32[8,384]{1,0:T(8,128)}, f32[1,8]{1,0:T(1,128)}) custom-call(f32[320,128]{1,0:T(8,128)S(1)} %convert_element_type.48.refs_0_, f32[320,128]{1,0:T(8,128)S(1)} %convert_element_type.49.refs_1_, f32[320,128]{1,0:T(8,128)S(1)} %convert_element_type.50.refs_2_, f32[320,128]{1,0:T(8,128)S(1)} %convert_element_type.51.refs_3_), custom_call_target="tpu_custom_call" | custom-call | bytes 1257504 | tf_op jit(solution)/shard_map/pallas_call | solution.py:323
  (12 shorter events, 0.2 us)
Async XLA Ops:
  0.6 12.9 %collective-permute-start = (bf16[512,384]{1,0:T(8,128)(2,1)}, bf16[512,384]{1,0:T(8,128)(2,1)S(1)}, u32[]{:S(2)}, u32[]{:S(2)}) collective-permute-start(bf16[512,384]{1,0:T(8,128)(2,1)} %refs_0_.3), channel_id=1, source_target_pairs={{0,8},{4,12},{8,0},{12,4},{16,24},{20,28},{24,16},{28,20},{1,9},{5... | collective-permute-start | bytes 1179656 | tf_op jit(solution)/shard_map/ppermute | solution.py:340
  3.6 9.9 %collective-permute-start.3 = (bf16[512,384]{1,0:T(8,128)(2,1)}, bf16[512,384]{1,0:T(8,128)(2,1)S(1)}, u32[]{:S(2)}, u32[]{:S(2)}) collective-permute-start(bf16[512,384]{1,0:T(8,128)(2,1)} %refs_0_.3), channel_id=1, source_target_pairs={{0,4},{4,0},{8,12},{12,8},{16,20},{20,16},{24,28},{28,24},{1,5},{5... | collective-permute-start | bytes 1179656 | tf_op jit(solution)/shard_map/ppermute | solution.py:340
  3.6 9.9 %collective-permute-start.1 = (bf16[384,384]{1,0:T(8,128)(2,1)}, bf16[384,384]{1,0:T(8,128)(2,1)S(1)}, u32[]{:S(2)}, u32[]{:S(2)}) collective-permute-start(bf16[384,384]{1,0:T(8,128)(2,1)} %bitcast.4), channel_id=1, source_target_pairs={{0,16},{4,20},{8,24},{12,28},{16,0},{20,4},{24,8},{28,12},{1,17},{... | collective-permute-start | bytes 884744 | tf_op jit(solution)/shard_map/ppermute | solution.py:340
  6.7 6.8 %collective-permute-start.2 = (bf16[16,384]{1,0:T(8,128)(2,1)S(1)}, bf16[16,384]{1,0:T(8,128)(2,1)S(1)}, u32[]{:S(2)}, u32[]{:S(2)}) collective-permute-start(bf16[16,384]{1,0:T(8,128)(2,1)S(1)} %maximum_maximum_fusion.tail_ref.refs_5_.refs_4_), channel_id=1, source_target_pairs={{0,16},{4,20},{8,24},{12,28},{16,0},{20,4},{24,8},{28,12},{1,17},{... | collective-permute-start | bytes 36872 | tf_op jit(solution)/shard_map/ppermute | solution.py:340
  7.2 1.0 %copy-start = (bf16[512,384]{1,0:T(8,128)(2,1)S(1)}, bf16[512,384]{1,0:T(8,128)(2,1)}, u32[]{:S(2)}) copy-start(bf16[512,384]{1,0:T(8,128)(2,1)} %refs_0_.3) | copy-start | bytes 1179652
  8.2 1.0 %copy-start.2 = (bf16[1,384,384]{2,1,0:T(8,128)(2,1)S(1)}, bf16[1,384,384]{2,1,0:T(8,128)(2,1)}, u32[]{:S(2)}) copy-start(bf16[1,384,384]{2,1,0:T(8,128)(2,1)} %param.5) | copy-start | bytes 884740
  9.2 10.6 %copy-start.1 = (bf16[512,384]{1,0:T(8,128)(2,1)S(1)}, bf16[512,384]{1,0:T(8,128)(2,1)}, u32[]{:S(2)}) copy-start(bf16[512,384]{1,0:T(8,128)(2,1)} %refs_0_.3) | copy-start | bytes 1179652
  13.5 1.8 %collective-permute-start.4 = (bf16[512,384]{1,0:T(8,128)(2,1)S(1)}, bf16[512,384]{1,0:T(8,128)(2,1)S(1)}, u32[]{:S(2)}, u32[]{:S(2)}) collective-permute-start(bf16[512,384]{1,0:T(8,128)(2,1)S(1)} %collective-permute-done.refs_1_), channel_id=1, source_target_pairs={{0,4},{4,0},{8,12},{12,8},{16,20},{20,16},{24,28},{28,24},{1,5},{5... | collective-permute-start | bytes 1179656 | tf_op jit(solution)/shard_map/ppermute | solution.py:340
  16.0 3.8 %collective-permute-start.6 = (f32[2,2048]{1,0:T(2,128)S(1)}, f32[2,2048]{1,0:T(2,128)S(1)}, u32[]{:S(2)}, u32[]{:S(2)}) collective-permute-start(f32[2,2048]{1,0:T(2,128)S(1)} %shard_map.77.refs_0_), channel_id=1, source_target_pairs={{0,8},{4,12},{8,0},{12,4},{16,24},{20,28},{24,16},{28,20},{1,9},{5... | collective-permute-start | bytes 49160 | tf_op jit(solution)/shard_map/ppermute | solution.py:340
  17.1 3.3 %collective-permute-start.5 = (f32[2,2048]{1,0:T(2,128)S(1)}, f32[2,2048]{1,0:T(2,128)S(1)}, u32[]{:S(2)}, u32[]{:S(2)}) collective-permute-start(f32[2,2048]{1,0:T(2,128)S(1)} %shard_map.77.refs_0_), channel_id=1, source_target_pairs={{0,4},{4,0},{8,12},{12,8},{16,20},{20,16},{24,28},{28,24},{1,5},{5... | collective-permute-start | bytes 49160 | tf_op jit(solution)/shard_map/ppermute | solution.py:340
  19.8 1.2 %collective-permute-start.7 = (f32[2,2048]{1,0:T(2,128)S(1)}, f32[2,2048]{1,0:T(2,128)S(1)}, u32[]{:S(2)}, u32[]{:S(2)}) collective-permute-start(f32[2,2048]{1,0:T(2,128)S(1)} %collective-permute-done.6.refs_2_), channel_id=1, source_target_pairs={{0,4},{4,0},{8,12},{12,8},{16,20},{20,16},{24,28},{28,24},{1,5},{5... | collective-permute-start | bytes 49160 | tf_op jit(solution)/shard_map/ppermute | solution.py:340
  22.4 5.5 %collective-permute-start.8 = (f16[320,128]{1,0:T(8,128)(2,1)S(1)}, f16[320,128]{1,0:T(8,128)(2,1)S(1)}, u32[]{:S(2)}, u32[]{:S(2)}) collective-permute-start(f16[320,128]{1,0:T(8,128)(2,1)S(1)} %get-tuple-element.61), channel_id=1, source_target_pairs={{0,17},{1,16},{2,19},{3,18},{4,21},{5,20},{6,23},{7,22},{8,25},{9,... | collective-permute-start | bytes 245768 | tf_op jit(solution)/shard_map/ppermute | solution.py:346
  25.0 4.6 %collective-permute-start.9 = (f16[320,128]{1,0:T(8,128)(2,1)S(1)}, f16[320,128]{1,0:T(8,128)(2,1)S(1)}, u32[]{:S(2)}, u32[]{:S(2)}) collective-permute-start(f16[320,128]{1,0:T(8,128)(2,1)S(1)} %get-tuple-element.60), channel_id=1, source_target_pairs={{0,16},{4,20},{8,24},{12,28},{16,0},{20,4},{24,8},{28,12},{1,17},{... | collective-permute-start | bytes 245768 | tf_op jit(solution)/shard_map/ppermute | solution.py:340
  26.8 4.5 %collective-permute-start.10 = (f16[320,128]{1,0:T(8,128)(2,1)S(1)}, f16[320,128]{1,0:T(8,128)(2,1)S(1)}, u32[]{:S(2)}, u32[]{:S(2)}) collective-permute-start(f16[320,128]{1,0:T(8,128)(2,1)S(1)} %get-tuple-element.58), channel_id=1, source_target_pairs={{0,1},{1,0},{2,3},{3,2},{4,5},{5,4},{6,7},{7,6},{8,9},{9,8},{10,11... | collective-permute-start | bytes 245768 | tf_op jit(solution)/shard_map/ppermute | solution.py:342
  31.5 7.9 %collective-permute-start.11 = (f16[320,128]{1,0:T(8,128)(2,1)S(1)}, f16[320,128]{1,0:T(8,128)(2,1)S(1)}, u32[]{:S(2)}, u32[]{:S(2)}) collective-permute-start(f16[320,128]{1,0:T(8,128)(2,1)S(1)} %convert_element_type.47), channel_id=1, source_target_pairs={{0,2},{1,3},{2,0},{3,1},{4,6},{5,7},{6,4},{7,5},{8,10},{9,11},{10,... | collective-permute-start | bytes 245768 | tf_op jit(solution)/shard_map/ppermute | solution.py:342
  34.2 6.3 %collective-permute-start.12 = (f16[320,128]{1,0:T(8,128)(2,1)S(1)}, f16[320,128]{1,0:T(8,128)(2,1)S(1)}, u32[]{:S(2)}, u32[]{:S(2)}) collective-permute-start(f16[320,128]{1,0:T(8,128)(2,1)S(1)} %convert_element_type.47), channel_id=1, source_target_pairs={{0,3},{1,2},{2,1},{3,0},{4,7},{5,6},{6,5},{7,4},{8,11},{9,10},{10,... | collective-permute-start | bytes 245768 | tf_op jit(solution)/shard_map/ppermute | solution.py:342
  34.4 6.2 %collective-permute-start.13 = (f16[320,128]{1,0:T(8,128)(2,1)S(1)}, f16[320,128]{1,0:T(8,128)(2,1)S(1)}, u32[]{:S(2)}, u32[]{:S(2)}) collective-permute-start(f16[320,128]{1,0:T(8,128)(2,1)S(1)} %convert_element_type.47), channel_id=1, source_target_pairs={{0,1},{1,0},{2,3},{3,2},{4,5},{5,4},{6,7},{7,6},{8,9},{9,8},{10,11... | collective-permute-start | bytes 245768 | tf_op jit(solution)/shard_map/ppermute | solution.py:342
